TPU v7x, 32 devices: a whole 2x2x4 slice. The times are simulated.
32 devices in a mesh: pipe: 4 (over y, x), tensor: 8 (over z, core).
Axes of the slice: x: 2, y: 2, z: 4, core: 2. Of those that a mesh axis runs over, the one named last changes fastest.
Arguments:
- layer_input: bfloat16 [768, 8192], P('tensor', 'pipe'), may hold values from -6 to 6
- out_grad: bfloat16 [768, 8192], P('tensor', 'pipe'), may hold values from -2 to 2
- gate_pre: bfloat16 [768, 28672], P(None, 'tensor'), may hold values from -8 to 8
- up_pre: bfloat16 [768, 28672], P(None, 'tensor'), may hold values from -6 to 6
- gate_weight: bfloat16 [8192, 28672], P('pipe', 'tensor'), may hold values from -0.0625 to 0.0625
- up_weight: bfloat16 [8192, 28672], P('pipe', 'tensor'), may hold values from -0.0625 to 0.0625
- down_weight: bfloat16 [28672, 8192], P('tensor', 'pipe'), may hold values from -0.03125 to 0.03125
- gate_mask: int32 [64, 224], P('pipe', 'tensor'), may hold values from 0 to 1, as said below
- up_mask: int32 [64, 224], P('pipe', 'tensor'), may hold values from 0 to 1, as said below
- down_mask: int32 [224, 64], P('tensor', 'pipe'), may hold values from 0 to 1, as said below
Outputs:
- grad_input: bfloat16 [768, 8192], P('tensor', 'pipe')
- grad_gate: bfloat16 [8192, 28672], P('pipe', 'tensor')
- grad_up: bfloat16 [8192, 28672], P('pipe', 'tensor')
- grad_down: bfloat16 [28672, 8192], P('tensor', 'pipe')
Inputs may be any that keep to these rules, and one draw needn't show every extreme that they name: `gate_mask`: each entry is 1 for a kept block and 0 for a pruned one; the share of kept blocks differs from block column to block column. `up_mask`: each entry is 1 for a kept block and 0 for a pruned one; the share of kept blocks differs from block column to block column. `down_mask`: each entry is 1 for a kept block and 0 for a pruned one; the share of kept blocks differs from block row to block row.
All inputs are finite; a program needn't handle non-finite values.
Results may differ from a plain program's by a relative error of at most 0.005.
Values may be sent and summed in bfloat16 or wider, within the bound.
No kernel may reach another device: no remote copies, remote signals or barrier semaphores. Data moves between devices by JAX's collectives and lax.ppermute only.
A program may use at most 256 MiB of HBM per device.

v0:
```python
import jax
import jax.numpy as jnp
from jax import lax
from jax.sharding import PartitionSpec as P

BLOCK = 128


def expand(mask):
    return jnp.repeat(jnp.repeat(mask, BLOCK, axis=0), BLOCK, axis=1)


def local_grads(hidden_grad, gate_val, up_val, sigma_val):
    gate_grad = (hidden_grad * up_val * sigma_val * (1.0 + gate_val * (1.0 - sigma_val))).astype(
        jnp.bfloat16
    )
    up_grad = (hidden_grad * gate_val * sigma_val).astype(jnp.bfloat16)
    return (gate_grad, up_grad)


def shards(
    layer_input,
    out_grad,
    gate_pre,
    up_pre,
    gate_weight,
    up_weight,
    down_weight,
    gate_mask,
    up_mask,
    down_mask,
):
    mask_gate = expand(gate_mask)
    mask_up = expand(up_mask)
    mask_down = expand(down_mask)
    gate_masked = gate_weight * mask_gate.astype(jnp.bfloat16)
    up_masked = up_weight * mask_up.astype(jnp.bfloat16)
    down_masked = down_weight * mask_down.astype(jnp.bfloat16)
    gate_val = gate_pre.astype(jnp.float32)
    up_val = up_pre.astype(jnp.float32)
    sigma_val = jax.nn.sigmoid(gate_val)
    hidden = (gate_val * sigma_val * up_val).astype(jnp.bfloat16)
    piece = lax.all_gather(out_grad, "tensor", axis=0, tiled=True)
    down_acc = lax.dot_general(
        hidden, piece, (((0,), (0,)), ((), ())), preferred_element_type=jnp.float32
    )
    partial_rows = lax.dot_general(
        piece, down_masked, (((1,), (1,)), ((), ())), preferred_element_type=jnp.float32
    )
    hidden_grad = partial_rows
    down_acc, hidden_partial = (down_acc, hidden_grad)
    grad_down = (down_acc * mask_down.astype(jnp.float32)).astype(jnp.bfloat16)
    hidden_grad = lax.psum(hidden_partial, "pipe")
    gate_grad, up_grad = local_grads(hidden_grad, gate_val, up_val, sigma_val)
    piece = lax.all_gather(layer_input, "tensor", axis=0, tiled=True)
    gate_rows = gate_grad
    up_rows = up_grad
    gate_acc = lax.dot_general(
        piece, gate_rows, (((0,), (0,)), ((), ())), preferred_element_type=jnp.float32
    )
    up_acc = lax.dot_general(
        piece, up_rows, (((0,), (0,)), ((), ())), preferred_element_type=jnp.float32
    )
    gate_acc, up_acc = (gate_acc, up_acc)
    grad_gate = (gate_acc * mask_gate.astype(jnp.float32)).astype(jnp.bfloat16)
    grad_up = (up_acc * mask_up.astype(jnp.float32)).astype(jnp.bfloat16)
    gate_rows = gate_grad
    up_rows = up_grad
    total = lax.dot_general(
        gate_rows, gate_masked, (((1,), (1,)), ((), ())), preferred_element_type=jnp.float32
    )
    grad_input = lax.psum_scatter(
        total
        + lax.dot_general(
            up_rows, up_masked, (((1,), (1,)), ((), ())), preferred_element_type=jnp.float32
        ),
        "tensor",
        scatter_dimension=0,
        tiled=True,
    ).astype(jnp.bfloat16)
    return (grad_input, grad_gate, grad_up, grad_down)


def solution(mesh):
    in_specs = (
        P("tensor", "pipe"),
        P("tensor", "pipe"),
        P(None, "tensor"),
        P(None, "tensor"),
        P("pipe", "tensor"),
        P("pipe", "tensor"),
        P("tensor", "pipe"),
        P("pipe", "tensor"),
        P("pipe", "tensor"),
        P("tensor", "pipe"),
    )
    out_specs = (P("tensor", "pipe"), P("pipe", "tensor"), P("pipe", "tensor"), P("tensor", "pipe"))
    return jax.shard_map(shards, mesh=mesh, in_specs=in_specs, out_specs=out_specs, check_vma=False)
```

profile of v0, /device:TPU:0, one launch (start us, length us, event | category | flops | bytes accessed | tf_op | source)
XLA Modules:
  0.0 474.6 jit_solution(14005885888927603082)
XLA Ops:
  7.2 0.7 all-gather.3.cloned.1.call-update
  7.9 0.8 fusion.21
  8.8 41.8 %all-gather.3.cloned.1.call-done = bf16[768,2048]{1,0:T(8,128)(2,1)} async-done(((bf16[96,2048]{1,0:T(8,128)(2,1)}), bf16[768,2048]{1,0:T(8,128)(2,1)}) %all-gather.3.cloned.1.call-update) | async-done | bytes 3145744 | tf_op jit(solution)/shard_map/all_gather | solution.py:43
  50.7 0.1 broadcast_in_dim.30
  50.8 9.8 %broadcast_in_dim.31 = bf16[3584,16,128]{2,1,0:T(8,128)(2,1)} broadcast(bf16[3584,16]{1,0:T(8,128)(2,1)S(1)} %bitcast.68), dimensions={0,1} | broadcast | bytes 14794752 | tf_op jit(solution)/shard_map/broadcast_in_dim | solution.py:10
  60.6 22.5 %fusion.15 = f32[768,3584]{0,1:T(8,128)} fusion(bf16[768,2048]{1,0:T(8,128)(2,1)} %all-gather.3.cloned.1.call-done, bf16[3584,2048]{1,0:T(8,128)(2,1)} %param.16, bf16[448,8,16,128]{3,2,1,0:T(8,128)(2,1)} %bitcast.66), kind=kOutput, calls=%fused_computation.27 | convolution fusion | flops 11281629184 | bytes 43515904 | tf_op jit(solution)/shard_map/dot_general | solution.py:47
  83.2 0.7 all-gather.5.cloned.1.call-update
  83.8 0.2 reduce-scatter.2.cloned.1.call-start
  84.3 0.1 broadcast_bitcast_fusion.2
  84.5 0.1 broadcast_bitcast_fusion.3
  84.7 7.9 %copy.24 = bf16[768,3584]{0,1:T(8,128)(2,1)} copy(bf16[768,3584]{1,0:T(8,128)(2,1)} %param.12) | data formatting | bytes 11010048 | tf_op args[2]
  92.6 8.3 %copy.23 = bf16[768,3584]{0,1:T(8,128)(2,1)} copy(bf16[768,3584]{1,0:T(8,128)(2,1)} %param.13) | data formatting | bytes 11010048 | tf_op args[3]
  100.9 20.3 %copy.26 = bf16[2048,3584]{0,1:T(8,128)(2,1)} copy(bf16[2048,3584]{1,0:T(8,128)(2,1)} %param.14) | data formatting | bytes 29360128 | tf_op args[4]
  121.2 20.4 %copy.28 = bf16[2048,3584]{0,1:T(8,128)(2,1)} copy(bf16[2048,3584]{1,0:T(8,128)(2,1)} %param.15) | data formatting | bytes 29360128 | tf_op args[5]
  141.6 13.9 %bitcast_multiply_fusion.6 = bf16[2048,3584]{0,1:T(8,128)(2,1)} fusion(bf16[2048,3584]{0,1:T(8,128)(2,1)} %copy.26, bf16[2048,28]{0,1:T(8,128)(2,1)S(1)} %bitcast.72), kind=kLoop, calls=%fused_computation.14 | loop fusion | flops 7340032 | bytes 29474816 | tf_op jit(solution)/shard_map/mul | solution.py:36
  155.5 1.6 copy-done
  157.1 5.9 %bitcast_multiply_fusion.5 = bf16[2048,3584]{0,1:T(8,128)(2,1)} fusion(bf16[2048,3584]{0,1:T(8,128)(2,1)S(1)} %copy-done, bf16[2048,28]{0,1:T(8,128)(2,1)S(1)} %bitcast.71), kind=kLoop, calls=%fused_computation.13 | loop fusion | flops 7340032 | bytes 29474816 | tf_op jit(solution)/shard_map/mul | solution.py:37
  163.1 133.4 %all-reduce.2.cloned.1.call-done = f32[768,3584]{0,1:T(8,128)} async-done(((f32[768,3584]{0,1:T(8,128)}), f32[768,3584]{0,1:T(8,128)}) %all-reduce.2.cloned.1.call-update) | async-done | bytes 11010064 | tf_op jit(solution)/shard_map/psum | solution.py:53
  296.4 10.6 %fusion.7 = bf16[768,3584]{0,1:T(8,128)(2,1)S(1)} fusion(f32[768,3584]{0,1:T(8,128)} %all-reduce.2.cloned.1.call-done, bf16[768,3584]{0,1:T(8,128)(2,1)} %copy.23, bf16[768,3584]{0,1:T(8,128)(2,1)} %copy.24), kind=kLoop, calls=%fused_computation.19 | loop fusion | flops 33030144 | bytes 27525120 | tf_op jit(solution)/shard_map/convert_element_type | solution.py:14
  307.0 2.8 copy-done.2
  309.8 0.3 copy-done.1
  310.1 13.5 %fusion.24 = f32[768,2048]{1,0:T(8,128)} fusion(bf16[768,3584]{0,1:T(8,128)(2,1)S(1)} %fusion.7, bf16[2048,3584]{0,1:T(8,128)(2,1)S(1)} %copy-done.1), kind=kOutput, calls=%fused_computation.38 | convolution fusion | flops 11274289152 | bytes 26476544 | tf_op jit(solution)/shard_map/dot_general | solution.py:69
  323.6 21.8 %convolution_add_fusion = f32[768,2048]{1,0:T(8,128)} fusion(f32[768,2048]{1,0:T(8,128)} %fusion.24, bf16[2048,3584]{0,1:T(8,128)(2,1)} %bitcast_multiply_fusion.5, f32[768,3584]{0,1:T(8,128)} %all-reduce.2.cloned.1.call-done, bf16[768,3584]{0,1:T(8,128)(2,1)S(1)} %bitcast.65), kind=kOutput, calls=%fused_computation.29 | convolution fusion | flops 11295129600 | bytes 43778048 | tf_op jit(solution)/shard_map/dot_general | solution.py:74
  345.7 0.1 broadcast_bitcast_fusion
  346.2 0.1 broadcast_in_dim.40
  346.3 10.2 %broadcast_in_dim.41 = f32[3584,16,128]{2,1,0:T(8,128)} broadcast(f32[3584,16]{1,0:T(8,128)S(1)} %bitcast.67), dimensions={0,1} | broadcast | bytes 29589504 | tf_op jit(solution)/shard_map/broadcast_in_dim | solution.py:10
  356.6 30.9 %fusion = bf16[3584,2048]{1,0:T(8,128)(2,1)} fusion(f32[448,8,16,128]{3,2,1,0:T(8,128)} %bitcast.63, bf16[768,2048]{1,0:T(8,128)(2,1)} %all-gather.3.cloned.1.call-done, bf16[768,3584]{0,1:T(8,128)(2,1)} %copy.23, bf16[768,3584]{0,1:T(8,128)(2,1)} %copy.24), kind=kOutput, calls=%fused_computation.1 | convolution fusion | flops 11310989312 | bytes 58195968 | tf_op jit(solution)/shard_map/dot_general | solution.py:44
  387.5 18.3 %fusion.2 = bf16[2048,3584]{0,1:T(8,128)(2,1)} fusion(bf16[768,3584]{0,1:T(8,128)(2,1)} %copy-done.2, bf16[768,2048]{1,0:T(8,128)(2,1)} %all-gather.5.cloned.1.call-done, f32[2048,28]{0,1:T(8,128)S(1)} %bitcast.76), kind=kOutput, calls=%fused_computation.5 | convolution fusion | flops 11288969216 | bytes 23560192 | tf_op jit(solution)/shard_map/dot_general | solution.py:58
  405.7 18.8 %copy.32 = bf16[2048,3584]{1,0:T(8,128)(2,1)} copy(bf16[2048,3584]{0,1:T(8,128)(2,1)} %fusion.2) | data formatting | bytes 29360128
  424.6 22.4 %fusion.1 = bf16[2048,3584]{0,1:T(8,128)(2,1)} fusion(bf16[768,2048]{1,0:T(8,128)(2,1)S(1)} %copy-done.5, f32[2048,28]{0,1:T(8,128)S(1)} %bitcast.75, f32[768,3584]{0,1:T(8,128)} %all-reduce.2.cloned.1.call-done, bf16[768,3584]{0,1:T(8,128)(2,1)} %copy.24), kind=kOutput, calls=%fused_computation.3 | convolution fusion | flops 11308236800 | bytes 34570240 | tf_op jit(solution)/shard_map/dot_general | solution.py:61
  447.0 18.6 %copy.33 = bf16[2048,3584]{1,0:T(8,128)(2,1)} copy(bf16[2048,3584]{0,1:T(8,128)(2,1)} %fusion.1) | data formatting | bytes 29360128
  465.6 1.9 convert_element_type.106
  (38 shorter events, 1.2 us)
Async XLA Ops:
  7.2 43.5 %all-gather.3.cloned.1.call-start = ((), (), s32[]{:S(2)}) async-start(), calls=%async_computation.1 | async-start | bytes 3538944 | tf_op jit(solution)/shard_map/all_gather | solution.py:43
  7.9 288.5 %all-reduce.2.cloned.1.call-start = ((), (), s32[]{:S(2)}) async-start(), calls=%async_computation.2 | async-start | bytes 22020096 | tf_op jit(solution)/shard_map/psum | solution.py:53
  83.1 1.0 copy-start.3
  83.1 1.1 copy-start.4
  83.1 304.4 %all-gather.5.cloned.1.call-start = ((), (), s32[]{:S(2)}) async-start(), calls=%async_computation.4 | async-start | bytes 3538944 | tf_op jit(solution)/shard_map/all_gather | solution.py:55
  83.8 381.8 %reduce-scatter.2.cloned.1.call-start = ((), (), s32[]{:S(2)}) async-start(), calls=%async_computation.3 | async-start | bytes 7077888 | tf_op jit(solution)/shard_map/reduce_scatter | solution.py:72
  141.6 15.5 %copy-start = (bf16[2048,3584]{0,1:T(8,128)(2,1)S(1)}, bf16[2048,3584]{0,1:T(8,128)(2,1)}, u32[]{:S(2)}) copy-start(bf16[2048,3584]{0,1:T(8,128)(2,1)} %copy.28) | copy-start | bytes 44040196
  296.4 13.7 %copy-start.1 = (bf16[2048,3584]{0,1:T(8,128)(2,1)S(1)}, bf16[2048,3584]{0,1:T(8,128)(2,1)}, u32[]{:S(2)}) copy-start(bf16[2048,3584]{0,1:T(8,128)(2,1)} %bitcast_multiply_fusion.6) | copy-start | bytes 44040196
  296.4 27.2 %slice-start = ((s8[5505024]{0:T(1024)(128)(4,1)}), s8[4194304]{0:T(1024)(128)(4,1)S(1)}, s32[]{:S(2)}) async-start(s8[5505024]{0:T(1024)(128)(4,1)} %bitcast.64), calls=%async_computation.5 | async-start | bytes 8388608
  307.0 2.8 copy-start.2
  310.1 13.5 %slice-start.1 = ((s8[5505024]{0:T(1024)(128)(4,1)}), s8[1310720]{0:T(1024)(128)(4,1)S(1)}, s32[]{:S(2)}) async-start(s8[5505024]{0:T(1024)(128)(4,1)} %bitcast.64), calls=%async_computation.6 | async-start | bytes 2621440
  405.7 18.8 %copy-start.5 = (bf16[768,2048]{1,0:T(8,128)(2,1)S(1)}, bf16[768,2048]{1,0:T(8,128)(2,1)}, u32[]{:S(2)}) copy-start(bf16[768,2048]{1,0:T(8,128)(2,1)} %all-gather.5.cloned.1.call-done) | copy-start | bytes 9437188
Sparse Core Ops, SparseCore 0:
  9.6 40.9 all-gather.2
  83.2 213.1 all-reduce.1
  298.1 38.2 all-gather.4
  345.6 69.9 reduce-scatter.1
where the time goes:
time: 483 us; the launch traced here: 475 us
  waiting for transfers between devices  177 us (37%)
  matrix products  129 us (27%)
  local copies, waits for them, and re-layouts  121 us (25%)
  other arithmetic  33.1 us (7%)
  between operations  14.5 us (3%)
    psum x1, waiting for transfers between devices, shards(): hidden_grad = lax.psum(hidden_partial, 'pipe')  133 us
    unnamed x34, local copies, waits for them, and re-layouts  99.9 us
    all_gather x1, waiting for transfers between devices, shards(): piece = lax.all_gather(out_grad, 'tensor', axis=0, tiled=True)  41.8 us
    dot_general x1, matrix products, shards(): lax.dot_general(hidden, piece, (((0,), (0,)), ((), ())), preferred_elemen...  30.9 us
    dot_general x1, matrix products, shards(): lax.dot_general(piece, down_masked, (((1,), (1,)), ((), ())), preferred_e...  22.5 us
    dot_general x1, matrix products, shards(): lax.dot_general(piece, up_rows, (((0,), (0,)), ((), ())), preferred_eleme...  22.4 us
    dot_general x1, matrix products, shards(): lax.dot_general(up_rows, up_masked, (((1,), (1,)), ((), ())), preferred_e...  21.8 us
    broadcast_in_dim x4, local copies, waits for them, and re-layouts, expand(): return jnp.repeat(jnp.repeat(mask, BLOCK, axis=0), BLOCK, axis=1)  20.3 us
  transfers between devices with their start and end apart: 4, of which 2 were waited for; matrix products, arithmetic and copies ran while one was open for 51% of the time, Pallas kernels for 0%

commit v1 on v0

v1 whole, which is shorter than its diff:
```python
import functools

import jax
import jax.numpy as jnp
from jax import lax
from jax.experimental import pallas as pl
from jax.experimental.pallas import tpu as pltpu
from jax.sharding import PartitionSpec as P

BLOCK = 128
COLS = 256
BF16 = jnp.bfloat16
F32 = jnp.float32
VMEM_BYTES = 60 * 1024 * 1024
NT = (((1,), (1,)), ((), ()))
NN = (((1,), (0,)), ((), ()))


def params():
    return pltpu.CompilerParams(vmem_limit_bytes=VMEM_BYTES)


def ring_of(chips):
    return [0] + list(range(1, chips, 2)) + [c for c in range(chips - 1, 0, -1) if c % 2 == 0]


class Axes:
    def __init__(self, mesh):
        self.pipe = mesh.shape["pipe"]
        self.tensor = mesh.shape["tensor"]
        self.chips = self.tensor // 2
        ring = ring_of(self.chips)
        table = [[ring[(ring.index(c) - s) % self.chips] for s in range(self.chips)] for c in range(self.chips)]
        self.ring = ring
        self.table = table

    def scalars(self):
        me = lax.axis_index("tensor")
        slots = lax.dynamic_slice(jnp.array(self.table, jnp.int32), (me // 2, 0), (1, self.chips))[0]
        head = jnp.stack([lax.axis_index("pipe"), me % 2]).astype(jnp.int32)
        return jnp.concatenate([head, slots])

    def to_core(self, x):
        return lax.ppermute(x, "tensor", [(t, t ^ 1) for t in range(self.tensor)])

    def to_next(self, x):
        pairs = [(self.ring[i], self.ring[(i + 1) % self.chips]) for i in range(self.chips)]
        return lax.ppermute(x, "tensor", [(2 * a + k, 2 * b + k) for a, b in pairs for k in range(2)])

    def to_pipe(self, x, bit):
        return lax.ppermute(x, "pipe", [(i, i ^ bit) for i in range(self.pipe)])


def place_in(index, order):
    out = 0
    for bit in order:
        out = out * 2 + (1 if index & bit else 0)
    return out


def partial_kernel(cfg, scal, *refs):
    own, sib = refs[: cfg["slots"]], refs[cfg["slots"] : 2 * cfg["slots"]]
    down, mask = refs[2 * cfg["slots"] : 2 * cfg["slots"] + 2]
    outs = refs[2 * cfg["slots"] + 2 : -1]
    rows = refs[-1]
    step = pl.program_id(0)
    pipe, part, tok, unit = cfg["pipe"], cfg["part"], cfg["tok"], cfg["unit"]

    @pl.when(step == 0)
    def _():
        place, core = scal[0], scal[1]
        for s in range(cfg["slots"]):
            for ref, which in ((own[s], core), (sib[s], 1 - core)):
                for h in range(tok // unit):
                    at = (2 * s + which) * tok + h * unit
                    quarter = lax.div(at, part)
                    to = (quarter ^ place) * part + (at - quarter * part)
                    rows[pl.ds(pl.multiple_of(to, 16), unit), :] = ref[h * unit : (h + 1) * unit, :]

    kept = [down[i * BLOCK : (i + 1) * BLOCK, :] * mask[i].astype(BF16) for i in range(COLS // BLOCK)]
    acc = lax.dot_general(rows[...], jnp.concatenate(kept, axis=0), NT, preferred_element_type=F32)
    half = pipe // 2
    first = 0
    for i, (order, steps) in enumerate(cfg["subs"]):
        send, keep = outs[2 * i], outs[2 * i + 1]

        def store(send=send, keep=keep, order=order):
            for r in range(pipe):
                to = place_in(r, order)
                block = acc[r * part : (r + 1) * part, :]
                if to >= half:
                    send[to - half] = block.astype(BF16)
                else:
                    keep[to] = block

        if len(cfg["subs"]) == 1:
            store()
        else:
            pl.when((step >= first) & (step < first + steps))(store)
        first += steps


def partial_sums(axes, scal, own, sib, down, mask, subs):
    tok, width = own[0].shape
    slots = len(own)
    rows = 2 * slots * tok
    part = rows // axes.pipe
    unit = max(u for u in (16, 32, 48, 96, 144) if tok % u == 0 and part % u == 0)
    start = subs[0][0] // COLS
    steps = sum(w for _, w, _ in subs) // COLS
    half = axes.pipe // 2
    cfg = dict(slots=slots, pipe=axes.pipe, part=part, tok=tok, unit=unit, subs=[(o, w // COLS) for _, w, o in subs])
    shapes, specs = [], []
    first = 0
    for _, w, _ in subs:
        n = w // COLS

        def where(k, _, first=first, n=n):
            return (0, 0, jnp.clip(k - first, 0, n - 1))

        for kind in (BF16, F32):
            shapes.append(jax.ShapeDtypeStruct((half, part, w), kind))
            specs.append(pl.BlockSpec((half, part, COLS), where))
        first += n
    whole = pl.BlockSpec((tok, width), lambda k, _: (0, 0))
    blocks = COLS // BLOCK
    out = pl.pallas_call(
        functools.partial(partial_kernel, cfg),
        out_shape=shapes,
        grid_spec=pltpu.PrefetchScalarGridSpec(
            num_scalar_prefetch=1,
            grid=(steps,),
            in_specs=[whole] * (2 * slots)
            + [
                pl.BlockSpec((COLS, width), lambda k, _: (start + k, 0)),
                pl.BlockSpec((blocks, 1, width), lambda k, _: (start + k, 0, 0)),
            ],
            out_specs=specs,
            scratch_shapes=[pltpu.VMEM((rows, width), BF16)],
        ),
        compiler_params=params(),
        cost_estimate=pl.CostEstimate(
            flops=2 * rows * width * steps * COLS,
            bytes_accessed=2 * (rows * width + width * steps * COLS) + 3 * rows * steps * COLS,
            transcendentals=0,
        ),
        name="partial_sums",
    )(scal, *own, *sib, down, mask)
    return [(out[2 * i], out[2 * i + 1]) for i in range(len(subs))]


def reduce_over_pipe(axes, send, keep, order):
    count = axes.pipe // 2
    for bit in order:
        total = keep + axes.to_pipe(send, bit).astype(F32)
        count //= 2
        if count:
            send, keep = total[count:].astype(BF16), total[:count]
    held = {0: total[0].astype(BF16)}
    for bit in reversed(order):
        for r in list(held):
            held[r ^ bit] = axes.to_pipe(held[r], bit)
    return [held[r] for r in range(axes.pipe)]


def grads_kernel(cfg, scal, *refs):
    refs = list(refs)
    sources = []
    for src in cfg["sources"]:
        sources.append([refs.pop(0) for _ in range(cfg["pipe"])])
    gate_pre, up_pre, gate_w, up_w, gate_m, up_m = [refs.pop(0) for _ in range(6)]
    acc_in = refs.pop(0) if cfg["acc_in"] else None
    gate_out, up_out = refs.pop(0), refs.pop(0)
    if cfg["last"]:
        mine = [refs.pop(0) for _ in range(cfg["chips"])]
        theirs = refs.pop(0)
    else:
        acc_out = refs.pop(0)
    hidden, both, acc = refs
    step = pl.program_id(0)
    place, core = scal[0], scal[1]
    per = 2 * cfg["tok"]

    for src, arrays in zip(cfg["sources"], sources):

        def copy(src=src, arrays=arrays):
            for r in range(cfg["pipe"]):
                to = src["base"] + (place ^ r) * src["part"]
                hidden[pl.ds(pl.multiple_of(to, 16), src["part"]), :] = arrays[r][...]

        if src["lo"] <= 0 and src["hi"] >= cfg["steps"]:
            copy()
        else:
            pl.when((step >= src["lo"]) & (step < src["hi"]))(copy)

    for s in range(cfg["chips"]):
        at = pl.ds(pl.multiple_of(scal[2 + s] * per, 16), per)
        rows = slice(s * per, (s + 1) * per)
        g = gate_pre[at, :].astype(F32)
        u = up_pre[at, :].astype(F32)
        h = hidden[rows, :].astype(F32)
        sig = 1.0 / (1.0 + jnp.exp(-g))
        gg = (h * u * sig * (1.0 + g * (1.0 - sig))).astype(BF16)
        ug = (h * g * sig).astype(BF16)
        gate_out[rows, :] = gg
        up_out[rows, :] = ug
        both[rows, :COLS] = gg
        both[rows, COLS:] = ug

    def tile(n, first):
        def masked(w, m):
            two = []
            for i in range(COLS // BLOCK):
                at = pl.ds(pl.multiple_of(n * COLS + i * BLOCK, BLOCK), BLOCK)
                two.append(w[at, :] * m[pl.ds(n * (COLS // BLOCK) + i, 1), :].astype(BF16))
            return jnp.concatenate(two, axis=0)

        w = jnp.concatenate([masked(gate_w, gate_m), masked(up_w, up_m)], axis=1)
        to = pl.ds(pl.multiple_of(n * COLS, COLS), COLS)
        term = lax.dot_general(both[...], w, NT, preferred_element_type=F32)
        if first:
            acc[:, to] = term
        else:
            acc[:, to] += term

    tiles = cfg["width"] // COLS

    @pl.when(step == 0)
    def _():
        pl.loop(0, tiles)(lambda n: tile(n, True))

    @pl.when(step > 0)
    def _():
        pl.loop(0, tiles)(lambda n: tile(n, False))

    @pl.when(step == cfg["steps"] - 1)
    def _():
        tok = cfg["tok"]
        if not cfg["last"]:
            acc_out[...] = acc[...] + acc_in[...] if cfg["acc_in"] else acc[...]
            return

        def take(s, which):
            at = pl.ds(pl.multiple_of(s * per + which * tok, 16), tok)
            return acc[at, :] + acc_in[at, :] if cfg["acc_in"] else acc[at, :]

        for s in range(cfg["chips"]):
            mine[s][...] = take(s, core)
            theirs[s] = take(s, 1 - core).astype(BF16)


def grads(axes, scal, sources, gate_pre, up_pre, gate_w, up_w, gate_m, up_m, acc, start, cols, last):
    tokens = gate_pre.shape[0]
    width = gate_w.shape[0]
    tok = tokens // axes.tensor
    steps = cols // COLS
    first = start // COLS
    infos, specs, arrays = [], [], []
    for parts, base, part, c0, w in sources:
        lo, n = (c0 - start) // COLS, w // COLS
        infos.append(dict(base=base, part=part, lo=lo, hi=lo + n))
        for a in parts:
            arrays.append(a)
            specs.append(pl.BlockSpec((part, COLS), lambda k, _, lo=lo, n=n: (0, jnp.clip(k - lo, 0, n - 1))))
    col = lambda k, _: (0, first + k)
    one = lambda k, _: (0, 0)
    specs += [pl.BlockSpec((tokens, COLS), col)] * 2
    specs += [pl.BlockSpec((width, COLS), col)] * 2
    specs += [pl.BlockSpec((gate_m.shape[0], COLS), col)] * 2
    arrays += [gate_pre, up_pre, gate_w, up_w, gate_m, up_m]
    if acc is not None:
        specs.append(pl.BlockSpec((tokens, width), one, pipeline_mode=pl.Buffered(1)))
        arrays.append(acc)
    shapes = [jax.ShapeDtypeStruct((tokens, cols), BF16)] * 2
    out_specs = [pl.BlockSpec((tokens, COLS), lambda k, _: (0, k))] * 2
    if last:
        shapes += [jax.ShapeDtypeStruct((tok, width), F32)] * axes.chips
        out_specs += [pl.BlockSpec((tok, width), one)] * axes.chips
        shapes.append(jax.ShapeDtypeStruct((axes.chips, tok, width), BF16))
        out_specs.append(pl.BlockSpec((axes.chips, tok, width), lambda k, _: (0, 0, 0)))
    else:
        shapes.append(jax.ShapeDtypeStruct((tokens, width), F32))
        out_specs.append(pl.BlockSpec((tokens, width), one))
    cfg = dict(
        sources=infos, pipe=axes.pipe, chips=axes.chips, tok=tok, steps=steps, width=width, last=last,
        acc_in=acc is not None,
    )
    return pl.pallas_call(
        functools.partial(grads_kernel, cfg),
        out_shape=shapes,
        grid_spec=pltpu.PrefetchScalarGridSpec(
            num_scalar_prefetch=1,
            grid=(steps,),
            in_specs=specs,
            out_specs=out_specs,
            scratch_shapes=[
                pltpu.VMEM((tokens, COLS), BF16),
                pltpu.VMEM((tokens, 2 * COLS), BF16),
                pltpu.VMEM((tokens, width), F32),
            ],
        ),
        compiler_params=params(),
        cost_estimate=pl.CostEstimate(
            flops=4 * tokens * width * cols,
            bytes_accessed=4 * width * cols + 10 * tokens * cols + 8 * tokens * width,
            transcendentals=tokens * cols,
        ),
        name="hidden_grads",
    )(scal, *arrays)


def weights_kernel(cfg, x, gate, up, gate_m, up_m, *refs):
    outs = refs[-2:]
    chunk = cfg["chunk"]
    for g, m, out in ((gate, gate_m, outs[0]), (up, up_m, outs[1])):

        def tile(n, g=g, m=m, out=out):
            at = pl.ds(pl.multiple_of(n * chunk, chunk), chunk)
            term = lax.dot_general(x[at, :], g[...], NN, preferred_element_type=F32)
            for i in range(chunk // BLOCK):
                to = pl.ds(pl.multiple_of(n * chunk + i * BLOCK, BLOCK), BLOCK)
                row = m[pl.ds(n * (chunk // BLOCK) + i, 1), :]
                out[to, :] = (term[i * BLOCK : (i + 1) * BLOCK, :] * row).astype(BF16)

        pl.loop(0, cfg["width"] // chunk)(tile)


def weight_grads(x_t, gate, up, gate_m, up_m, before, shape, start):
    width, tokens = x_t.shape
    steps = gate.shape[1] // COLS
    first = start // COLS
    chunk = 512 if width % 512 == 0 else BLOCK
    col = lambda k: (0, first + k)
    specs = [
        pl.BlockSpec((width, tokens), lambda k: (0, 0), pipeline_mode=pl.Buffered(1)),
        pl.BlockSpec((tokens, COLS), lambda k: (0, k)),
        pl.BlockSpec((tokens, COLS), lambda k: (0, k)),
        pl.BlockSpec((gate_m.shape[0], COLS), col),
        pl.BlockSpec((gate_m.shape[0], COLS), col),
    ]
    arrays = [x_t, gate, up, gate_m, up_m]
    alias = {}
    if before is not None:
        specs += [pl.BlockSpec(memory_space=pl.ANY)] * 2
        arrays += list(before)
        alias = {5: 0, 6: 1}
    return pl.pallas_call(
        functools.partial(weights_kernel, dict(width=width, chunk=chunk)),
        out_shape=[jax.ShapeDtypeStruct(shape, BF16)] * 2,
        grid=(steps,),
        in_specs=specs,
        out_specs=[pl.BlockSpec((width, COLS), col)] * 2,
        input_output_aliases=alias,
        compiler_params=params(),
        cost_estimate=pl.CostEstimate(
            flops=4 * tokens * width * steps * COLS,
            bytes_accessed=4 * (width + tokens) * steps * COLS + 2 * tokens * width,
            transcendentals=0,
        ),
        name="weight_grads",
    )(*arrays)


def down_kernel(cfg, scal, *refs):
    chips, tok = cfg["chips"], cfg["tok"]
    own, sib = refs[:chips], refs[chips : 2 * chips]
    gate_pre, up_pre, mask, out, rows = refs[2 * chips :]
    core = scal[1]
    per = 2 * tok

    @pl.when(pl.program_id(0) == 0)
    def _():
        for s in range(chips):
            base = scal[2 + s] * per
            for ref, which in ((own[s], core), (sib[s], 1 - core)):
                rows[pl.ds(pl.multiple_of(base + which * tok, 16), tok), :] = ref[...]

    g = gate_pre[...].astype(F32)
    u = up_pre[...].astype(F32)
    hidden = (g * (1.0 / (1.0 + jnp.exp(-g))) * u).astype(BF16).T
    chunk = cfg["chunk"]

    def tile(n):
        at = pl.ds(pl.multiple_of(n * chunk, chunk), chunk)
        term = lax.dot_general(hidden, rows[:, at], NN, preferred_element_type=F32)
        for i in range(COLS // BLOCK):
            part = slice(i * BLOCK, (i + 1) * BLOCK)
            out[part, at] = (term[part, :] * mask[i, :, at]).astype(BF16)

    pl.loop(0, cfg["width"] // chunk)(tile)


def down_grad(axes, scal, own, sib, gate_pre, up_pre, mask):
    tokens, hid = gate_pre.shape
    tok, width = own[0].shape
    whole = pl.BlockSpec((tok, width), lambda k, _: (0, 0), pipeline_mode=pl.Buffered(1))
    blocks = COLS // BLOCK
    cfg = dict(chips=axes.chips, tok=tok, width=width, chunk=512 if width % 512 == 0 else BLOCK)
    return pl.pallas_call(
        functools.partial(down_kernel, cfg),
        out_shape=jax.ShapeDtypeStruct((hid, width), BF16),
        grid_spec=pltpu.PrefetchScalarGridSpec(
            num_scalar_prefetch=1,
            grid=(hid // COLS,),
            in_specs=[whole] * (2 * axes.chips)
            + [pl.BlockSpec((tokens, COLS), lambda k, _: (0, k))] * 2
            + [pl.BlockSpec((blocks, 1, width), lambda k, _: (k, 0, 0))],
            out_specs=pl.BlockSpec((COLS, width), lambda k, _: (k, 0)),
            scratch_shapes=[pltpu.VMEM((tokens, width), BF16)],
        ),
        compiler_params=params(),
        cost_estimate=pl.CostEstimate(
            flops=2 * tokens * width * hid,
            bytes_accessed=2 * (tokens * width + 2 * tokens * hid + width * hid),
            transcendentals=tokens * hid,
        ),
        name="down_grad",
    )(scal, *own, *sib, gate_pre, up_pre, mask)


def gather(axes, x):
    own = [x]
    for _ in range(axes.chips - 1):
        own.append(axes.to_next(own[-1]))
    return own, [axes.to_core(a) for a in own]


def pieces_of(hid, orders):
    pieces, at = [], 0
    while at < hid:
        width = min(1024, hid - at)
        half = width // 2 // COLS * COLS
        if half:
            pieces.append([(at, half, orders[0]), (at + half, width - half, orders[1])])
        else:
            pieces.append([(at, width, orders[0])])
        at += width
    return pieces


def shards(axes, layer_input, out_grad, gate_pre, up_pre, gate_weight, up_weight, down_weight, gate_mask, up_mask, down_mask):
    tokens, hid = gate_pre.shape
    tok = out_grad.shape[0]
    scal = axes.scalars()
    gate_m = jnp.repeat(gate_mask, BLOCK, axis=1).astype(F32)
    up_m = jnp.repeat(up_mask, BLOCK, axis=1).astype(F32)
    down_m = jnp.repeat(down_mask, BLOCK, axis=1).astype(F32)[:, None, :]

    bits = [1 << i for i in range(axes.pipe.bit_length() - 1)]
    orders = [bits, bits[::-1]]
    own, sib = gather(axes, out_grad)
    x_own, x_sib = gather(axes, lax.optimization_barrier((layer_input, own[-1]))[0])

    early = 1 if (2 * tok) % (16 * axes.pipe) == 0 and axes.chips > 1 else 0
    pieces = pieces_of(hid, orders)
    sources = []
    if early:
        part = 2 * tok // axes.pipe
        split = sum(w for _, w, _ in pieces[0] + (pieces[1] if len(pieces) > 1 else []))
        subs = [(0, split, orders[0])] + ([(split, hid - split, orders[1])] if split < hid else [])
        for sub in subs:
            send, keep = partial_sums(axes, scal, own[:1], sib[:1], down_weight, down_m, [sub])[0]
            sources.append((reduce_over_pipe(axes, send, keep, sub[2]), 0, part, sub[0], sub[1]))
    part = (tokens - early * 2 * tok) // axes.pipe
    late = []
    for subs in pieces:
        sums = partial_sums(axes, scal, own[early:], sib[early:], down_weight, down_m, subs)
        late.append(
            [
                (reduce_over_pipe(axes, send, keep, sub[2]), early * 2 * tok, part, sub[0], sub[1])
                for (send, keep), sub in zip(sums, subs)
            ]
        )

    grad_down = down_grad(axes, scal, own, sib, gate_pre, up_pre, down_m)
    core = lax.axis_index("tensor") % 2
    ordered = []
    for a, b in zip(x_own, x_sib):
        ordered += [jnp.where(core == 0, a, b), jnp.where(core == 0, b, a)]
    x_t = jnp.concatenate(ordered, axis=0).T

    acc, weights = None, None
    for i, subs in enumerate(pieces):
        start, cols = subs[0][0], sum(w for _, w, _ in subs)
        using = [s for s in sources if s[3] < start + cols and s[3] + s[4] > start] + late[i]
        last = i == len(pieces) - 1
        out = grads(
            axes, scal, using, gate_pre, up_pre, gate_weight, up_weight, gate_m, up_m, acc, start, cols, last
        )
        acc = out[2]
        weights = weight_grads(x_t, out[0], out[1], gate_m, up_m, weights, gate_weight.shape, start)
    mine, theirs = out[2:-1], axes.to_core(out[-1])
    total = [m + theirs[s].astype(F32) for s, m in enumerate(mine)]
    run = None
    for s in list(range(1, axes.chips)) + [0]:
        run = total[s] if run is None else axes.to_next(run.astype(BF16)).astype(F32) + total[s]
    return (run.astype(BF16), weights[0], weights[1], grad_down)


def solution(mesh):
    in_specs = (
        P("tensor", "pipe"),
        P("tensor", "pipe"),
        P(None, "tensor"),
        P(None, "tensor"),
        P("pipe", "tensor"),
        P("pipe", "tensor"),
        P("tensor", "pipe"),
        P("pipe", "tensor"),
        P("pipe", "tensor"),
        P("tensor", "pipe"),
    )
    out_specs = (P("tensor", "pipe"), P("pipe", "tensor"), P("pipe", "tensor"), P("tensor", "pipe"))
    return jax.shard_map(
        functools.partial(shards, Axes(mesh)), mesh=mesh, in_specs=in_specs, out_specs=out_specs, check_vma=False
    )
```

time: 483 us -> 391 us (0.81); the launches traced: 475 us -> 389 us
  Pallas kernels: 0 us -> 219 us
  matrix products: 129 us -> 0 us
  waiting for transfers between devices: 177 us -> 65.9 us
  local copies, waits for them, and re-layouts: 121 us -> 13.4 us
  starting transfers between devices: 0.33 us -> 74.2 us
  other arithmetic: 33.1 us -> 15.2 us
  between operations: 14.5 us -> 1.49 us
    pallas_call x0 -> x15, Pallas kernels: none -> 219 us  [the longest x4 84.4 us: grads(): pl.pallas_call(functools.partial(grads_kernel, cfg), out_shape=shapes, gr...]
    psum x1 -> x0, waiting for transfers between devices: 133 us -> none  [shards(): hidden_grad = lax.psum(hidden_partial, 'pipe')]
    dot_general x6 -> x0, matrix products: 129 us -> none  [the longest x1 30.9 us: shards(): lax.dot_general(hidden, piece, (((0,), (0,)), ((), ())), preferred_elemen...]
    unnamed x34 -> x114, local copies, waits for them, and re-layouts: 99.9 us -> 2.71 us
    ppermute x0 -> x68, starting transfers between devices: none -> 74.2 us  [the longest x50 57.6 us: to_pipe(): return lax.ppermute(x, 'pipe', [(i, i ^ bit) for i in range(self.pipe)])]
    ppermute x0 -> x68, waiting for transfers between devices: none -> 65.9 us  [the longest x50 51.7 us: to_pipe(): return lax.ppermute(x, 'pipe', [(i, i ^ bit) for i in range(self.pipe)])]
    all_gather x2 -> x0, waiting for transfers between devices: 41.8 us -> none  [the longest x1 41.8 us: shards(): piece = lax.all_gather(out_grad, 'tensor', axis=0, tiled=True)]
    mul x2 -> x0, other arithmetic: 19.8 us -> none  [the longest x1 13.9 us: shards(): gate_masked = gate_weight * mask_gate.astype(jnp.bfloat16)]
  transfers between devices with their start and end apart: 4 -> 68, of which waited for: 2 -> 20; matrix products, arithmetic and copies ran while one was open for 51% -> 5% of each run, Pallas kernels for 0% -> 56%
where the time goes in v1:
time: 391 us; the launch traced here: 389 us
  Pallas kernels  219 us (56%)
  starting transfers between devices  74.2 us (19%)
  waiting for transfers between devices  65.9 us (17%)
  other arithmetic  15.2 us (4%)
  local copies, waits for them, and re-layouts  13.4 us (3%)
    pallas_call x4, Pallas kernels, grads(): pl.pallas_call(functools.partial(grads_kernel, cfg), out_shape=shapes, gr...  84.4 us
    ppermute x50, starting transfers between devices, to_pipe(): return lax.ppermute(x, 'pipe', [(i, i ^ bit) for i in range(self.pipe)])  57.6 us
    pallas_call x4, Pallas kernels, weight_grads(): pl.pallas_call(functools.partial(weights_kernel, dict(width=width, chunk=...  57.4 us
    ppermute x50, waiting for transfers between devices, to_pipe(): return lax.ppermute(x, 'pipe', [(i, i ^ bit) for i in range(self.pipe)])  51.7 us
    pallas_call x6, Pallas kernels, partial_sums(): pl.pallas_call(functools.partial(partial_kernel, cfg), out_shape=shapes,...  47 us
    pallas_call x1, Pallas kernels, down_grad(): pl.pallas_call(functools.partial(down_kernel, cfg), out_shape=jax.ShapeDt...  30.4 us
    ppermute x9, starting transfers between devices, to_next(): lax.ppermute(x, 'tensor', [(2 * a + k, 2 * b + k) for a, b in pairs for k...  14.8 us
    ppermute x9, waiting for transfers between devices, to_next(): lax.ppermute(x, 'tensor', [(2 * a + k, 2 * b + k) for a, b in pairs for k...  12.4 us
  transfers between devices with their start and end apart: 68, of which 20 were waited for; matrix products, arithmetic and copies ran while one was open for 5% of the time, Pallas kernels for 56%

profile of v1, /device:TPU:0, one launch (start us, length us, event | category | flops | bytes accessed | tf_op | source)
XLA Modules:
  0.0 389.5 jit_solution(10618296901522861606)
XLA Ops:
  1.1 2.6 collective-permute-start.6
  6.8 8.1 %partial_sums.6 = (bf16[2,48,1536]{2,1,0:T(8,128)(2,1)}, f32[2,48,1536]{2,1,0:T(8,128)}) custom-call(s32[6]{0:T(128)} %pad_add_fusion.scal, bf16[96,2048]{1,0:T(8,128)(2,1)} %refs_0_.5, bf16[96,2048]{1,0:T(8,128)(2,1)} %copy-done.7, bf16[3584,2048]{1,0:T(8,128)(2,1)} %refs_6_.7, f32[28,1,2048]{2,1,0:T(1,128)} %bitcast.56), custom_call_target="tpu_custom_call" | custom-call | flops 1207959552 | bytes 7962624 | tf_op jit(solution)/shard_map/partial_sums/pallas_call | solution.py:127
  16.4 10.0 %partial_sums.9 = (bf16[2,48,2048]{2,1,0:T(8,128)(2,1)}, f32[2,48,2048]{2,1,0:T(8,128)}) custom-call(s32[6]{0:T(128)} %pad_add_fusion.scal, bf16[96,2048]{1,0:T(8,128)(2,1)} %refs_0_.5, bf16[96,2048]{1,0:T(8,128)(2,1)} %copy-done.7, bf16[3584,2048]{1,0:T(8,128)(2,1)} %refs_6_.7, f32[28,1,2048]{2,1,0:T(1,128)} %bitcast.57), custom_call_target="tpu_custom_call" | custom-call | flops 1610612736 | bytes 10354688 | tf_op jit(solution)/shard_map/partial_sums/pallas_call | solution.py:127
  27.9 2.6 collective-permute-start.7
  31.2 7.4 %collective-permute-done.32 = bf16[2,48,2048]{2,1,0:T(8,128)(2,1)S(1)} collective-permute-done((bf16[2,48,2048]{2,1,0:T(8,128)(2,1)}, bf16[2,48,2048]{2,1,0:T(8,128)(2,1)S(1)}, u32[]{:S(2)}, u32[]{:S(2)}) %collective-permute-start.32) | collective-permute-done | bytes 393248 | tf_op jit(solution)/shard_map/ppermute | solution.py:51
  40.4 2.6 collective-permute-start.8
  56.0 5.5 %partial_sums.7 = (bf16[2,144,256]{2,1,0:T(8,128)(2,1)}, f32[2,144,256]{2,1,0:T(8,128)}, bf16[2,144,256]{2,1,0:T(8,128)(2,1)}, f32[2,144,256]{2,1,0:T(8,128)}) custom-call(s32[6]{0:T(128)} %pad_add_fusion.scal, bf16[96,2048]{1,0:T(8,128)(2,1)} %copy-done, bf16[96,2048]{1,0:T(8,128)(2,1)} %copy-done.1, bf16[96,2048]{1,0:T(8,128)(2,1)} %copy-done.2, ...), custom_call_target="tpu_custom_call" | custom-call | flops 1207959552 | bytes 5341184 | tf_op jit(solution)/shard_map/partial_sums/pallas_call | solution.py:127
  63.7 7.7 %partial_sums.8 = (bf16[2,144,512]{2,1,0:T(8,128)(2,1)}, f32[2,144,512]{2,1,0:T(8,128)}, bf16[2,144,512]{2,1,0:T(8,128)(2,1)}, f32[2,144,512]{2,1,0:T(8,128)}) custom-call(s32[6]{0:T(128)} %pad_add_fusion.scal, bf16[96,2048]{1,0:T(8,128)(2,1)} %copy-done, bf16[96,2048]{1,0:T(8,128)(2,1)} %copy-done.1, bf16[96,2048]{1,0:T(8,128)(2,1)} %copy-done.2, ...), custom_call_target="tpu_custom_call" | custom-call | flops 2415919104 | bytes 8323072 | tf_op jit(solution)/shard_map/partial_sums/pallas_call | solution.py:127
  71.5 7.8 %partial_sums.10 = (bf16[2,144,512]{2,1,0:T(8,128)(2,1)}, f32[2,144,512]{2,1,0:T(8,128)}, bf16[2,144,512]{2,1,0:T(8,128)(2,1)}, f32[2,144,512]{2,1,0:T(8,128)}) custom-call(s32[6]{0:T(128)} %pad_add_fusion.scal, bf16[96,2048]{1,0:T(8,128)(2,1)} %copy-done, bf16[96,2048]{1,0:T(8,128)(2,1)} %copy-done.1, bf16[96,2048]{1,0:T(8,128)(2,1)} %copy-done.2, ...), custom_call_target="tpu_custom_call" | custom-call | flops 2415919104 | bytes 8323072 | tf_op jit(solution)/shard_map/partial_sums/pallas_call | solution.py:127
  79.3 30.4 %down_grad.1 = bf16[3584,2048]{1,0:T(8,128)(2,1)} custom-call(s32[6]{0:T(128)} %pad_add_fusion.scal, bf16[96,2048]{1,0:T(8,128)(2,1)} %refs_0_.5, bf16[96,2048]{1,0:T(8,128)(2,1)} %copy-done, bf16[96,2048]{1,0:T(8,128)(2,1)} %copy-done.1, bf16[96,2048]{1,0:T(8,128)(2,1)} %copy-done.2, bf16[96,2048]{1,0:T(8,128)(2,1)} %copy-done.7, ...), custom_call_target="tpu_custom_call" | custom-call | flops 11274289152 | bytes 28835840 | tf_op jit(solution)/shard_map/down_grad/pallas_call | solution.py:399
  109.7 7.9 %partial_sums.11 = (bf16[2,144,512]{2,1,0:T(8,128)(2,1)}, f32[2,144,512]{2,1,0:T(8,128)}, bf16[2,144,512]{2,1,0:T(8,128)(2,1)}, f32[2,144,512]{2,1,0:T(8,128)}) custom-call(s32[6]{0:T(128)} %pad_add_fusion.scal, bf16[96,2048]{1,0:T(8,128)(2,1)} %copy-done, bf16[96,2048]{1,0:T(8,128)(2,1)} %copy-done.1, bf16[96,2048]{1,0:T(8,128)(2,1)} %copy-done.2, ...), custom_call_target="tpu_custom_call" | custom-call | flops 2415919104 | bytes 8323072 | tf_op jit(solution)/shard_map/partial_sums/pallas_call | solution.py:127
  120.7 3.0 collective-permute-done.13
  125.2 2.9 collective-permute-done.18
  132.1 3.7 collective-permute-done.27
  139.6 3.9 %collective-permute-done.42 = bf16[2,144,512]{2,1,0:T(8,128)(2,1)S(1)} collective-permute-done((bf16[2,144,512]{2,1,0:T(8,128)(2,1)}, bf16[2,144,512]{2,1,0:T(8,128)(2,1)S(1)}, u32[]{:S(2)}, u32[]{:S(2)}) %collective-permute-start.42) | collective-permute-done | bytes 294944 | tf_op jit(solution)/shard_map/ppermute | solution.py:51
  146.7 5.1 %collective-permute-done.52 = bf16[2,144,512]{2,1,0:T(8,128)(2,1)S(1)} collective-permute-done((bf16[2,144,512]{2,1,0:T(8,128)(2,1)S(1)}, bf16[2,144,512]{2,1,0:T(8,128)(2,1)S(1)}, u32[]{:S(2)}, u32[]{:S(2)}) %collective-permute-start.52) | collective-permute-done | bytes 294944 | tf_op jit(solution)/shard_map/ppermute | solution.py:51
  153.3 4.2 %collective-permute-done.23 = bf16[1,144,512]{2,1,0:T(8,128)(2,1)S(1)} collective-permute-done((bf16[1,144,512]{2,1,0:T(8,128)(2,1)S(1)}, bf16[1,144,512]{2,1,0:T(8,128)(2,1)S(1)}, u32[]{:S(2)}, u32[]{:S(2)}) %collective-permute-start.23) | collective-permute-done | bytes 147488 | tf_op jit(solution)/shard_map/ppermute | solution.py:51
  159.0 3.7 collective-permute-done.38
  164.1 3.7 collective-permute-done.48
  174.3 3.3 collective-permute-done.34.refs_1_
  178.1 3.8 collective-permute-done.36.refs_3_
  188.6 2.4 collective-permute-start.55
  201.8 21.5 %hidden_grads.4 = (bf16[768,1024]{1,0:T(8,128)(2,1)}, bf16[768,1024]{1,0:T(8,128)(2,1)}, f32[768,2048]{1,0:T(8,128)}) custom-call(s32[6]{0:T(128)} %pad_add_fusion.scal, bf16[48,2048]{1,0:T(8,128)(2,1)} %copy-done.6, bf16[48,2048]{1,0:T(8,128)(2,1)} %copy-done.10, bf16[48,2048]{1,0:T(8,128)(2,1)} %copy-done.9, bf16[48,2048]{1,0:T(8,128)(2,1)} %copy-done.11, ...), custom_call_target="tpu_custom_call" | custom-call | flops 6442450944 | bytes 28835840 | tf_op jit(solution)/shard_map/hidden_grads/pallas_call | solution.py:288
  229.2 23.8 %hidden_grads.5 = (bf16[768,1024]{1,0:T(8,128)(2,1)}, bf16[768,1024]{1,0:T(8,128)(2,1)}, f32[768,2048]{1,0:T(8,128)}) custom-call(s32[6]{0:T(128)} %pad_add_fusion.scal, bf16[48,2048]{1,0:T(8,128)(2,1)} %copy-done.6, bf16[48,2048]{1,0:T(8,128)(2,1)} %copy-done.10, bf16[48,2048]{1,0:T(8,128)(2,1)} %copy-done.9, bf16[48,2048]{1,0:T(8,128)(2,1)} %copy-done.11, ...), custom_call_target="tpu_custom_call" | custom-call | flops 6442450944 | bytes 28835840 | tf_op jit(solution)/shard_map/hidden_grads/pallas_call | solution.py:288
  257.4 23.8 %hidden_grads.6 = (bf16[768,1024]{1,0:T(8,128)(2,1)}, bf16[768,1024]{1,0:T(8,128)(2,1)}, f32[768,2048]{1,0:T(8,128)}) custom-call(s32[6]{0:T(128)} %pad_add_fusion.scal, bf16[48,1536]{1,0:T(8,128)(2,1)} %copy-done.8, bf16[48,1536]{1,0:T(8,128)(2,1)} %collective-permute-done.3.refs_1_, bf16[48,1536]{1,0:T(8,128)(2,1)} %collective-permute-done.4.refs_2_, ...), custom_call_target="tpu_custom_call" | custom-call | flops 6442450944 | bytes 28835840 | tf_op jit(solution)/shard_map/hidden_grads/pallas_call | solution.py:288
  283.1 15.4 %hidden_grads.7 = (bf16[768,512]{1,0:T(8,128)(2,1)}, bf16[768,512]{1,0:T(8,128)(2,1)}, f32[96,2048]{1,0:T(8,128)}, f32[96,2048]{1,0:T(8,128)}, f32[96,2048]{1,0:...) custom-call(s32[6]{0:T(128)} %pad_add_fusion.scal, bf16[48,1536]{1,0:T(8,128)(2,1)} %copy-done.8, ...), custom_call_target="tpu_custom_call" | custom-call | flops 3221225472 | bytes 20709376 | tf_op jit(solution)/shard_map/hidden_grads/pallas_call | solution.py:288
  301.8 12.4 %collective-permute-done.66 = bf16[96,2048]{0,1:T(8,128)(2,1)S(1)} collective-permute-done((bf16[96,2048]{0,1:T(8,128)(2,1)S(1)}, bf16[96,2048]{0,1:T(8,128)(2,1)S(1)}, u32[]{:S(2)}, u32[]{:S(2)}) %collective-permute-start.66) | collective-permute-done | bytes 393248 | tf_op jit(solution)/shard_map/ppermute | solution.py:48
  317.1 6.3 %concatenate.7 = bf16[768,2048]{0,1:T(8,128)(2,1)} concatenate(bf16[96,2048]{0,1:T(8,128)(2,1)S(1)} %get-tuple-element.101, bf16[96,2048]{0,1:T(8,128)(2,1)S(1)} %get-tuple-element.100, bf16[96,2048]{0,1:T(8,128)(2,1)S(1)} %get-tuple-element.99, bf16[96,2048]{0,1:T(8,128)(2,1)S(1)} %get-tuple-element.98, bf16[96,2048]{0,1:T(8,128)(2,1)S(1)} %get-tuple-element.97, ...), dimensions={0} | concatenate | bytes 6291456 | tf_op jit(solution)/shard_map/concatenate | solution.py:480
  325.4 16.0 %weight_grads.4 = (bf16[2048,3584]{1,0:T(8,128)(2,1)}, bf16[2048,3584]{1,0:T(8,128)(2,1)}) custom-call(bf16[2048,768]{1,0:T(8,128)(2,1)} %bitcast.52, bf16[768,1024]{1,0:T(8,128)(2,1)} %get-tuple-element.84.gate, bf16[768,1024]{1,0:T(8,128)(2,1)} %get-tuple-element.85.up, f32[16,3584]{1,0:T(8,128)} %get-tuple-element.103.refs_16_.gate_m, ...), custom_call_target="tpu_custom_call" | custom-call | flops 6442450944 | bytes 14680064 | tf_op jit(solution)/shard_map/weight_grads/pallas_call | solution.py:347
  343.7 15.9 %weight_grads.5 = (bf16[2048,3584]{1,0:T(8,128)(2,1)}, bf16[2048,3584]{1,0:T(8,128)(2,1)}) custom-call(bf16[2048,768]{1,0:T(8,128)(2,1)} %bitcast.53, bf16[768,1024]{1,0:T(8,128)(2,1)} %get-tuple-element.82.gate, bf16[768,1024]{1,0:T(8,128)(2,1)} %get-tuple-element.83.up, ...), custom_call_target="tpu_custom_call", output_to_operand_aliasing={{0}: (5, {}), {1}: (6, {})} | custom-call | flops 6442450944 | bytes 14680064 | tf_op jit(solution)/shard_map/weight_grads/pallas_call | solution.py:347
  362.0 15.8 %weight_grads.6 = (bf16[2048,3584]{1,0:T(8,128)(2,1)}, bf16[2048,3584]{1,0:T(8,128)(2,1)}) custom-call(bf16[2048,768]{1,0:T(8,128)(2,1)} %bitcast.54, bf16[768,1024]{1,0:T(8,128)(2,1)} %get-tuple-element.80.gate, bf16[768,1024]{1,0:T(8,128)(2,1)} %get-tuple-element.81.up, ...), custom_call_target="tpu_custom_call", output_to_operand_aliasing={{0}: (5, {}), {1}: (6, {})} | custom-call | flops 6442450944 | bytes 14680064 | tf_op jit(solution)/shard_map/weight_grads/pallas_call | solution.py:347
  377.8 9.7 %weight_grads.7 = (bf16[2048,3584]{1,0:T(8,128)(2,1)}, bf16[2048,3584]{1,0:T(8,128)(2,1)}) custom-call(bf16[2048,768]{1,0:T(8,128)(2,1)} %bitcast.55, bf16[768,512]{1,0:T(8,128)(2,1)} %get-tuple-element.78.gate, bf16[768,512]{1,0:T(8,128)(2,1)} %get-tuple-element.79.up, ...), custom_call_target="tpu_custom_call", output_to_operand_aliasing={{0}: (5, {}), {1}: (6, {})} | custom-call | flops 3221225472 | bytes 8912896 | tf_op jit(solution)/shard_map/weight_grads/pallas_call | solution.py:347
  (283 shorter events, 95.2 us)
Async XLA Ops:
  1.1 26.7 %collective-permute-start.6 = (bf16[96,2048]{1,0:T(8,128)(2,1)}, bf16[96,2048]{1,0:T(8,128)(2,1)S(1)}, u32[]{:S(2)}, u32[]{:S(2)}) collective-permute-start(bf16[96,2048]{1,0:T(8,128)(2,1)} %refs_0_.5), channel_id=1, source_target_pairs={{0,2},{1,3},{2,6},{3,7},{6,4},{7,5},{4,0},{5,1},{8,10},{9,11},{10,... | collective-permute-start | bytes 1179656 | tf_op jit(solution)/shard_map/ppermute | solution.py:48
  14.8 15.6 %collective-permute-start.1 = (bf16[2,48,1536]{2,1,0:T(8,128)(2,1)}, bf16[2,48,1536]{2,1,0:T(8,128)(2,1)S(1)}, u32[]{:S(2)}, u32[]{:S(2)}) collective-permute-start(bf16[2,48,1536]{2,1,0:T(8,128)(2,1)} %get-tuple-element.50), channel_id=1, source_target_pairs={{0,16},{8,24},{16,0},{24,8},{1,17},{9,25},{17,1},{25,9},{2,18},{10... | collective-permute-start | bytes 884744 | tf_op jit(solution)/shard_map/ppermute | solution.py:51
  48.4 120.7 %collective-permute-start.4 = (bf16[48,1536]{1,0:T(8,128)(2,1)S(1)}, bf16[48,1536]{1,0:T(8,128)(2,1)}, u32[]{:S(2)}, u32[]{:S(2)}) collective-permute-start(bf16[48,1536]{1,0:T(8,128)(2,1)S(1)} %fusion.16.refs_0_), channel_id=1, source_target_pairs={{0,16},{8,24},{16,0},{24,8},{1,17},{9,25},{17,1},{25,9},{2,18},{10... | collective-permute-start | bytes 442376 | tf_op jit(solution)/shard_map/ppermute | solution.py:51
  49.9 121.3 %collective-permute-start.5 = (bf16[48,1536]{1,0:T(8,128)(2,1)}, bf16[48,1536]{1,0:T(8,128)(2,1)}, u32[]{:S(2)}, u32[]{:S(2)}) collective-permute-start(bf16[48,1536]{1,0:T(8,128)(2,1)} %collective-permute-done.3.refs_1_), channel_id=1, source_target_pairs={{0,16},{8,24},{16,0},{24,8},{1,17},{9,25},{17,1},{25,9},{2,18},{10... | collective-permute-start | bytes 442376 | tf_op jit(solution)/shard_map/ppermute | solution.py:51
  53.1 116.9 %collective-permute-start.35 = (bf16[48,2048]{1,0:T(8,128)(2,1)S(1)}, bf16[48,2048]{1,0:T(8,128)(2,1)S(1)}, u32[]{:S(2)}, u32[]{:S(2)}) collective-permute-start(bf16[48,2048]{1,0:T(8,128)(2,1)S(1)} %fusion.15.refs_0_), channel_id=1, source_target_pairs={{0,16},{8,24},{16,0},{24,8},{1,17},{9,25},{17,1},{25,9},{2,18},{10... | collective-permute-start | bytes 589832 | tf_op jit(solution)/shard_map/ppermute | solution.py:51
  61.5 56.1 %collective-permute-start.12 = (bf16[2,144,256]{2,1,0:T(8,128)(2,1)}, bf16[2,144,256]{2,1,0:T(8,128)(2,1)S(1)}, u32[]{:S(2)}, u32[]{:S(2)}) collective-permute-start(bf16[2,144,256]{2,1,0:T(8,128)(2,1)} %get-tuple-element.52), channel_id=1, source_target_pairs={{0,8},{8,0},{16,24},{24,16},{1,9},{9,1},{17,25},{25,17},{2,10},{10... | collective-permute-start | bytes 442376 | tf_op jit(solution)/shard_map/ppermute | solution.py:51
  63.0 56.2 %collective-permute-start.17 = (bf16[2,144,256]{2,1,0:T(8,128)(2,1)}, bf16[2,144,256]{2,1,0:T(8,128)(2,1)S(1)}, u32[]{:S(2)}, u32[]{:S(2)}) collective-permute-start(bf16[2,144,256]{2,1,0:T(8,128)(2,1)} %get-tuple-element.54), channel_id=1, source_target_pairs={{0,16},{8,24},{16,0},{24,8},{1,17},{9,25},{17,1},{25,9},{2,18},{10... | collective-permute-start | bytes 442376 | tf_op jit(solution)/shard_map/ppermute | solution.py:51
  145.4 38.7 %collective-permute-start.62 = (bf16[96,2048]{0,1:T(8,128)(2,1)S(1)}, bf16[96,2048]{0,1:T(8,128)(2,1)}, u32[]{:S(2)}, u32[]{:S(2)}) collective-permute-start(bf16[96,2048]{0,1:T(8,128)(2,1)S(1)} %copy.28), channel_id=1, source_target_pairs={{0,2},{1,3},{2,6},{3,7},{6,4},{7,5},{4,0},{5,1},{8,10},{9,11},{10,... | collective-permute-start | bytes 1179656 | tf_op jit(solution)/shard_map/ppermute | solution.py:48
  171.2 13.0 %collective-permute-start.15 = (bf16[144,256]{1,0:T(8,128)(2,1)S(1)}, bf16[144,256]{1,0:T(8,128)(2,1)S(1)}, u32[]{:S(2)}, u32[]{:S(2)}) collective-permute-start(bf16[144,256]{1,0:T(8,128)(2,1)S(1)} %fusion.25.refs_4_), channel_id=1, source_target_pairs={{0,16},{8,24},{16,0},{24,8},{1,17},{9,25},{17,1},{25,9},{2,18},{10... | collective-permute-start | bytes 221192 | tf_op jit(solution)/shard_map/ppermute | solution.py:51
  197.0 27.8 %collective-permute-start.39 = (bf16[144,512]{1,0:T(8,128)(2,1)S(1)}, bf16[144,512]{1,0:T(8,128)(2,1)S(1)}, u32[]{:S(2)}, u32[]{:S(2)}) collective-permute-start(bf16[144,512]{1,0:T(8,128)(2,1)S(1)} %fusion.19.refs_4_), channel_id=1, source_target_pairs={{0,8},{8,0},{16,24},{24,16},{1,9},{9,1},{17,25},{25,17},{2,10},{10... | collective-permute-start | bytes 442376 | tf_op jit(solution)/shard_map/ppermute | solution.py:51
  197.6 27.9 %collective-permute-start.45 = (bf16[144,512]{1,0:T(8,128)(2,1)S(1)}, bf16[144,512]{1,0:T(8,128)(2,1)S(1)}, u32[]{:S(2)}, u32[]{:S(2)}) collective-permute-start(bf16[144,512]{1,0:T(8,128)(2,1)S(1)} %fusion.20.refs_8_), channel_id=1, source_target_pairs={{0,16},{8,24},{16,0},{24,8},{1,17},{9,25},{17,1},{25,9},{2,18},{10... | collective-permute-start | bytes 442376 | tf_op jit(solution)/shard_map/ppermute | solution.py:51
  199.1 24.2 %collective-permute-start.29 = (bf16[144,512]{1,0:T(8,128)(2,1)S(1)}, bf16[144,512]{1,0:T(8,128)(2,1)S(1)}, u32[]{:S(2)}, u32[]{:S(2)}) collective-permute-start(bf16[144,512]{1,0:T(8,128)(2,1)S(1)} %fusion.18.refs_8_), channel_id=1, source_target_pairs={{0,8},{8,0},{16,24},{24,16},{1,9},{9,1},{17,25},{25,17},{2,10},{10... | collective-permute-start | bytes 442376 | tf_op jit(solution)/shard_map/ppermute | solution.py:51
  200.5 26.6 %collective-permute-start.41 = (bf16[144,512]{1,0:T(8,128)(2,1)S(1)}, bf16[144,512]{1,0:T(8,128)(2,1)S(1)}, u32[]{:S(2)}, u32[]{:S(2)}) collective-permute-start(bf16[144,512]{1,0:T(8,128)(2,1)S(1)} %collective-permute-done.40.refs_6_), channel_id=1, source_target_pairs={{0,8},{8,0},{16,24},{24,16},{1,9},{9,1},{17,25},{25,17},{2,10},{10... | collective-permute-start | bytes 442376 | tf_op jit(solution)/shard_map/ppermute | solution.py:51
  201.1 27.4 %collective-permute-start.46 = (bf16[144,512]{1,0:T(8,128)(2,1)S(1)}, bf16[144,512]{1,0:T(8,128)(2,1)S(1)}, u32[]{:S(2)}, u32[]{:S(2)}) collective-permute-start(bf16[144,512]{1,0:T(8,128)(2,1)S(1)} %collective-permute-done.44.refs_9_), channel_id=1, source_target_pairs={{0,16},{8,24},{16,0},{24,8},{1,17},{9,25},{17,1},{25,9},{2,18},{10... | collective-permute-start | bytes 442376 | tf_op jit(solution)/shard_map/ppermute | solution.py:51
  223.4 29.6 %collective-permute-start.19 = (bf16[144,256]{1,0:T(8,128)(2,1)S(1)}, bf16[144,256]{1,0:T(8,128)(2,1)S(1)}, u32[]{:S(2)}, u32[]{:S(2)}) collective-permute-start(bf16[144,256]{1,0:T(8,128)(2,1)S(1)} %fusion.26.refs_8_), channel_id=1, source_target_pairs={{0,8},{8,0},{16,24},{24,16},{1,9},{9,1},{17,25},{25,17},{2,10},{10... | collective-permute-start | bytes 221192 | tf_op jit(solution)/shard_map/ppermute | solution.py:51
  224.8 28.3 %collective-permute-start.24 = (bf16[144,512]{1,0:T(8,128)(2,1)S(1)}, bf16[144,512]{1,0:T(8,128)(2,1)S(1)}, u32[]{:S(2)}, u32[]{:S(2)}) collective-permute-start(bf16[144,512]{1,0:T(8,128)(2,1)S(1)} %fusion.17.refs_4_), channel_id=1, source_target_pairs={{0,8},{8,0},{16,24},{24,16},{1,9},{9,1},{17,25},{25,17},{2,10},{10... | collective-permute-start | bytes 442376 | tf_op jit(solution)/shard_map/ppermute | solution.py:51
  225.5 28.3 %collective-permute-start.30 = (bf16[144,512]{1,0:T(8,128)(2,1)S(1)}, bf16[144,512]{1,0:T(8,128)(2,1)S(1)}, u32[]{:S(2)}, u32[]{:S(2)}) collective-permute-start(bf16[144,512]{1,0:T(8,128)(2,1)S(1)} %fusion.18.refs_8_), channel_id=1, source_target_pairs={{0,16},{8,24},{16,0},{24,8},{1,17},{9,25},{17,1},{25,9},{2,18},{10... | collective-permute-start | bytes 442376 | tf_op jit(solution)/shard_map/ppermute | solution.py:51
  227.1 28.2 %collective-permute-start.26 = (bf16[144,512]{1,0:T(8,128)(2,1)S(1)}, bf16[144,512]{1,0:T(8,128)(2,1)S(1)}, u32[]{:S(2)}, u32[]{:S(2)}) collective-permute-start(bf16[144,512]{1,0:T(8,128)(2,1)S(1)} %collective-permute-done.25.refs_6_), channel_id=1, source_target_pairs={{0,8},{8,0},{16,24},{24,16},{1,9},{9,1},{17,25},{25,17},{2,10},{10... | collective-permute-start | bytes 442376 | tf_op jit(solution)/shard_map/ppermute | solution.py:51
  228.5 28.2 %collective-permute-start.31 = (bf16[144,512]{1,0:T(8,128)(2,1)S(1)}, bf16[144,512]{1,0:T(8,128)(2,1)S(1)}, u32[]{:S(2)}, u32[]{:S(2)}) collective-permute-start(bf16[144,512]{1,0:T(8,128)(2,1)S(1)} %collective-permute-done.29.refs_9_), channel_id=1, source_target_pairs={{0,16},{8,24},{16,0},{24,8},{1,17},{9,25},{17,1},{25,9},{2,18},{10... | collective-permute-start | bytes 442376 | tf_op jit(solution)/shard_map/ppermute | solution.py:51
  253.0 45.7 %collective-permute-start.61 = (bf16[96,2048]{0,1:T(8,128)(2,1)S(1)}, bf16[96,2048]{0,1:T(8,128)(2,1)S(1)}, u32[]{:S(2)}, u32[]{:S(2)}) collective-permute-start(bf16[96,2048]{0,1:T(8,128)(2,1)S(1)} %copy.28), channel_id=1, source_target_pairs={{0,1},{1,0},{2,3},{3,2},{4,5},{5,4},{6,7},{7,6},{8,9},{9,8},{10,11... | collective-permute-start | bytes 1179656 | tf_op jit(solution)/shard_map/ppermute | solution.py:44
  253.1 28.1 %collective-permute-start.14 = (bf16[144,256]{1,0:T(8,128)(2,1)S(1)}, bf16[144,256]{1,0:T(8,128)(2,1)S(1)}, u32[]{:S(2)}, u32[]{:S(2)}) collective-permute-start(bf16[144,256]{1,0:T(8,128)(2,1)S(1)} %fusion.25.refs_4_), channel_id=1, source_target_pairs={{0,8},{8,0},{16,24},{24,16},{1,9},{9,1},{17,25},{25,17},{2,10},{10... | collective-permute-start | bytes 221192 | tf_op jit(solution)/shard_map/ppermute | solution.py:51
  253.8 27.5 %collective-permute-start.20 = (bf16[144,256]{1,0:T(8,128)(2,1)S(1)}, bf16[144,256]{1,0:T(8,128)(2,1)S(1)}, u32[]{:S(2)}, u32[]{:S(2)}) collective-permute-start(bf16[144,256]{1,0:T(8,128)(2,1)S(1)} %fusion.26.refs_8_), channel_id=1, source_target_pairs={{0,16},{8,24},{16,0},{24,8},{1,17},{9,25},{17,1},{25,9},{2,18},{10... | collective-permute-start | bytes 221192 | tf_op jit(solution)/shard_map/ppermute | solution.py:51
  255.3 27.1 %collective-permute-start.16 = (bf16[144,256]{1,0:T(8,128)(2,1)S(1)}, bf16[144,256]{1,0:T(8,128)(2,1)S(1)}, u32[]{:S(2)}, u32[]{:S(2)}) collective-permute-start(bf16[144,256]{1,0:T(8,128)(2,1)S(1)} %collective-permute-done.15.refs_6_), channel_id=1, source_target_pairs={{0,8},{8,0},{16,24},{24,16},{1,9},{9,1},{17,25},{25,17},{2,10},{10... | collective-permute-start | bytes 221192 | tf_op jit(solution)/shard_map/ppermute | solution.py:51
  256.8 25.6 %collective-permute-start.21 = (bf16[144,256]{1,0:T(8,128)(2,1)S(1)}, bf16[144,256]{1,0:T(8,128)(2,1)S(1)}, u32[]{:S(2)}, u32[]{:S(2)}) collective-permute-start(bf16[144,256]{1,0:T(8,128)(2,1)S(1)} %collective-permute-done.19.refs_9_), channel_id=1, source_target_pairs={{0,16},{8,24},{16,0},{24,8},{1,17},{9,25},{17,1},{25,9},{2,18},{10... | collective-permute-start | bytes 221192 | tf_op jit(solution)/shard_map/ppermute | solution.py:51
  281.2 19.5 %collective-permute-start.63 = (bf16[96,2048]{0,1:T(8,128)(2,1)}, bf16[96,2048]{0,1:T(8,128)(2,1)S(1)}, u32[]{:S(2)}, u32[]{:S(2)}) collective-permute-start(bf16[96,2048]{0,1:T(8,128)(2,1)} %collective-permute-done.62), channel_id=1, source_target_pairs={{0,1},{1,0},{2,3},{3,2},{4,5},{5,4},{6,7},{7,6},{8,9},{9,8},{10,11... | collective-permute-start | bytes 1179656 | tf_op jit(solution)/shard_map/ppermute | solution.py:44
  281.3 17.4 %collective-permute-start.64 = (bf16[96,2048]{0,1:T(8,128)(2,1)}, bf16[96,2048]{0,1:T(8,128)(2,1)S(1)}, u32[]{:S(2)}, u32[]{:S(2)}) collective-permute-start(bf16[96,2048]{0,1:T(8,128)(2,1)} %collective-permute-done.62), channel_id=1, source_target_pairs={{0,2},{1,3},{2,6},{3,7},{6,4},{7,5},{4,0},{5,1},{8,10},{9,11},{10,... | collective-permute-start | bytes 1179656 | tf_op jit(solution)/shard_map/ppermute | solution.py:48
  298.4 25.0 %collective-permute-start.57 = (bf16[4,96,2048]{2,1,0:T(8,128)(2,1)}, bf16[4,96,2048]{2,1,0:T(8,128)(2,1)}, u32[]{:S(2)}, u32[]{:S(2)}) collective-permute-start(bf16[4,96,2048]{2,1,0:T(8,128)(2,1)} %get-tuple-element.73), channel_id=1, source_target_pairs={{0,1},{1,0},{2,3},{3,2},{4,5},{5,4},{6,7},{7,6},{8,9},{9,8},{10,11... | collective-permute-start | bytes 4718600 | tf_op jit(solution)/shard_map/ppermute | solution.py:44
  298.8 15.4 %collective-permute-start.65 = (bf16[96,2048]{0,1:T(8,128)(2,1)S(1)}, bf16[96,2048]{0,1:T(8,128)(2,1)S(1)}, u32[]{:S(2)}, u32[]{:S(2)}) collective-permute-start(bf16[96,2048]{0,1:T(8,128)(2,1)S(1)} %collective-permute-done.64), channel_id=1, source_target_pairs={{0,1},{1,0},{2,3},{3,2},{4,5},{5,4},{6,7},{7,6},{8,9},{9,8},{10,11... | collective-permute-start | bytes 1179656 | tf_op jit(solution)/shard_map/ppermute | solution.py:44
  299.2 15.0 %collective-permute-start.66 = (bf16[96,2048]{0,1:T(8,128)(2,1)S(1)}, bf16[96,2048]{0,1:T(8,128)(2,1)S(1)}, u32[]{:S(2)}, u32[]{:S(2)}) collective-permute-start(bf16[96,2048]{0,1:T(8,128)(2,1)S(1)} %collective-permute-done.64), channel_id=1, source_target_pairs={{0,2},{1,3},{2,6},{3,7},{6,4},{7,5},{4,0},{5,1},{8,10},{9,11},{10,... | collective-permute-start | bytes 1179656 | tf_op jit(solution)/shard_map/ppermute | solution.py:48
  324.7 16.6 %collective-permute-start.58 = (bf16[96,2048]{1,0:T(8,128)(2,1)S(1)}, bf16[96,2048]{1,0:T(8,128)(2,1)S(1)}, u32[]{:S(2)}, u32[]{:S(2)}) collective-permute-start(bf16[96,2048]{1,0:T(8,128)(2,1)S(1)} %fusion.6), channel_id=1, source_target_pairs={{0,2},{1,3},{2,6},{3,7},{6,4},{7,5},{4,0},{5,1},{8,10},{9,11},{10,... | collective-permute-start | bytes 1179656 | tf_op jit(solution)/shard_map/ppermute | solution.py:48
  342.5 17.1 %collective-permute-start.59 = (bf16[96,2048]{1,0:T(8,128)(2,1)S(1)}, bf16[96,2048]{1,0:T(8,128)(2,1)S(1)}, u32[]{:S(2)}, u32[]{:S(2)}) collective-permute-start(bf16[96,2048]{1,0:T(8,128)(2,1)S(1)} %fusion.5), channel_id=1, source_target_pairs={{0,2},{1,3},{2,6},{3,7},{6,4},{7,5},{4,0},{5,1},{8,10},{9,11},{10,... | collective-permute-start | bytes 1179656 | tf_op jit(solution)/shard_map/ppermute | solution.py:48
  360.7 26.8 %collective-permute-start.60 = (bf16[96,2048]{1,0:T(8,128)(2,1)S(1)}, bf16[96,2048]{1,0:T(8,128)(2,1)S(1)}, u32[]{:S(2)}, u32[]{:S(2)}) collective-permute-start(bf16[96,2048]{1,0:T(8,128)(2,1)S(1)} %fusion.3), channel_id=1, source_target_pairs={{0,2},{1,3},{2,6},{3,7},{6,4},{7,5},{4,0},{5,1},{8,10},{9,11},{10,... | collective-permute-start | bytes 1179656 | tf_op jit(solution)/shard_map/ppermute | solution.py:48
  (93 other events, 1565.8 us)

commit v2 on v0

v2 whole, which is shorter than its diff:
```python
import functools

import jax
import jax.numpy as jnp
from jax import lax
from jax.experimental import pallas as pl
from jax.experimental.pallas import tpu as pltpu
from jax.sharding import PartitionSpec as P

BLOCK = 128
BF16 = jnp.bfloat16
F32 = jnp.float32
VMEM_BYTES = 60 * 1024 * 1024
NT = (((1,), (1,)), ((), ()))
NN = (((1,), (0,)), ((), ()))


def params():
    return pltpu.CompilerParams(vmem_limit_bytes=VMEM_BYTES)


def after(x, *others):
    return lax.optimization_barrier((x, *others))[0]


def step_of(hid):
    return 512 if hid % 512 == 0 else 256


def chunk_of(size, most):
    return max(c for c in (128, 256, 512, 1024) if size % c == 0 and c <= most)


def ring_of(chips):
    return [0] + list(range(1, chips, 2)) + [c for c in range(chips - 1, 0, -1) if c % 2 == 0]


class Axes:
    def __init__(self, mesh):
        self.tensor = mesh.shape["tensor"]
        self.chips = self.tensor // 2
        self.ring = ring_of(self.chips)

    def rows(self, tok):
        me = lax.axis_index("tensor")
        n = self.chips
        table = [[self.ring[(self.ring.index(c) - s) % n] for s in range(n)] for c in range(n)]
        chip = lax.dynamic_slice(jnp.array(table, jnp.int32), (me // 2, 0), (1, n))[0] * 2
        core = (me % 2).astype(jnp.int32)
        mine, other = (chip + core) * tok, (chip + 1 - core) * tok
        return jnp.concatenate([mine[:1], other[:1], mine[1:], other[1:]])

    def to_core(self, x):
        return lax.ppermute(x, "tensor", [(t, t ^ 1) for t in range(self.tensor)])

    def to_next(self, x):
        pairs = [(self.ring[i], self.ring[(i + 1) % self.chips]) for i in range(self.chips)]
        return lax.ppermute(x, "tensor", [(2 * a + k, 2 * b + k) for a, b in pairs for k in range(2)])


def partial_kernel(count, step, *refs):
    tokens = refs[:count]
    down, mask, out, rows = refs[count:]

    @pl.when(pl.program_id(0) == 0)
    def _():
        at = 0
        for ref in tokens:
            rows[at : at + ref.shape[0], :] = ref[...]
            at += ref.shape[0]

    kept = [down[i * BLOCK : (i + 1) * BLOCK, :] * mask[i].astype(BF16) for i in range(step // BLOCK)]
    acc = lax.dot_general(rows[...], jnp.concatenate(kept, axis=0), NT, preferred_element_type=F32)
    out[...] = acc.astype(BF16)


def partial_sums(tokens, down, mask, start, cols):
    width = down.shape[1]
    step = step_of(down.shape[0])
    rows = sum(t.shape[0] for t in tokens)
    first = start // step
    return pl.pallas_call(
        functools.partial(partial_kernel, len(tokens), step),
        out_shape=jax.ShapeDtypeStruct((rows, cols), BF16),
        grid=(cols // step,),
        in_specs=[pl.BlockSpec(t.shape, lambda k: (0, 0), pipeline_mode=pl.Buffered(1)) for t in tokens]
        + [
            pl.BlockSpec((step, width), lambda k: (first + k, 0)),
            pl.BlockSpec((step // BLOCK, 1, width), lambda k: (first + k, 0, 0)),
        ],
        out_specs=pl.BlockSpec((rows, step), lambda k: (0, k)),
        scratch_shapes=[pltpu.VMEM((rows, width), BF16)],
        compiler_params=params(),
        cost_estimate=pl.CostEstimate(
            flops=2 * rows * width * cols,
            bytes_accessed=2 * (rows * width + width * cols + rows * cols),
            transcendentals=0,
        ),
        name="partial_sums",
    )(*tokens, down, mask)


def grads_kernel(cfg, at_rows, *refs):
    refs = list(refs)
    take = lambda n: [refs.pop(0) for _ in range(n)]
    hidden = take(cfg["sources"])
    gate_pre, up_pre, gate_w, up_w, gate_m, up_m = take(6)
    acc_in = take(4) if cfg["acc_in"] else None
    gate_out, up_out, *acc = take(6)
    (both,) = refs
    step, tok = cfg["step"], cfg["tok"]
    k = pl.program_id(0)

    for i in range(cfg["groups"]):
        at = pl.ds(pl.multiple_of(at_rows[i], 16), tok)
        rows = slice(i * tok, (i + 1) * tok)
        lo = i * tok
        for ref in hidden:
            if lo < ref.shape[0]:
                break
            lo -= ref.shape[0]
        g = gate_pre[at, :].astype(F32)
        u = up_pre[at, :].astype(F32)
        h = ref[lo : lo + tok, :].astype(F32)
        sig = 1.0 / (1.0 + jnp.exp(-g))
        gg = (h * u * sig * (1.0 + g * (1.0 - sig))).astype(BF16)
        ug = (h * g * sig).astype(BF16)
        gate_out[rows, :] = gg
        up_out[rows, :] = ug
        both[rows, :step] = gg
        both[rows, step:] = ug

    chunk = cfg["chunk"]

    def tile(n, first):
        def masked(w, m):
            rows = []
            for i in range(chunk // BLOCK):
                at = pl.ds(pl.multiple_of(n * chunk + i * BLOCK, BLOCK), BLOCK)
                rows.append(w[at, :] * m[pl.ds(n * (chunk // BLOCK) + i, 1), :].astype(BF16))
            return jnp.concatenate(rows, axis=0)

        w = jnp.concatenate([masked(gate_w, gate_m), masked(up_w, up_m)], axis=1)
        to = pl.ds(pl.multiple_of(n * chunk, chunk), chunk)
        term = lax.dot_general(both[...], w, NT, preferred_element_type=F32)
        lo = 0
        for i, ref in enumerate(acc):
            part = term[lo : lo + ref.shape[0], :]
            lo += ref.shape[0]
            if not first:
                part += ref[:, to]
            elif acc_in is not None:
                part += acc_in[i][:, to]
            ref[:, to] = part

    tiles = cfg["width"] // chunk

    @pl.when(k == 0)
    def _():
        pl.loop(0, tiles)(lambda n: tile(n, True))

    @pl.when(k > 0)
    def _():
        pl.loop(0, tiles)(lambda n: tile(n, False))


def grads(at_rows, sources, gate_pre, up_pre, gate_w, up_w, gate_m, up_m, acc, tok, start, cols):
    tokens, hid = gate_pre.shape
    width = gate_w.shape[0]
    step = step_of(hid)
    first = start // step
    specs = [
        pl.BlockSpec((a.shape[0], step), lambda k, _, off=off // step: (0, off + k)) for a, off in sources
    ]
    col = lambda k, _: (0, first + k)
    one = lambda k, _: (0, 0)
    specs += [pl.BlockSpec((tokens, step), col)] * 2
    specs += [pl.BlockSpec((width, step), col)] * 2
    specs += [pl.BlockSpec((gate_m.shape[0], step), col)] * 2
    arrays = [a for a, _ in sources] + [gate_pre, up_pre, gate_w, up_w, gate_m, up_m]
    parts = [tok, tok, tokens // 2 - tok, tokens // 2 - tok]
    if acc is not None:
        specs += [pl.BlockSpec((n, width), one, pipeline_mode=pl.Buffered(1)) for n in parts]
        arrays += list(acc)
    cfg = dict(
        sources=len(sources), groups=tokens // tok, tok=tok, step=step, width=width, chunk=chunk_of(width, 1024),
        acc_in=acc is not None,
    )
    out = pl.pallas_call(
        functools.partial(grads_kernel, cfg),
        out_shape=[jax.ShapeDtypeStruct((tokens, cols), BF16)] * 2
        + [jax.ShapeDtypeStruct((n, width), F32) for n in parts],
        grid_spec=pltpu.PrefetchScalarGridSpec(
            num_scalar_prefetch=1,
            grid=(cols // step,),
            in_specs=specs,
            out_specs=[pl.BlockSpec((tokens, step), lambda k, _: (0, k))] * 2
            + [pl.BlockSpec((n, width), one) for n in parts],
            scratch_shapes=[pltpu.VMEM((tokens, 2 * step), BF16)],
        ),
        compiler_params=params(),
        cost_estimate=pl.CostEstimate(
            flops=4 * tokens * width * cols,
            bytes_accessed=4 * width * cols + 10 * tokens * cols + 8 * tokens * width,
            transcendentals=tokens * cols,
        ),
        name="hidden_grads",
    )(at_rows, *arrays)
    return out[0], out[1], out[2:]


def weights_kernel(cfg, x, gate, up, gate_m, up_m, *refs):
    outs = refs[-2:]
    chunk = cfg["chunk"]
    for g, m, out in ((gate, gate_m, outs[0]), (up, up_m, outs[1])):

        def tile(n, g=g, m=m, out=out):
            at = pl.ds(pl.multiple_of(n * chunk, chunk), chunk)
            term = lax.dot_general(x[at, :], g[...], NN, preferred_element_type=F32)
            for i in range(chunk // BLOCK):
                to = pl.ds(pl.multiple_of(n * chunk + i * BLOCK, BLOCK), BLOCK)
                row = m[pl.ds(n * (chunk // BLOCK) + i, 1), :]
                out[to, :] = (term[i * BLOCK : (i + 1) * BLOCK, :] * row).astype(BF16)

        pl.loop(0, cfg["width"] // chunk)(tile)


def weight_grads(x_t, gate, up, gate_m, up_m, before, shape, start):
    width, tokens = x_t.shape
    step = step_of(shape[1])
    steps = gate.shape[1] // step
    first = start // step
    col = lambda k: (0, first + k)
    specs = [
        pl.BlockSpec((width, tokens), lambda k: (0, 0), pipeline_mode=pl.Buffered(1)),
        pl.BlockSpec((tokens, step), lambda k: (0, k)),
        pl.BlockSpec((tokens, step), lambda k: (0, k)),
        pl.BlockSpec((gate_m.shape[0], step), col),
        pl.BlockSpec((gate_m.shape[0], step), col),
    ]
    arrays = [x_t, gate, up, gate_m, up_m]
    alias = {}
    if before is not None:
        specs += [pl.BlockSpec(memory_space=pl.ANY)] * 2
        arrays += list(before)
        alias = {5: 0, 6: 1}
    return pl.pallas_call(
        functools.partial(weights_kernel, dict(width=width, chunk=chunk_of(width, 1024))),
        out_shape=[jax.ShapeDtypeStruct(shape, BF16)] * 2,
        grid=(steps,),
        in_specs=specs,
        out_specs=[pl.BlockSpec((width, step), col)] * 2,
        input_output_aliases=alias,
        compiler_params=params(),
        cost_estimate=pl.CostEstimate(
            flops=4 * tokens * width * steps * step,
            bytes_accessed=4 * (width + tokens) * steps * step + 2 * tokens * width,
            transcendentals=0,
        ),
        name="weight_grads",
    )(*arrays)


def down_kernel(cfg, at_rows, *refs):
    tokens = refs[:4]
    gate_pre, up_pre, mask, out, rows, hidden = refs[4:]
    tok = cfg["tok"]

    @pl.when(pl.program_id(0) == 0)
    def _():
        at = 0
        for ref in tokens:
            rows[at : at + ref.shape[0], :] = ref[...]
            at += ref.shape[0]

    for i in range(cfg["groups"]):
        at = pl.ds(pl.multiple_of(at_rows[i], 16), tok)
        g = gate_pre[at, :].astype(F32)
        u = up_pre[at, :].astype(F32)
        hidden[i * tok : (i + 1) * tok, :] = (g * (1.0 / (1.0 + jnp.exp(-g))) * u).astype(BF16)
    across = hidden[...].T
    chunk = cfg["chunk"]

    def tile(n):
        at = pl.ds(pl.multiple_of(n * chunk, chunk), chunk)
        term = lax.dot_general(across, rows[:, at], NN, preferred_element_type=F32)
        for i in range(cfg["step"] // BLOCK):
            part = slice(i * BLOCK, (i + 1) * BLOCK)
            out[part, at] = (term[part, :] * mask[i, :, at]).astype(BF16)

    pl.loop(0, cfg["width"] // chunk)(tile)


def down_grad(at_rows, out_grad, gate_pre, up_pre, mask, tok):
    tokens, hid = gate_pre.shape
    width = out_grad[0].shape[1]
    step = step_of(hid)
    cfg = dict(groups=tokens // tok, tok=tok, width=width, step=step, chunk=chunk_of(width, 1024))
    return pl.pallas_call(
        functools.partial(down_kernel, cfg),
        out_shape=jax.ShapeDtypeStruct((hid, width), BF16),
        grid_spec=pltpu.PrefetchScalarGridSpec(
            num_scalar_prefetch=1,
            grid=(hid // step,),
            in_specs=[pl.BlockSpec(t.shape, lambda k, _: (0, 0), pipeline_mode=pl.Buffered(1)) for t in out_grad]
            + [pl.BlockSpec((tokens, step), lambda k, _: (0, k))] * 2
            + [pl.BlockSpec((step // BLOCK, 1, width), lambda k, _: (k, 0, 0))],
            out_specs=pl.BlockSpec((step, width), lambda k, _: (k, 0)),
            scratch_shapes=[pltpu.VMEM((tokens, width), BF16), pltpu.VMEM((tokens, step), BF16)],
        ),
        compiler_params=params(),
        cost_estimate=pl.CostEstimate(
            flops=2 * tokens * width * hid,
            bytes_accessed=2 * (tokens * width + 2 * tokens * hid + width * hid),
            transcendentals=tokens * hid,
        ),
        name="down_grad",
    )(at_rows, *out_grad, gate_pre, up_pre, mask)


def round_ring(axes, x):
    got = [x]
    for _ in range(axes.chips - 1):
        got.append(axes.to_next(got[-1]))
    return jnp.concatenate(got[1:], axis=0)


def shards(axes, layer_input, out_grad, gate_pre, up_pre, gate_weight, up_weight, down_weight, gate_mask, up_mask, down_mask):
    tokens, hid = gate_pre.shape
    tok = out_grad.shape[0]
    step = step_of(hid)
    at_rows = axes.rows(tok)
    gate_m = jnp.repeat(gate_mask, BLOCK, axis=1).astype(F32)
    up_m = jnp.repeat(up_mask, BLOCK, axis=1).astype(F32)
    down_m = jnp.repeat(down_mask, BLOCK, axis=1).astype(F32)[:, None, :]

    near = [out_grad, axes.to_core(out_grad)]
    early = lax.psum(partial_sums(near, down_weight, down_m, 0, hid), "pipe")
    far = round_ring(axes, out_grad)
    far = [far, axes.to_core(far)]
    x_far = round_ring(axes, after(layer_input, far[0]))
    x_other = axes.to_core(jnp.concatenate([layer_input, x_far], axis=0))

    pieces, at = [], 0
    while at < hid:
        pieces.append((at, min(2 * step, hid - at)))
        at += pieces[-1][1]
    parts = [partial_sums(far, down_weight, down_m, start, cols) for start, cols in pieces]
    late, last = [], early
    for p in parts:
        last = lax.psum(after(p, last), "pipe")
        late.append(last)
    grad_down = down_grad(after(at_rows, *parts), near + far, gate_pre, up_pre, down_m, tok)
    x_t = jnp.concatenate([layer_input, x_other[:tok], x_far, x_other[tok:]], axis=0).T

    acc, weights = None, None
    at_rows = after(at_rows, grad_down, x_t)
    for i, ((start, cols), hidden) in enumerate(zip(pieces, late)):
        if i >= 1 and i < len(pieces) - 1:
            at_rows, *weights = lax.optimization_barrier((at_rows, *weights))
        gate, up, acc = grads(
            at_rows, [(early, start), (hidden, 0)], gate_pre, up_pre, gate_weight, up_weight, gate_m, up_m, acc, tok,
            start, cols,
        )
        weights = weight_grads(x_t, gate, up, gate_m, up_m, weights, gate_weight.shape, start)
    mine, other, mine_far, other_far = acc
    far = mine_far + axes.to_core(other_far)
    near = mine + axes.to_core(other)
    run = far[:tok]
    for s in range(1, axes.chips):
        term = far[s * tok : (s + 1) * tok] if s < axes.chips - 1 else near
        run = axes.to_next(run.astype(BF16)).astype(F32) + term
    return (run.astype(BF16), weights[0], weights[1], grad_down)


def solution(mesh):
    in_specs = (
        P("tensor", "pipe"),
        P("tensor", "pipe"),
        P(None, "tensor"),
        P(None, "tensor"),
        P("pipe", "tensor"),
        P("pipe", "tensor"),
        P("tensor", "pipe"),
        P("pipe", "tensor"),
        P("pipe", "tensor"),
        P("tensor", "pipe"),
    )
    out_specs = (P("tensor", "pipe"), P("pipe", "tensor"), P("pipe", "tensor"), P("tensor", "pipe"))
    return jax.shard_map(
        functools.partial(shards, Axes(mesh)), mesh=mesh, in_specs=in_specs, out_specs=out_specs, check_vma=False
    )
```

time: 483 us -> 410 us (0.85); the launches traced: 475 us -> 409 us
  Pallas kernels: 0 us -> 171 us
  matrix products: 129 us -> 0 us
  local copies, waits for them, and re-layouts: 121 us -> 15.7 us
  other arithmetic: 33.1 us -> 7.7 us
  waiting for transfers between devices: 177 us -> 190 us
  starting transfers between devices: 0.33 us -> 10.7 us
    pallas_call x0 -> x14, Pallas kernels: none -> 171 us  [the longest x4 67.2 us: grads(): pl.pallas_call(functools.partial(grads_kernel, cfg), out_shape=[jax.Shape...]
    dot_general x6 -> x0, matrix products: 129 us -> none  [the longest x1 30.9 us: shards(): lax.dot_general(hidden, piece, (((0,), (0,)), ((), ())), preferred_elemen...]
    unnamed x34 -> x21, local copies, waits for them, and re-layouts: 99.9 us -> 3.56 us
    ppermute x0 -> x14, waiting for transfers between devices: none -> 69.7 us  [the longest x9 64.9 us: to_next(): lax.ppermute(x, 'tensor', [(2 * a + k, 2 * b + k) for a, b in pairs for k...]
    all_gather x2 -> x0, waiting for transfers between devices: 41.8 us -> none  [the longest x1 41.8 us: shards(): piece = lax.all_gather(out_grad, 'tensor', axis=0, tiled=True)]
    broadcast_in_dim x4 -> x3, local copies, waits for them, and re-layouts: 20.3 us -> 1.06 us  [the longest x1 0.81 us: shards(): down_m = jnp.repeat(down_mask, BLOCK, axis=1).astype(F32)[:, None, :]]
    mul x2 -> x1, other arithmetic: 19.8 us -> 0.69 us  [rows(): mine, other = ((chip + core) * tok, (chip + 1 - core) * tok)]
    psum x1 -> x5, waiting for transfers between devices: 133 us -> 121 us  [the longest x4 105 us: shards(): last = lax.psum(after(p, last), 'pipe')]
  transfers between devices with their start and end apart: 4 -> 19, of which waited for: 2 -> 13; matrix products, arithmetic and copies ran while one was open for 51% -> 4% of each run, Pallas kernels for 0% -> 39%
where the time goes in v2:
time: 410 us; the launch traced here: 409 us
  waiting for transfers between devices  190 us (46%)
  Pallas kernels  171 us (42%)
  local copies, waits for them, and re-layouts  15.7 us (4%)
  between operations  14.1 us (3%)
  starting transfers between devices  10.7 us (3%)
  other arithmetic  7.7 us (2%)
    psum x4, waiting for transfers between devices, shards(): last = lax.psum(after(p, last), 'pipe')  105 us
    pallas_call x4, Pallas kernels, grads(): pl.pallas_call(functools.partial(grads_kernel, cfg), out_shape=[jax.Shape...  67.2 us
    ppermute x9, waiting for transfers between devices, to_next(): lax.ppermute(x, 'tensor', [(2 * a + k, 2 * b + k) for a, b in pairs for k...  64.9 us
    pallas_call x4, Pallas kernels, weight_grads(): pl.pallas_call(functools.partial(weights_kernel, dict(width=width, chunk=...  46.1 us
    pallas_call x5, Pallas kernels, partial_sums(): pl.pallas_call(functools.partial(partial_kernel, len(tokens), step), out_...  34.3 us
    pallas_call x1, Pallas kernels, down_grad(): pl.pallas_call(functools.partial(down_kernel, cfg), out_shape=jax.ShapeDt...  23 us
    psum x1, waiting for transfers between devices, shards(): early = lax.psum(partial_sums(near, down_weight, down_m, 0, hid), 'pipe')  15.5 us
    ppermute x9, starting transfers between devices, to_next(): lax.ppermute(x, 'tensor', [(2 * a + k, 2 * b + k) for a, b in pairs for k...  10.2 us
  transfers between devices with their start and end apart: 19, of which 13 were waited for; matrix products, arithmetic and copies ran while one was open for 4% of the time, Pallas kernels for 39%

profile of v2, /device:TPU:0, one launch (start us, length us, event | category | flops | bytes accessed | tf_op | source)
XLA Modules:
  0.0 409.1 jit_solution(11688469352550087119)
XLA Ops:
  7.2 3.1 collective-permute-start
  10.3 10.3 %collective-permute-done = bf16[96,2048]{1,0:T(8,128)(2,1)S(1)} collective-permute-done((bf16[96,2048]{1,0:T(8,128)(2,1)}, bf16[96,2048]{1,0:T(8,128)(2,1)S(1)}, u32[]{:S(2)}, u32[]{:S(2)}) %collective-permute-start) | collective-permute-done | bytes 393248 | tf_op jit(solution)/shard_map/ppermute | solution.py:58
  21.6 10.3 %collective-permute-done.1 = bf16[96,2048]{1,0:T(8,128)(2,1)S(1)} collective-permute-done((bf16[96,2048]{1,0:T(8,128)(2,1)S(1)}, bf16[96,2048]{1,0:T(8,128)(2,1)S(1)}, u32[]{:S(2)}, u32[]{:S(2)}) %collective-permute-start.1) | collective-permute-done | bytes 393248 | tf_op jit(solution)/shard_map/ppermute | solution.py:58
  32.4 9.7 %collective-permute-done.2 = bf16[96,2048]{1,0:T(8,128)(2,1)S(1)} collective-permute-done((bf16[96,2048]{1,0:T(8,128)(2,1)S(1)}, bf16[96,2048]{1,0:T(8,128)(2,1)S(1)}, u32[]{:S(2)}, u32[]{:S(2)}) %collective-permute-start.2) | collective-permute-done | bytes 393248 | tf_op jit(solution)/shard_map/ppermute | solution.py:58
  44.4 11.1 %partial_sums.9 = bf16[192,3584]{1,0:T(8,128)(2,1)} custom-call(bf16[96,2048]{1,0:T(8,128)(2,1)} %refs_0_.3, bf16[96,2048]{1,0:T(8,128)(2,1)} %collective-permute-done.4.refs_1_, bf16[3584,2048]{1,0:T(8,128)(2,1)} %refs_2_.13, f32[28,1,2048]{2,1,0:T(1,128)} %bitcast.20), custom_call_target="tpu_custom_call" | custom-call | flops 2818572288 | bytes 16842752 | tf_op jit(solution)/shard_map/partial_sums/pallas_call | solution.py:82
  56.9 1.9 collective-permute-done.5
  61.8 11.6 %collective-permute-done.6 = bf16[96,2048]{0,1:T(8,128)(2,1)} collective-permute-done((bf16[96,2048]{0,1:T(8,128)(2,1)S(1)}, bf16[96,2048]{0,1:T(8,128)(2,1)}, u32[]{:S(2)}, u32[]{:S(2)}) %collective-permute-start.6) | collective-permute-done | bytes 393248 | tf_op jit(solution)/shard_map/ppermute | solution.py:58
  75.6 6.2 %partial_sums.7 = bf16[576,1024]{1,0:T(8,128)(2,1)} custom-call(bf16[288,2048]{1,0:T(8,128)(2,1)} %copy-done, bf16[288,2048]{1,0:T(8,128)(2,1)} %copy-done.1, bf16[3584,2048]{1,0:T(8,128)(2,1)} %refs_2_.13, f32[28,1,2048]{2,1,0:T(1,128)} %bitcast.21), custom_call_target="tpu_custom_call" | custom-call | flops 2415919104 | bytes 7733248 | tf_op jit(solution)/shard_map/partial_sums/pallas_call | solution.py:82
  81.8 6.2 %partial_sums.6 = bf16[576,1024]{1,0:T(8,128)(2,1)} custom-call(bf16[288,2048]{1,0:T(8,128)(2,1)} %copy-done, bf16[288,2048]{1,0:T(8,128)(2,1)} %copy-done.1, bf16[3584,2048]{1,0:T(8,128)(2,1)} %refs_2_.13, f32[28,1,2048]{2,1,0:T(1,128)} %bitcast.22), custom_call_target="tpu_custom_call" | custom-call | flops 2415919104 | bytes 7733248 | tf_op jit(solution)/shard_map/partial_sums/pallas_call | solution.py:82
  88.0 4.6 %partial_sums.8 = bf16[576,512]{1,0:T(8,128)(2,1)} custom-call(bf16[288,2048]{1,0:T(8,128)(2,1)} %copy-done, bf16[288,2048]{1,0:T(8,128)(2,1)} %copy-done.1, bf16[3584,2048]{1,0:T(8,128)(2,1)} %refs_2_.13, f32[28,1,2048]{2,1,0:T(1,128)} %bitcast.23), custom_call_target="tpu_custom_call" | custom-call | flops 1207959552 | bytes 5046272 | tf_op jit(solution)/shard_map/partial_sums/pallas_call | solution.py:82
  92.6 6.2 %partial_sums.5 = bf16[576,1024]{1,0:T(8,128)(2,1)} custom-call(bf16[288,2048]{1,0:T(8,128)(2,1)} %copy-done, bf16[288,2048]{1,0:T(8,128)(2,1)} %copy-done.1, bf16[3584,2048]{1,0:T(8,128)(2,1)} %refs_2_.13, f32[28,1,2048]{2,1,0:T(1,128)} %bitcast.24), custom_call_target="tpu_custom_call" | custom-call | flops 2415919104 | bytes 7733248 | tf_op jit(solution)/shard_map/partial_sums/pallas_call | solution.py:82
  98.8 15.5 %all-reduce.6.cloned.1.call-done.refs_0_ = bf16[192,3584]{1,0:T(8,128)(2,1)} async-done(((bf16[192,3584]{1,0:T(8,128)(2,1)}), bf16[192,3584]{1,0:T(8,128)(2,1)}) %all-reduce.6.cloned.1.call-update) | async-done | bytes 1376272 | tf_op jit(solution)/shard_map/psum | solution.py:338
  114.3 3.3 pad_maximum_fusion
  119.0 23.0 %down_grad.1 = bf16[3584,2048]{1,0:T(8,128)(2,1)} custom-call(s32[8]{0:T(128)} %pad_add_fusion.at_rows, bf16[96,2048]{1,0:T(8,128)(2,1)} %refs_0_.3, bf16[96,2048]{1,0:T(8,128)(2,1)} %collective-permute-done.4.refs_1_, bf16[288,2048]{1,0:T(8,128)(2,1)} %copy-done, bf16[288,2048]{1,0:T(8,128)(2,1)} %copy-done.1, bf16[768,3584]{1,0:T(8,128)(2,1)} %refs_2_.17, ...), custom_call_target="tpu_custom_call" | custom-call | flops 11274289152 | bytes 28835840 | tf_op jit(solution)/shard_map/down_grad/pallas_call | solution.py:299
  142.1 30.3 %all-reduce.8.cloned.1.call-done.refs_1_ = bf16[576,1024]{1,0:T(8,128)(2,1)} async-done(((bf16[576,1024]{1,0:T(8,128)(2,1)}), bf16[576,1024]{1,0:T(8,128)(2,1)}) %all-reduce.8.cloned.1.call-update) | async-done | bytes 1179664 | tf_op jit(solution)/shard_map/psum | solution.py:351
  173.8 2.3 slice.54
  176.1 6.5 %concatenate.18 = bf16[768,2048]{0,1:T(8,128)(2,1)} concatenate(bf16[96,2048]{0,1:T(8,128)(2,1)S(1)} %copy.28, bf16[96,2048]{0,1:T(8,128)(2,1)S(1)} %slice-done, bf16[96,2048]{0,1:T(8,128)(2,1)S(1)} %collective-permute-done.5, bf16[96,2048]{0,1:T(8,128)(2,1)} %collective-permute-done.6, bf16[96,2048]{0,1:T(8,128)(2,1)} %collective-permute-done.7, bf16[288,2048]{0,1:T(8,128)(2,1)S(1)} %slice.54), dimensions={0} | concatenate | bytes 6291456 | tf_op jit(solution)/shard_map/concatenate | solution.py:354
  182.5 16.1 %hidden_grads.4 = (bf16[768,1024]{1,0:T(8,128)(2,1)}, bf16[768,1024]{1,0:T(8,128)(2,1)}, f32[96,2048]{1,0:T(8,128)}, f32[96,2048]{1,0:T(8,128)}, f32[288,2048]{1,0:T(8,128)}, /*index=5*/f32[288,2048]{1,0:T(8,128)}) custom-call(s32[8]{0:T(128)} %pad_add_fusion.at_rows, bf16[192,3584]{1,0:T(8,128)(2,1)} %all-reduce.6.cloned.1.call-done.refs_0_, ...), custom_call_target="tpu_custom_call" | custom-call | flops 6442450944 | bytes 28835840 | tf_op jit(solution)/shard_map/hidden_grads/pallas_call | solution.py:189
  198.7 12.8 %weight_grads.4 = (bf16[2048,3584]{1,0:T(8,128)(2,1)}, bf16[2048,3584]{1,0:T(8,128)(2,1)}) custom-call(bf16[2048,768]{1,0:T(8,128)(2,1)} %bitcast.16, bf16[768,1024]{1,0:T(8,128)(2,1)} %get-tuple-element.53.gate, bf16[768,1024]{1,0:T(8,128)(2,1)} %get-tuple-element.54.up, f32[16,3584]{1,0:T(8,128)} %get-tuple-element.99.refs_6_.gate_m, ...), custom_call_target="tpu_custom_call" | custom-call | flops 6442450944 | bytes 14680064 | tf_op jit(solution)/shard_map/weight_grads/pallas_call | solution.py:247
  211.5 18.8 %all-reduce.10.cloned.1.call-done.refs_1_ = bf16[576,1024]{1,0:T(8,128)(2,1)} async-done(((bf16[576,1024]{1,0:T(8,128)(2,1)}), bf16[576,1024]{1,0:T(8,128)(2,1)}) %all-reduce.10.cloned.1.call-update) | async-done | bytes 1179664 | tf_op jit(solution)/shard_map/psum | solution.py:351
  230.4 19.1 %hidden_grads.5 = (bf16[768,1024]{1,0:T(8,128)(2,1)}, bf16[768,1024]{1,0:T(8,128)(2,1)}, f32[96,2048]{1,0:T(8,128)}, f32[96,2048]{1,0:T(8,128)}, f32[288,2048]{1,0:T(8,128)}, /*index=5*/f32[288,2048]{1,0:T(8,128)}) custom-call(s32[8]{0:T(128)} %pad_add_fusion.at_rows, bf16[192,3584]{1,0:T(8,128)(2,1)} %all-reduce.6.cloned.1.call-done.refs_0_, ...), custom_call_target="tpu_custom_call" | custom-call | flops 6442450944 | bytes 28835840 | tf_op jit(solution)/shard_map/hidden_grads/pallas_call | solution.py:189
  249.5 12.6 %weight_grads.5 = (bf16[2048,3584]{1,0:T(8,128)(2,1)}, bf16[2048,3584]{1,0:T(8,128)(2,1)}) custom-call(bf16[2048,768]{1,0:T(8,128)(2,1)} %bitcast.17, bf16[768,1024]{1,0:T(8,128)(2,1)} %get-tuple-element.63.gate, bf16[768,1024]{1,0:T(8,128)(2,1)} %get-tuple-element.64.up, ...), custom_call_target="tpu_custom_call", output_to_operand_aliasing={{0}: (5, {}), {1}: (6, {})} | custom-call | flops 6442450944 | bytes 14680064 | tf_op jit(solution)/shard_map/weight_grads/pallas_call | solution.py:247
  262.0 25.8 %all-reduce.12.cloned.1.call-done.refs_1_ = bf16[576,1024]{1,0:T(8,128)(2,1)} async-done(((bf16[576,1024]{1,0:T(8,128)(2,1)}), bf16[576,1024]{1,0:T(8,128)(2,1)}) %all-reduce.12.cloned.1.call-update) | async-done | bytes 1179664 | tf_op jit(solution)/shard_map/psum | solution.py:351
  287.8 18.9 %hidden_grads.6 = (bf16[768,1024]{1,0:T(8,128)(2,1)}, bf16[768,1024]{1,0:T(8,128)(2,1)}, f32[96,2048]{1,0:T(8,128)}, f32[96,2048]{1,0:T(8,128)}, f32[288,2048]{1,0:T(8,128)}, /*index=5*/f32[288,2048]{1,0:T(8,128)}) custom-call(s32[8]{0:T(128)} %pad_add_fusion.at_rows, bf16[192,3584]{1,0:T(8,128)(2,1)} %all-reduce.6.cloned.1.call-done.refs_0_, ...), custom_call_target="tpu_custom_call" | custom-call | flops 6442450944 | bytes 28835840 | tf_op jit(solution)/shard_map/hidden_grads/pallas_call | solution.py:189
  306.8 30.3 %all-reduce.14.cloned.1.call-done.refs_1_ = bf16[576,512]{1,0:T(8,128)(2,1)} async-done(((bf16[576,512]{1,0:T(8,128)(2,1)}), bf16[576,512]{1,0:T(8,128)(2,1)}) %all-reduce.14.cloned.1.call-update) | async-done | bytes 589840 | tf_op jit(solution)/shard_map/psum | solution.py:351
  337.0 13.1 %hidden_grads.7 = (bf16[768,512]{1,0:T(8,128)(2,1)}, bf16[768,512]{1,0:T(8,128)(2,1)}, f32[96,2048]{1,0:T(8,128)}, f32[96,2048]{1,0:T(8,128)}, f32[288,2048]{1,0:T(8,128)}, /*index=5*/f32[288,2048]{1,0:T(8,128)}) custom-call(s32[8]{0:T(128)} %pad_add_fusion.at_rows, bf16[192,3584]{1,0:T(8,128)(2,1)} %all-reduce.6.cloned.1.call-done.refs_0_, ...), custom_call_target="tpu_custom_call" | custom-call | flops 3221225472 | bytes 20709376 | tf_op jit(solution)/shard_map/hidden_grads/pallas_call | solution.py:189
  350.1 4.7 %collective-permute-done.9 = f32[288,2048]{1,0:T(8,128)S(1)} collective-permute-done((f32[288,2048]{1,0:T(8,128)}, f32[288,2048]{1,0:T(8,128)S(1)}, u32[]{:S(2)}, u32[]{:S(2)}) %collective-permute-start.9) | collective-permute-done | bytes 2359328 | tf_op jit(solution)/shard_map/ppermute | solution.py:54
  354.8 2.0 add.49
  358.4 10.6 %collective-permute-done.10 = bf16[96,2048]{1,0:T(8,128)(2,1)S(1)} collective-permute-done((bf16[96,2048]{1,0:T(8,128)(2,1)S(1)}, bf16[96,2048]{1,0:T(8,128)(2,1)S(1)}, u32[]{:S(2)}, u32[]{:S(2)}) %collective-permute-start.10) | collective-permute-done | bytes 393248 | tf_op jit(solution)/shard_map/ppermute | solution.py:58
  369.7 10.6 %collective-permute-done.11 = bf16[96,2048]{1,0:T(8,128)(2,1)S(1)} collective-permute-done((bf16[96,2048]{1,0:T(8,128)(2,1)S(1)}, bf16[96,2048]{1,0:T(8,128)(2,1)S(1)}, u32[]{:S(2)}, u32[]{:S(2)}) %collective-permute-start.11) | collective-permute-done | bytes 393248 | tf_op jit(solution)/shard_map/ppermute | solution.py:58
  381.0 12.5 %weight_grads.6 = (bf16[2048,3584]{1,0:T(8,128)(2,1)}, bf16[2048,3584]{1,0:T(8,128)(2,1)}) custom-call(bf16[2048,768]{1,0:T(8,128)(2,1)} %bitcast.18, bf16[768,1024]{1,0:T(8,128)(2,1)} %get-tuple-element.86.gate, bf16[768,1024]{1,0:T(8,128)(2,1)} %get-tuple-element.87.up, ...), custom_call_target="tpu_custom_call", output_to_operand_aliasing={{0}: (5, {}), {1}: (6, {})} | custom-call | flops 6442450944 | bytes 14680064 | tf_op jit(solution)/shard_map/weight_grads/pallas_call | solution.py:247
  393.6 8.2 %weight_grads.7 = (bf16[2048,3584]{1,0:T(8,128)(2,1)}, bf16[2048,3584]{1,0:T(8,128)(2,1)}) custom-call(bf16[2048,768]{1,0:T(8,128)(2,1)} %bitcast.19, bf16[768,512]{1,0:T(8,128)(2,1)} %get-tuple-element.84.gate, bf16[768,512]{1,0:T(8,128)(2,1)} %get-tuple-element.85.up, ...), custom_call_target="tpu_custom_call", output_to_operand_aliasing={{0}: (5, {}), {1}: (6, {})} | custom-call | flops 3221225472 | bytes 8912896 | tf_op jit(solution)/shard_map/weight_grads/pallas_call | solution.py:247
  (69 shorter events, 17.0 us)
Async XLA Ops:
  7.2 35.1 %copy-start.5 = (s32[28,16]{0,1:T(8,128)S(1)}, s32[28,16]{0,1:T(8,128)}, u32[]{:S(2)}) copy-start(s32[28,16]{0,1:T(8,128)} %param.20) | copy-start | bytes 5380
  7.2 35.2 %copy-start.3 = (bf16[96,2048]{1,0:T(8,128)(2,1)S(1)}, bf16[96,2048]{1,0:T(8,128)(2,1)}, u32[]{:S(2)}) copy-start(bf16[96,2048]{1,0:T(8,128)(2,1)} %param.11) | copy-start | bytes 1179652
  7.2 107.1 %all-reduce.6.cloned.1.call-start = ((), (), s32[]{:S(2)}) async-start(), calls=%async_computation | async-start | bytes 2752512 | tf_op jit(solution)/shard_map/psum | solution.py:338
  7.2 13.4 %collective-permute-start = (bf16[96,2048]{1,0:T(8,128)(2,1)}, bf16[96,2048]{1,0:T(8,128)(2,1)S(1)}, u32[]{:S(2)}, u32[]{:S(2)}) collective-permute-start(bf16[96,2048]{1,0:T(8,128)(2,1)} %refs_0_.3), channel_id=1, source_target_pairs={{0,2},{1,3},{2,6},{3,7},{6,4},{7,5},{4,0},{5,1},{8,10},{9,11},{10,... | collective-permute-start | bytes 1179656 | tf_op jit(solution)/shard_map/ppermute | solution.py:58
  20.6 11.2 %collective-permute-start.1 = (bf16[96,2048]{1,0:T(8,128)(2,1)S(1)}, bf16[96,2048]{1,0:T(8,128)(2,1)S(1)}, u32[]{:S(2)}, u32[]{:S(2)}) collective-permute-start(bf16[96,2048]{1,0:T(8,128)(2,1)S(1)} %collective-permute-done), channel_id=1, source_target_pairs={{0,2},{1,3},{2,6},{3,7},{6,4},{7,5},{4,0},{5,1},{8,10},{9,11},{10,... | collective-permute-start | bytes 1179656 | tf_op jit(solution)/shard_map/ppermute | solution.py:58
  21.6 22.0 %collective-permute-start.4 = (bf16[96,2048]{1,0:T(8,128)(2,1)}, bf16[96,2048]{1,0:T(8,128)(2,1)}, u32[]{:S(2)}, u32[]{:S(2)}) collective-permute-start(bf16[96,2048]{1,0:T(8,128)(2,1)} %refs_0_.3), channel_id=1, source_target_pairs={{0,1},{1,0},{2,3},{3,2},{4,5},{5,4},{6,7},{7,6},{8,9},{9,8},{10,11... | collective-permute-start | bytes 1179656 | tf_op jit(solution)/shard_map/ppermute | solution.py:54
  31.8 10.3 %collective-permute-start.2 = (bf16[96,2048]{1,0:T(8,128)(2,1)S(1)}, bf16[96,2048]{1,0:T(8,128)(2,1)S(1)}, u32[]{:S(2)}, u32[]{:S(2)}) collective-permute-start(bf16[96,2048]{1,0:T(8,128)(2,1)S(1)} %collective-permute-done.1), channel_id=1, source_target_pairs={{0,2},{1,3},{2,6},{3,7},{6,4},{7,5},{4,0},{5,1},{8,10},{9,11},{10,... | collective-permute-start | bytes 1179656 | tf_op jit(solution)/shard_map/ppermute | solution.py:58
  42.2 13.3 %copy-start = (bf16[288,2048]{1,0:T(8,128)(2,1)}, bf16[288,2048]{1,0:T(8,128)(2,1)S(1)}, u32[]{:S(2)}) copy-start(bf16[288,2048]{1,0:T(8,128)(2,1)S(1)} %constant_dynamic-update-slice_fusion.refs_0_.refs_2_) | copy-start | bytes 3538948
  42.2 32.3 %collective-permute-start.3 = (bf16[288,2048]{1,0:T(8,128)(2,1)S(1)}, bf16[288,2048]{1,0:T(8,128)(2,1)S(1)}, u32[]{:S(2)}, u32[]{:S(2)}) collective-permute-start(bf16[288,2048]{1,0:T(8,128)(2,1)S(1)} %constant_dynamic-update-slice_fusion.refs_0_.refs_2_), channel_id=1, source_target_pairs={{0,1},{1,0},{2,3},{3,2},{4,5},{5,4},{6,7},{7,6},{8,9},{9,8},{10,11... | collective-permute-start | bytes 3538952 | tf_op jit(solution)/shard_map/ppermute | solution.py:54
  43.4 15.4 %collective-permute-start.5 = (bf16[96,2048]{0,1:T(8,128)(2,1)}, bf16[96,2048]{0,1:T(8,128)(2,1)S(1)}, u32[]{:S(2)}, u32[]{:S(2)}) collective-permute-start(bf16[96,2048]{0,1:T(8,128)(2,1)} %copy.26), channel_id=1, source_target_pairs={{0,2},{1,3},{2,6},{3,7},{6,4},{7,5},{4,0},{5,1},{8,10},{9,11},{10,... | collective-permute-start | bytes 1179656 | tf_op jit(solution)/shard_map/ppermute | solution.py:58
  44.4 12.5 %copy-start.6 = (s32[16,28]{1,0:T(8,128)S(1)}, s32[16,28]{1,0:T(8,128)}, u32[]{:S(2)}) copy-start(s32[16,28]{1,0:T(8,128)} %param.18) | copy-start | bytes 5380
  55.5 1.4 copy-start.7
  55.5 116.9 %all-reduce.8.cloned.1.call-start = ((), (), s32[]{:S(2)}) async-start(), calls=%async_computation.1 | async-start | bytes 2359296 | tf_op jit(solution)/shard_map/psum | solution.py:351
  58.8 14.5 %collective-permute-start.6 = (bf16[96,2048]{0,1:T(8,128)(2,1)S(1)}, bf16[96,2048]{0,1:T(8,128)(2,1)}, u32[]{:S(2)}, u32[]{:S(2)}) collective-permute-start(bf16[96,2048]{0,1:T(8,128)(2,1)S(1)} %collective-permute-done.5), channel_id=1, source_target_pairs={{0,2},{1,3},{2,6},{3,7},{6,4},{7,5},{4,0},{5,1},{8,10},{9,11},{10,... | collective-permute-start | bytes 1179656 | tf_op jit(solution)/shard_map/ppermute | solution.py:58
  73.3 41.0 %collective-permute-start.7 = (bf16[96,2048]{0,1:T(8,128)(2,1)}, bf16[96,2048]{0,1:T(8,128)(2,1)}, u32[]{:S(2)}, u32[]{:S(2)}) collective-permute-start(bf16[96,2048]{0,1:T(8,128)(2,1)} %collective-permute-done.6), channel_id=1, source_target_pairs={{0,2},{1,3},{2,6},{3,7},{6,4},{7,5},{4,0},{5,1},{8,10},{9,11},{10,... | collective-permute-start | bytes 1179656 | tf_op jit(solution)/shard_map/ppermute | solution.py:58
  74.5 1.1 copy-start.1
  117.6 55.1 %collective-permute-start.8 = (bf16[384,2048]{0,1:T(8,128)(2,1)}, bf16[384,2048]{0,1:T(8,128)(2,1)S(1)}, u32[]{:S(2)}, u32[]{:S(2)}) collective-permute-start(bf16[384,2048]{0,1:T(8,128)(2,1)} %pad_maximum_fusion), channel_id=1, source_target_pairs={{0,1},{1,0},{2,3},{3,2},{4,5},{5,4},{6,7},{7,6},{8,9},{9,8},{10,11... | collective-permute-start | bytes 4718600 | tf_op jit(solution)/shard_map/ppermute | solution.py:54
  117.6 112.7 %all-reduce.10.cloned.1.call-start = ((), (), s32[]{:S(2)}) async-start(), calls=%async_computation.2 | async-start | bytes 2359296 | tf_op jit(solution)/shard_map/psum | solution.py:351
  172.4 115.4 %all-reduce.12.cloned.1.call-start = ((), (), s32[]{:S(2)}) async-start(), calls=%async_computation.3 | async-start | bytes 2359296 | tf_op jit(solution)/shard_map/psum | solution.py:351
  172.7 1.1 copy-start.2
  173.8 2.3 slice-start
  230.3 106.7 %all-reduce.14.cloned.1.call-start = ((), (), s32[]{:S(2)}) async-start(), calls=%async_computation.4 | async-start | bytes 1179648 | tf_op jit(solution)/shard_map/psum | solution.py:351
  350.1 4.7 %collective-permute-start.9 = (f32[288,2048]{1,0:T(8,128)}, f32[288,2048]{1,0:T(8,128)S(1)}, u32[]{:S(2)}, u32[]{:S(2)}) collective-permute-start(f32[288,2048]{1,0:T(8,128)} %get-tuple-element.81), channel_id=1, source_target_pairs={{0,1},{1,0},{2,3},{3,2},{4,5},{5,4},{6,7},{7,6},{8,9},{9,8},{10,11... | collective-permute-start | bytes 7077896 | tf_op jit(solution)/shard_map/ppermute | solution.py:54
  356.8 12.9 %copy-start.8 = (f32[96,2048]{1,0:T(8,128)S(1)}, f32[96,2048]{1,0:T(8,128)}, u32[]{:S(2)}) copy-start(f32[96,2048]{1,0:T(8,128)} %get-tuple-element.83) | copy-start | bytes 2359300
  356.9 12.1 %collective-permute-start.10 = (bf16[96,2048]{1,0:T(8,128)(2,1)S(1)}, bf16[96,2048]{1,0:T(8,128)(2,1)S(1)}, u32[]{:S(2)}, u32[]{:S(2)}) collective-permute-start(bf16[96,2048]{1,0:T(8,128)(2,1)S(1)} %slice.67), channel_id=1, source_target_pairs={{0,2},{1,3},{2,6},{3,7},{6,4},{7,5},{4,0},{5,1},{8,10},{9,11},{10,... | collective-permute-start | bytes 1179656 | tf_op jit(solution)/shard_map/ppermute | solution.py:58
  369.1 11.3 %collective-permute-start.11 = (bf16[96,2048]{1,0:T(8,128)(2,1)S(1)}, bf16[96,2048]{1,0:T(8,128)(2,1)S(1)}, u32[]{:S(2)}, u32[]{:S(2)}) collective-permute-start(bf16[96,2048]{1,0:T(8,128)(2,1)S(1)} %fusion.1), channel_id=1, source_target_pairs={{0,2},{1,3},{2,6},{3,7},{6,4},{7,5},{4,0},{5,1},{8,10},{9,11},{10,... | collective-permute-start | bytes 1179656 | tf_op jit(solution)/shard_map/ppermute | solution.py:58
  369.7 32.0 %collective-permute-start.13 = (f32[96,2048]{1,0:T(8,128)S(1)}, f32[96,2048]{1,0:T(8,128)S(1)}, u32[]{:S(2)}, u32[]{:S(2)}) collective-permute-start(f32[96,2048]{1,0:T(8,128)S(1)} %copy-done.8), channel_id=1, source_target_pairs={{0,1},{1,0},{2,3},{3,2},{4,5},{5,4},{6,7},{7,6},{8,9},{9,8},{10,11... | collective-permute-start | bytes 2359304 | tf_op jit(solution)/shard_map/ppermute | solution.py:54
  380.5 21.3 %collective-permute-start.12 = (bf16[96,2048]{1,0:T(8,128)(2,1)S(1)}, bf16[96,2048]{1,0:T(8,128)(2,1)S(1)}, u32[]{:S(2)}, u32[]{:S(2)}) collective-permute-start(bf16[96,2048]{1,0:T(8,128)(2,1)S(1)} %fusion), channel_id=1, source_target_pairs={{0,2},{1,3},{2,6},{3,7},{6,4},{7,5},{4,0},{5,1},{8,10},{9,11},{10,... | collective-permute-start | bytes 1179656 | tf_op jit(solution)/shard_map/ppermute | solution.py:58
  393.6 8.2 %copy-start.4 = (f32[96,2048]{1,0:T(8,128)S(1)}, f32[96,2048]{1,0:T(8,128)}, u32[]{:S(2)}) copy-start(f32[96,2048]{1,0:T(8,128)} %get-tuple-element.82) | copy-start | bytes 2359300
Sparse Core Ops, SparseCore 0:
  55.6 58.6 all-reduce.5
  117.7 54.6 all-reduce.7
  175.8 54.4 all-reduce.9
  233.3 54.4 all-reduce.11
  290.9 46.0 all-reduce.13

commit v3 on v0

v3 whole, which is shorter than its diff:
```python
import functools
import math

import jax
import jax.numpy as jnp
from jax import lax
from jax.experimental import pallas as pl
from jax.experimental.pallas import tpu as pltpu
from jax.sharding import PartitionSpec as P

BLOCK = 128
BF16 = jnp.bfloat16
F32 = jnp.float32
VMEM_BYTES = 60 * 1024 * 1024
NT = (((1,), (1,)), ((), ()))
NN = (((1,), (0,)), ((), ()))


def params():
    return pltpu.CompilerParams(vmem_limit_bytes=VMEM_BYTES)


def after(x, *others):
    return lax.optimization_barrier((x, *others))[0]


def step_of(hid):
    return 512 if hid % 512 == 0 else 256


def chunk_of(size, most):
    return max(c for c in (128, 256, 512, 1024) if size % c == 0 and c <= most)


def ring_of(chips):
    return [0] + list(range(1, chips, 2)) + [c for c in range(chips - 1, 0, -1) if c % 2 == 0]


class Axes:
    def __init__(self, mesh):
        self.pipe = mesh.shape["pipe"]
        self.tensor = mesh.shape["tensor"]
        self.chips = self.tensor // 2
        self.ring = ring_of(self.chips)

    def slots(self):
        n = self.chips
        table = [[self.ring[(self.ring.index(c) - s) % n] for s in range(n)] for c in range(n)]
        return lax.dynamic_slice(jnp.array(table, jnp.int32), (lax.axis_index("tensor") // 2, 0), (1, n))[0]

    def rows(self, tok):
        chip = self.slots() * 2
        core = (lax.axis_index("tensor") % 2).astype(jnp.int32)
        mine, other = (chip + core) * tok, (chip + 1 - core) * tok
        place = lax.axis_index("pipe").astype(jnp.int32).reshape(1)
        return jnp.concatenate([mine[:1], other[:1], mine[1:], other[1:], place])

    def to_core(self, x):
        return lax.ppermute(x, "tensor", [(t, t ^ 1) for t in range(self.tensor)])

    def to_pipe(self, x, bit):
        return lax.ppermute(x, "pipe", [(i, i ^ bit) for i in range(self.pipe)])

    def to_next(self, x):
        pairs = [(self.ring[i], self.ring[(i + 1) % self.chips]) for i in range(self.chips)]
        return lax.ppermute(x, "tensor", [(2 * a + k, 2 * b + k) for a, b in pairs for k in range(2)])


def reduce_over_pipe(axes, partial, order):
    place = lax.axis_index("pipe")
    bits = axes.pipe.bit_length() - 1
    rows, cols = partial.shape
    left = partial.reshape((2,) * bits + (rows // axes.pipe, cols))
    for bit in order:
        axis = bits - bit.bit_length()
        here = (place // bit) % 2
        send = lax.dynamic_slice_in_dim(left, 1 - here, 1, axis).astype(BF16)
        keep = lax.dynamic_slice_in_dim(left, here, 1, axis)
        left = keep + axes.to_pipe(send, bit).astype(F32)
    held = {0: left.reshape(rows // axes.pipe, cols).astype(BF16)}
    for bit in reversed(order):
        for r in list(held):
            held[r ^ bit] = axes.to_pipe(held[r], bit)
    return [held[r] for r in range(axes.pipe)]


def grads_kernel(cfg, at_rows, *refs):
    refs = list(refs)
    sources = [[refs.pop(0) for _ in range(cfg["pipe"])] for _ in cfg["sources"]]
    gate_pre, up_pre, gate_out, up_out, hidden = refs
    k = pl.program_id(0)
    place = at_rows[cfg["groups"]]
    tok = cfg["tok"]

    for src, arrays in zip(cfg["sources"], sources):

        def copy(src=src, arrays=arrays):
            for r in range(cfg["pipe"]):
                to = src["base"] + (place ^ r) * src["part"]
                hidden[pl.ds(pl.multiple_of(to, 16), src["part"]), :] = arrays[r][...]

        if src["lo"] <= 0 and src["hi"] >= cfg["steps"]:
            copy()
        else:
            pl.when((k >= src["lo"]) & (k < src["hi"]))(copy)

    for i in range(cfg["groups"]):
        at = pl.ds(pl.multiple_of(at_rows[i], 16), tok)
        g = gate_pre[at, :].astype(F32)
        u = up_pre[at, :].astype(F32)
        h = hidden[i * tok : (i + 1) * tok, :].astype(F32)
        sig = 1.0 / (1.0 + jnp.exp(-g))
        gate_out[at, :] = (h * u * sig * (1.0 + g * (1.0 - sig))).astype(BF16)
        up_out[at, :] = (h * g * sig).astype(BF16)


def local_grads(axes, at_rows, sources, gate_pre, up_pre, tok, start, cols):
    tokens = gate_pre.shape[0]
    step = start
    for _, _, c0, w in sources:
        step = math.gcd(step, math.gcd(c0, w))
    step = step or cols
    first = start // step
    infos, specs, arrays = [], [], []
    for parts, base, c0, w in sources:
        part = parts[0].shape[0]
        lo, n = (c0 - start) // step, w // step
        infos.append(dict(base=base, part=part, lo=lo, hi=lo + n))
        arrays += parts
        spec = pl.BlockSpec((part, step), lambda k, _, lo=lo, n=n: (0, jnp.clip(k - lo, 0, n - 1)))
        specs += [spec] * len(parts)
    specs += [pl.BlockSpec((tokens, step), lambda k, _: (0, first + k))] * 2
    cfg = dict(sources=infos, pipe=axes.pipe, groups=tokens // tok, tok=tok, steps=cols // step)
    return pl.pallas_call(
        functools.partial(grads_kernel, cfg),
        out_shape=[jax.ShapeDtypeStruct((tokens, cols), BF16)] * 2,
        grid_spec=pltpu.PrefetchScalarGridSpec(
            num_scalar_prefetch=1,
            grid=(cols // step,),
            in_specs=specs,
            out_specs=[pl.BlockSpec((tokens, step), lambda k, _: (0, k))] * 2,
            scratch_shapes=[pltpu.VMEM((tokens, step), BF16)],
        ),
        compiler_params=params(),
        cost_estimate=pl.CostEstimate(
            flops=20 * tokens * cols, bytes_accessed=10 * tokens * cols, transcendentals=2 * tokens * cols
        ),
        name="local_grads",
    )(at_rows, *arrays, gate_pre, up_pre)


def down_kernel(cfg, at_rows, *refs):
    tokens = refs[:4]
    gate_pre, up_pre, mask, out, rows, hidden = refs[4:]
    tok = cfg["tok"]

    @pl.when(pl.program_id(0) == 0)
    def _():
        at = 0
        for ref in tokens:
            rows[at : at + ref.shape[0], :] = ref[...]
            at += ref.shape[0]

    for i in range(cfg["groups"]):
        at = pl.ds(pl.multiple_of(at_rows[i], 16), tok)
        g = gate_pre[at, :].astype(F32)
        u = up_pre[at, :].astype(F32)
        hidden[i * tok : (i + 1) * tok, :] = (g * (1.0 / (1.0 + jnp.exp(-g))) * u).astype(BF16)
    across = hidden[...].T
    chunk = cfg["chunk"]

    def tile(n):
        at = pl.ds(pl.multiple_of(n * chunk, chunk), chunk)
        term = lax.dot_general(across, rows[:, at], NN, preferred_element_type=F32)
        for i in range(cfg["step"] // BLOCK):
            part = slice(i * BLOCK, (i + 1) * BLOCK)
            out[part, at] = (term[part, :] * mask[i, :, at]).astype(BF16)

    pl.loop(0, cfg["width"] // chunk)(tile)


def down_grad(at_rows, out_grad, gate_pre, up_pre, mask, tok):
    tokens, hid = gate_pre.shape
    width = out_grad[0].shape[1]
    step = step_of(hid)
    cfg = dict(groups=tokens // tok, tok=tok, width=width, step=step, chunk=chunk_of(width, 1024))
    return pl.pallas_call(
        functools.partial(down_kernel, cfg),
        out_shape=jax.ShapeDtypeStruct((hid, width), BF16),
        grid_spec=pltpu.PrefetchScalarGridSpec(
            num_scalar_prefetch=1,
            grid=(hid // step,),
            in_specs=[pl.BlockSpec(t.shape, lambda k, _: (0, 0), pipeline_mode=pl.Buffered(1)) for t in out_grad]
            + [pl.BlockSpec((tokens, step), lambda k, _: (0, k))] * 2
            + [pl.BlockSpec((step // BLOCK, 1, width), lambda k, _: (k, 0, 0))],
            out_specs=pl.BlockSpec((step, width), lambda k, _: (k, 0)),
            scratch_shapes=[pltpu.VMEM((tokens, width), BF16), pltpu.VMEM((tokens, step), BF16)],
        ),
        compiler_params=params(),
        cost_estimate=pl.CostEstimate(
            flops=2 * tokens * width * hid,
            bytes_accessed=2 * (tokens * width + 2 * tokens * hid + width * hid),
            transcendentals=tokens * hid,
        ),
        name="down_grad",
    )(at_rows, *out_grad, gate_pre, up_pre, mask)


def masked(weight, mask):
    rows, cols = weight.shape
    return (weight.reshape(rows // BLOCK, BLOCK, cols) * mask.astype(BF16)[:, None, :]).reshape(rows, cols)


def round_ring(axes, x):
    half = x.shape[0] // 2
    now = [x[:half], x[half:]]
    got = []
    for _ in range(axes.chips - 1):
        now = [axes.to_next(a) for a in now]
        got += now
    return jnp.concatenate(got, axis=0)


def halves(start, cols):
    first = cols // 2 if cols // 2 % BLOCK == 0 else cols // 2 // BLOCK * BLOCK + BLOCK
    return [(start, first), (start + first, cols - first)]


def dot_nt(a, b):
    return lax.dot_general(a, b, NT, preferred_element_type=F32)


def weight_grad(x, grad, mask):
    tokens, width = x.shape
    blocks = width // BLOCK
    out = lax.dot_general(
        x.reshape(tokens, blocks, BLOCK), grad, (((0,), (0,)), ((), ())), preferred_element_type=F32
    )
    return (out * mask[:, None, :]).astype(BF16).reshape(width, grad.shape[1])


def shards(axes, layer_input, out_grad, gate_pre, up_pre, gate_weight, up_weight, down_weight, gate_mask, up_mask, down_mask):
    tokens, hid = gate_pre.shape
    tok, width = out_grad.shape
    at_rows = axes.rows(tok)
    gate_m = jnp.repeat(gate_mask, BLOCK, axis=1).astype(F32)
    up_m = jnp.repeat(up_mask, BLOCK, axis=1).astype(F32)
    down_m = jnp.repeat(down_mask, BLOCK, axis=1).astype(F32)
    bits = [1 << i for i in range(axes.pipe.bit_length() - 1)]
    orders = [bits, bits[::-1]]
    pieces = halves(0, hid)

    near = [out_grad, axes.to_core(out_grad)]
    far = round_ring(axes, out_grad)
    far = [far, axes.to_core(far)]

    downs = [masked(down_weight[c : c + w], down_m[c // BLOCK : (c + w) // BLOCK]) for c, w in pieces]
    near_rows = jnp.concatenate(near, axis=0)
    split_near = 2 * tok % (16 * axes.pipe) == 0
    sources = [[] for _ in pieces]
    if split_near:
        for j, (c, w) in enumerate(pieces):
            total = reduce_over_pipe(axes, dot_nt(near_rows, downs[j]), orders[j])
            sources[j].append((total, 0, c, w))
    gates = [masked(gate_weight[:, c : c + w], gate_m[:, c : c + w]) for c, w in pieces]
    ups = [masked(up_weight[:, c : c + w], up_m[:, c : c + w]) for c, w in pieces]
    far_rows = after(jnp.concatenate(far, axis=0), *gates, *ups)
    if not split_near:
        far_rows = jnp.concatenate([near_rows, far_rows], axis=0)
    parts = []
    for j, (c, w) in enumerate(pieces):
        parts.append(dot_nt(far_rows, downs[j]))
        for order, (sc, sw) in zip(orders, halves(c, w)):
            total = reduce_over_pipe(axes, parts[j][:, sc - c : sc - c + sw], order)
            sources[j].append((total, 2 * tok if split_near else 0, sc, sw))

    x = lax.all_gather(after(layer_input, far_rows), "tensor", axis=0, tiled=True)
    grad_down = down_grad(after(at_rows, *parts), near + far, gate_pre, up_pre, down_m[:, None, :], tok)
    at_rows = after(at_rows, grad_down)

    acc, gate_grads, up_grads = None, [], []
    for j, (c, w) in enumerate(pieces):
        gate, up = local_grads(axes, at_rows, sources[j], gate_pre, up_pre, tok, c, w)
        term = dot_nt(gate, gates[j]) + dot_nt(up, ups[j])
        acc = term if acc is None else acc + term
        gate_grads.append(gate)
        up_grads.append(up)

    core = lax.axis_index("tensor") % 2
    slots = axes.slots()
    by_core = acc.reshape(axes.chips, 2, tok, width)
    pick = lambda a, i, axis: lax.dynamic_index_in_dim(a, i, axis, keepdims=False)
    total = pick(by_core, core, 1) + axes.to_core(pick(by_core, 1 - core, 1))
    grad_input = []
    for i in range(2):
        half = total[:, :, i * (width // 2) : (i + 1) * (width // 2)]
        run = pick(half, slots[1 % axes.chips], 0)
        for s in range(1, axes.chips):
            run = axes.to_next(run.astype(BF16)).astype(F32) + pick(half, slots[(s + 1) % axes.chips], 0)
        grad_input.append(run.astype(BF16))
    grad_gate = weight_grad(x, jnp.concatenate(gate_grads, axis=1), gate_m)
    grad_up = weight_grad(x, jnp.concatenate(up_grads, axis=1), up_m)
    return (jnp.concatenate(grad_input, axis=1), grad_gate, grad_up, grad_down)


def solution(mesh):
    in_specs = (
        P("tensor", "pipe"),
        P("tensor", "pipe"),
        P(None, "tensor"),
        P(None, "tensor"),
        P("pipe", "tensor"),
        P("pipe", "tensor"),
        P("tensor", "pipe"),
        P("pipe", "tensor"),
        P("pipe", "tensor"),
        P("tensor", "pipe"),
    )
    out_specs = (P("tensor", "pipe"), P("pipe", "tensor"), P("pipe", "tensor"), P("tensor", "pipe"))
    return jax.shard_map(
        functools.partial(shards, Axes(mesh)), mesh=mesh, in_specs=in_specs, out_specs=out_specs, check_vma=False
    )
```

time: 483 us -> 358 us (0.74)
  local copies, waits for them, and re-layouts: 121 us -> 18 us
  waiting for transfers between devices: 177 us -> 88.9 us
  starting transfers between devices: 0.33 us -> 53.3 us
  Pallas kernels: 0 us -> 40.1 us
  matrix products: 129 us -> 93.1 us
  between operations: 14.5 us -> 22.8 us
    psum x1 -> x0, waiting for transfers between devices: 133 us -> none  [shards(): hidden_grad = lax.psum(hidden_partial, 'pipe')]
    unnamed x34 -> x99, local copies, waits for them, and re-layouts: 99.9 us -> 6.48 us
    ppermute x0 -> x45, waiting for transfers between devices: none -> 88.9 us  [the longest x12 48.3 us: to_next(): lax.ppermute(x, 'tensor', [(2 * a + k, 2 * b + k) for a, b in pairs for k...]
    ppermute x0 -> x45, starting transfers between devices: none -> 53.3 us  [the longest x30 38.2 us: to_pipe(): return lax.ppermute(x, 'pipe', [(i, i ^ bit) for i in range(self.pipe)])]
    all_gather x2 -> x1, waiting for transfers between devices: 41.8 us -> 0.01 us  [shards(): lax.all_gather(after(layer_input, far_rows), 'tensor', axis=0, tiled=True)]
    pallas_call x0 -> x3, Pallas kernels: none -> 40.1 us  [the longest x1 23.3 us: down_grad(): pl.pallas_call(functools.partial(down_kernel, cfg), out_shape=jax.ShapeDt...]
    dot_general x6 -> x10, matrix products: 129 us -> 93.1 us  [the longest x8 60.6 us: dot_nt(): return lax.dot_general(a, b, NT, preferred_element_type=F32)]
    broadcast_in_dim x4 -> x5, local copies, waits for them, and re-layouts: 20.3 us -> 1.29 us  [the longest x3 1.05 us: shards(): down_m = jnp.repeat(down_mask, BLOCK, axis=1).astype(F32)]
  transfers between devices with their start and end apart: 4 -> 46, of which waited for: 2 -> 15; matrix products, arithmetic and copies ran while one was open for 51% -> 20% of each run, Pallas kernels for 0% -> 9%
where the time goes in v3:
time: 358 us; the launch traced here: 352 us
  matrix products  93.1 us (26%)
  waiting for transfers between devices  88.9 us (25%)
  starting transfers between devices  53.3 us (15%)
  Pallas kernels  40.1 us (11%)
  other arithmetic  35.6 us (10%)
  between operations  22.8 us (6%)
  local copies, waits for them, and re-layouts  18 us (5%)
    dot_general x8, matrix products, dot_nt(): return lax.dot_general(a, b, NT, preferred_element_type=F32)  60.6 us
    ppermute x12, waiting for transfers between devices, to_next(): lax.ppermute(x, 'tensor', [(2 * a + k, 2 * b + k) for a, b in pairs for k...  48.3 us
    ppermute x30, starting transfers between devices, to_pipe(): return lax.ppermute(x, 'pipe', [(i, i ^ bit) for i in range(self.pipe)])  38.2 us
    ppermute x30, waiting for transfers between devices, to_pipe(): return lax.ppermute(x, 'pipe', [(i, i ^ bit) for i in range(self.pipe)])  37.4 us
    dot_general x2, matrix products, weight_grad(): lax.dot_general(x.reshape(tokens, blocks, BLOCK), grad, (((0,), (0,)), ((...  32.6 us
    mul x3, other arithmetic, masked(): weight.reshape(rows // BLOCK, BLOCK, cols) * mask.astype(BF16)[:, None, :]  25.4 us
    pallas_call x1, Pallas kernels, down_grad(): pl.pallas_call(functools.partial(down_kernel, cfg), out_shape=jax.ShapeDt...  23.3 us
    pallas_call x2, Pallas kernels, local_grads(): pl.pallas_call(functools.partial(grads_kernel, cfg), out_shape=[jax.Shape...  16.8 us
  transfers between devices with their start and end apart: 46, of which 15 were waited for; matrix products, arithmetic and copies ran while one was open for 20% of the time, Pallas kernels for 9%

profile of v3, /device:TPU:0, one launch (start us, length us, event | category | flops | bytes accessed | tf_op | source)
XLA Modules:
  0.0 351.9 jit_solution(6626145947579988484)
XLA Ops:
  18.8 12.1 %bitcast_multiply_fusion = (bf16[1792,2048]{1,0:T(8,128)(2,1)}, bf16[1792,2048]{1,0:T(8,128)(2,1)}) fusion(bf16[3584,2048]{1,0:T(8,128)(2,1)} %param.18, bf16[14,2048]{1,0:T(8,128)(2,1)S(1)} %bitcast.152, bf16[14,2048]{1,0:T(8,128)(2,1)S(1)} %bitcast.151), kind=kLoop, calls=%fused_computation.6 | loop fusion | flops 7340032 | bytes 29474816 | tf_op jit(solution)/shard_map/mul | solution.py:211
  33.6 7.6 %bitcast_multiply_fusion.4 = (bf16[2048,1792]{1,0:T(8,128)(2,1)}, bf16[2048,1792]{1,0:T(8,128)(2,1)}) fusion(bf16[2048,3584]{1,0:T(8,128)(2,1)S(1)} %bitcast.126, bf16[16,1792]{1,0:T(8,128)(2,1)S(1)} %get-tuple-element.52, bf16[16,1792]{1,0:T(8,128)(2,1)S(1)} %get-tuple-element.53), kind=kLoop, calls=%fused_computation.10 | loop fusion | flops 7340032 | bytes 29474816 | tf_op jit(solution)/shard_map/mul | solution.py:211
  43.0 5.7 %bitcast_multiply_fusion.2 = (bf16[2048,1792]{1,0:T(8,128)(2,1)}, bf16[2048,1792]{1,0:T(8,128)(2,1)}) fusion(bf16[2048,3584]{1,0:T(8,128)(2,1)S(1)} %bitcast.128, bf16[16,1792]{1,0:T(8,128)(2,1)S(1)} %get-tuple-element.50, bf16[16,1792]{1,0:T(8,128)(2,1)S(1)} %get-tuple-element.51), kind=kLoop, calls=%fused_computation.8 | loop fusion | flops 7340032 | bytes 29474816 | tf_op jit(solution)/shard_map/mul | solution.py:211
  50.2 5.8 %fusion = f32[2,2,48,1792]{3,2,1,0:T(8,128)S(1)} fusion(bf16[2,2,48,2048]{3,2,1,0:T(8,128)(2,1)S(1)} %bitcast.149, bf16[1792,2048]{1,0:T(8,128)(2,1)} %get-tuple-element.24), kind=kOutput, calls=%fused_computation.2 | convolution fusion | flops 1409286144 | bytes 9502720 | tf_op jit(solution)/shard_map/dot_general | solution.py:230
  63.7 2.7 collective-permute-start.4
  66.6 6.3 %collective-permute-done.4 = bf16[48,2048]{1,0:T(8,128)(2,1)S(1)} collective-permute-done((bf16[48,2048]{1,0:T(8,128)(2,1)S(1)}, bf16[48,2048]{1,0:T(8,128)(2,1)S(1)}, u32[]{:S(2)}, u32[]{:S(2)}) %collective-permute-start.4) | collective-permute-done | bytes 196640 | tf_op jit(solution)/shard_map/ppermute | solution.py:66
  74.5 5.5 %collective-permute-done.24 = bf16[1,1,48,1792]{3,2,1,0:T(8,128)(2,1)S(1)} collective-permute-done((bf16[1,1,48,1792]{3,2,1,0:T(8,128)(2,1)S(1)}, bf16[1,1,48,1792]{3,2,1,0:T(8,128)(2,1)S(1)}, u32[]{:S(2)}, u32[]{:S(2)}) %collective-permute-start.24) | collective-permute-done | bytes 172064 | tf_op jit(solution)/shard_map/ppermute | solution.py:62
  83.0 4.5 %fusion.36 = f32[576,1792]{1,0:T(8,128)S(1)} fusion(bf16[576,2048]{1,0:T(8,128)(2,1)S(1)} %constant_dynamic-update-slice_fusion.6, bf16[1792,2048]{1,0:T(8,128)(2,1)S(1)} %bitcast.132), kind=kOutput, calls=%fused_computation.104 | convolution fusion | flops 4227858432 | bytes 13828096 | tf_op jit(solution)/shard_map/dot_general | solution.py:230
  87.5 4.5 %fusion.35 = f32[576,1792]{1,0:T(8,128)S(1)} fusion(bf16[576,2048]{1,0:T(8,128)(2,1)S(1)} %constant_dynamic-update-slice_fusion.6, bf16[1792,2048]{1,0:T(8,128)(2,1)S(1)} %bitcast.130), kind=kOutput, calls=%fused_computation.103 | convolution fusion | flops 4227858432 | bytes 13828096 | tf_op jit(solution)/shard_map/dot_general | solution.py:230
  94.8 10.1 %collective-permute-done.33 = bf16[1,2,144,896]{3,2,1,0:T(8,128)(2,1)S(1)} collective-permute-done((bf16[1,2,144,896]{3,2,1,0:T(8,128)(2,1)S(1)}, bf16[1,2,144,896]{3,2,1,0:T(8,128)(2,1)S(1)}, u32[]{:S(2)}, u32[]{:S(2)}) %collective-permute-start.33) | collective-permute-done | bytes 516128 | tf_op jit(solution)/shard_map/ppermute | solution.py:62
  107.3 9.2 %collective-permute-done.18 = bf16[1,2,144,896]{3,2,1,0:T(8,128)(2,1)S(1)} collective-permute-done((bf16[1,2,144,896]{3,2,1,0:T(8,128)(2,1)S(1)}, bf16[1,2,144,896]{3,2,1,0:T(8,128)(2,1)S(1)}, u32[]{:S(2)}, u32[]{:S(2)}) %collective-permute-start.18) | collective-permute-done | bytes 516128 | tf_op jit(solution)/shard_map/ppermute | solution.py:62
  120.3 3.1 collective-permute-done.34
  136.3 8.5 %collective-permute-done.27.refs_3_ = bf16[48,1792]{1,0:T(8,128)(2,1)S(1)} collective-permute-done((bf16[48,1792]{1,0:T(8,128)(2,1)S(1)}, bf16[48,1792]{1,0:T(8,128)(2,1)S(1)}, u32[]{:S(2)}, u32[]{:S(2)}) %collective-permute-start.27) | collective-permute-done | bytes 172064 | tf_op jit(solution)/shard_map/ppermute | solution.py:62
  151.9 23.3 %down_grad.1 = bf16[3584,2048]{1,0:T(8,128)(2,1)} custom-call(s32[9]{0:T(128)} %concatenate.22.at_rows, bf16[96,2048]{1,0:T(8,128)(2,1)} %refs_0_.1, bf16[96,2048]{1,0:T(8,128)(2,1)} %copy-done.8, bf16[288,2048]{1,0:T(8,128)(2,1)} %copy-done.27, bf16[288,2048]{1,0:T(8,128)(2,1)} %copy-done.1, bf16[768,3584]{1,0:T(8,128)(2,1)} %refs_12_.3, ...), custom_call_target="tpu_custom_call" | custom-call | flops 11274289152 | bytes 28835840 | tf_op jit(solution)/shard_map/down_grad/pallas_call | solution.py:187
  177.9 8.4 %local_grads.3 = (bf16[768,1792]{1,0:T(8,128)(2,1)}, bf16[768,1792]{1,0:T(8,128)(2,1)}) custom-call(s32[9]{0:T(128)} %concatenate.22.at_rows, bf16[48,1792]{1,0:T(8,128)(2,1)} %copy-done.7, bf16[48,1792]{1,0:T(8,128)(2,1)} %copy-done.24, bf16[48,1792]{1,0:T(8,128)(2,1)} %copy-done.23, bf16[48,1792]{1,0:T(8,128)(2,1)} %copy-done.25, ...), custom_call_target="tpu_custom_call" | custom-call | flops 27525120 | bytes 13762560 | tf_op jit(solution)/shard_map/local_grads/pallas_call | solution.py:134
  189.0 10.6 %fusion.39 = f32[768,2048]{1,0:T(8,128)} fusion(bf16[768,1792]{1,0:T(8,128)(2,1)} %get-tuple-element.18, bf16[2048,1792]{1,0:T(8,128)(2,1)} %get-tuple-element.26), kind=kOutput, calls=%fused_computation.107 | convolution fusion | flops 5637144576 | bytes 16384000 | tf_op jit(solution)/shard_map/dot_general | solution.py:230
  201.3 8.4 %local_grads.2 = (bf16[768,1792]{1,0:T(8,128)(2,1)}, bf16[768,1792]{1,0:T(8,128)(2,1)}) custom-call(s32[9]{0:T(128)} %concatenate.22.at_rows, bf16[48,1792]{1,0:T(8,128)(2,1)} %copy-done.6, bf16[48,1792]{1,0:T(8,128)(2,1)} %collective-permute-done.10.refs_1_, bf16[48,1792]{1,0:T(8,128)(2,1)} %copy-done.22, bf16[48,1792]{1,0:T(8,128)(2,1)} %copy-done.26, ...), custom_call_target="tpu_custom_call" | custom-call | flops 27525120 | bytes 13762560 | tf_op jit(solution)/shard_map/local_grads/pallas_call | solution.py:134
  209.8 10.9 %fusion.38 = f32[768,2048]{1,0:T(8,128)} fusion(bf16[768,1792]{1,0:T(8,128)(2,1)} %get-tuple-element.16, bf16[2048,1792]{1,0:T(8,128)(2,1)} %get-tuple-element.27), kind=kOutput, calls=%fused_computation.106 | convolution fusion | flops 5637144576 | bytes 16384000 | tf_op jit(solution)/shard_map/dot_general | solution.py:230
  220.6 9.9 %fusion.37 = f32[768,2048]{1,0:T(8,128)} fusion(bf16[768,1792]{1,0:T(8,128)(2,1)S(1)} %copy-done.30, bf16[2048,1792]{1,0:T(8,128)(2,1)} %get-tuple-element.29), kind=kOutput, calls=%fused_computation.105 | convolution fusion | flops 5637144576 | bytes 16384000 | tf_op jit(solution)/shard_map/dot_general | solution.py:230
  230.6 11.8 %add_add_fusion = f32[768,2048]{1,0:T(8,128)} fusion(f32[768,2048]{1,0:T(8,128)} %fusion.39, f32[768,2048]{1,0:T(8,128)} %fusion.37, f32[768,2048]{1,0:T(8,128)} %fusion.38, bf16[768,1792]{1,0:T(8,128)(2,1)S(1)} %copy-done.29, bf16[2048,1792]{1,0:T(8,128)(2,1)S(1)} %bitcast.134), kind=kOutput, calls=%fused_computation.12 | convolution fusion | flops 5641863168 | bytes 35258368 | tf_op jit(solution)/shard_map/dot_general | solution.py:230
  247.2 3.2 collective-permute-done.38
  250.4 3.7 %bitcast_add_fusion = f32[4,96,2048]{2,1,0:T(8,128)S(1)} fusion(f32[4,96,2048]{2,1,0:T(8,128)} %collective-permute-done.38, f32[4,2,96,2048]{3,2,1,0:T(8,128)} %bitcast.144, s32[]{:T(128)S(6)} %select_n.126), kind=kLoop, calls=%fused_computation.19 | loop fusion | flops 786432 | bytes 9437188 | tf_op jit(solution)/shard_map/add | solution.py:293
  261.2 3.5 collective-permute-start.39
  264.7 6.5 %collective-permute-done.42 = bf16[96,1024]{1,0:T(8,128)(2,1)} collective-permute-done((bf16[96,1024]{1,0:T(8,128)(2,1)}, bf16[96,1024]{1,0:T(8,128)(2,1)}, u32[]{:S(2)}, u32[]{:S(2)}) %collective-permute-start.42) | collective-permute-done | bytes 196640 | tf_op jit(solution)/shard_map/ppermute | solution.py:66
  272.2 9.6 %collective-permute-done.39 = bf16[96,1024]{1,0:T(8,128)(2,1)S(1)} collective-permute-done((bf16[96,1024]{1,0:T(8,128)(2,1)S(1)}, bf16[96,1024]{1,0:T(8,128)(2,1)S(1)}, u32[]{:S(2)}, u32[]{:S(2)}) %collective-permute-start.39) | collective-permute-done | bytes 196640 | tf_op jit(solution)/shard_map/ppermute | solution.py:66
  281.9 8.5 %collective-permute-done.43 = bf16[96,1024]{1,0:T(8,128)(2,1)S(1)} collective-permute-done((bf16[96,1024]{1,0:T(8,128)(2,1)S(1)}, bf16[96,1024]{1,0:T(8,128)(2,1)S(1)}, u32[]{:S(2)}, u32[]{:S(2)}) %collective-permute-start.43) | collective-permute-done | bytes 196640 | tf_op jit(solution)/shard_map/ppermute | solution.py:66
  290.5 7.2 %collective-permute-done.40 = bf16[96,1024]{1,0:T(8,128)(2,1)S(1)} collective-permute-done((bf16[96,1024]{1,0:T(8,128)(2,1)S(1)}, bf16[96,1024]{1,0:T(8,128)(2,1)S(1)}, u32[]{:S(2)}, u32[]{:S(2)}) %collective-permute-start.40) | collective-permute-done | bytes 196640 | tf_op jit(solution)/shard_map/ppermute | solution.py:66
  297.8 5.3 %collective-permute-done.44 = bf16[96,1024]{1,0:T(8,128)(2,1)S(1)} collective-permute-done((bf16[96,1024]{1,0:T(8,128)(2,1)S(1)}, bf16[96,1024]{1,0:T(8,128)(2,1)S(1)}, u32[]{:S(2)}, u32[]{:S(2)}) %collective-permute-start.44) | collective-permute-done | bytes 196640 | tf_op jit(solution)/shard_map/ppermute | solution.py:66
  303.2 4.8 %collective-permute-done.41 = bf16[96,1024]{1,0:T(8,128)(2,1)S(1)} collective-permute-done((bf16[96,1024]{1,0:T(8,128)(2,1)S(1)}, bf16[96,1024]{1,0:T(8,128)(2,1)S(1)}, u32[]{:S(2)}, u32[]{:S(2)}) %collective-permute-start.41) | collective-permute-done | bytes 196640 | tf_op jit(solution)/shard_map/ppermute | solution.py:66
  308.8 3.2 copy.23
  312.0 16.8 %multiply_convert_fusion.1 = bf16[16,128,3584]{2,1,0:T(8,128)(2,1)} fusion(f32[16,3584]{1,0:T(8,128)S(1)} %get-tuple-element.23, bf16[768,16,128]{0,2,1:T(8,128)(2,1)S(1)} %bitcast.145, bf16[768,1792]{1,0:T(8,128)(2,1)} %get-tuple-element.17, bf16[768,1792]{1,0:T(8,128)(2,1)} %get-tuple-element.15), kind=kOutput, calls=%fused_computation.1 | convolution fusion | flops 11299979264 | bytes 23560192 | tf_op jit(solution)/shard_map/dot_general | solution.py:236
  328.8 15.8 %multiply_convert_fusion = bf16[16,128,3584]{2,1,0:T(8,128)(2,1)} fusion(f32[16,3584]{1,0:T(8,128)S(1)} %copy-done.21, bf16[768,16,128]{0,2,1:T(8,128)(2,1)S(1)} %bitcast.146, bf16[768,1792]{1,0:T(8,128)(2,1)S(1)} %copy-done.28, bf16[768,1792]{1,0:T(8,128)(2,1)} %get-tuple-element.16), kind=kOutput, calls=%fused_computation | convolution fusion | flops 11299979264 | bytes 23560192 | tf_op jit(solution)/shard_map/dot_general | solution.py:236
  (244 shorter events, 72.0 us)
Async XLA Ops:
  7.2 301.6 %all-gather.2.cloned.1.call-start = ((), (), s32[]{:S(2)}) async-start(), calls=%async_computation | async-start | bytes 3538944 | tf_op jit(solution)/shard_map/all_gather | solution.py:277
  7.2 42.9 %collective-permute-start.7 = (bf16[96,2048]{1,0:T(8,128)(2,1)}, bf16[96,2048]{1,0:T(8,128)(2,1)S(1)}, u32[]{:S(2)}, u32[]{:S(2)}) collective-permute-start(bf16[96,2048]{1,0:T(8,128)(2,1)} %refs_0_.1), channel_id=1, source_target_pairs={{0,1},{1,0},{2,3},{3,2},{4,5},{5,4},{6,7},{7,6},{8,9},{9,8},{10,11... | collective-permute-start | bytes 1179656 | tf_op jit(solution)/shard_map/ppermute | solution.py:59
  8.8 40.7 %collective-permute-start.1 = (bf16[48,2048]{1,0:T(8,128)(2,1)S(1)}, bf16[48,2048]{1,0:T(8,128)(2,1)S(1)}, u32[]{:S(2)}, u32[]{:S(2)}) collective-permute-start(bf16[48,2048]{1,0:T(8,128)(2,1)S(1)} %get-tuple-element.36), channel_id=1, source_target_pairs={{0,2},{1,3},{2,6},{3,7},{6,4},{7,5},{4,0},{5,1},{8,10},{9,11},{10,... | collective-permute-start | bytes 589832 | tf_op jit(solution)/shard_map/ppermute | solution.py:66
  11.4 38.5 %collective-permute-start = (bf16[48,2048]{1,0:T(8,128)(2,1)S(1)}, bf16[48,2048]{1,0:T(8,128)(2,1)S(1)}, u32[]{:S(2)}, u32[]{:S(2)}) collective-permute-start(bf16[48,2048]{1,0:T(8,128)(2,1)S(1)} %get-tuple-element.37), channel_id=1, source_target_pairs={{0,2},{1,3},{2,6},{3,7},{6,4},{7,5},{4,0},{5,1},{8,10},{9,11},{10,... | collective-permute-start | bytes 589832 | tf_op jit(solution)/shard_map/ppermute | solution.py:66
  49.5 12.7 %collective-permute-start.3 = (bf16[48,2048]{1,0:T(8,128)(2,1)S(1)}, bf16[48,2048]{1,0:T(8,128)(2,1)S(1)}, u32[]{:S(2)}, u32[]{:S(2)}) collective-permute-start(bf16[48,2048]{1,0:T(8,128)(2,1)S(1)} %collective-permute-done.1), channel_id=1, source_target_pairs={{0,2},{1,3},{2,6},{3,7},{6,4},{7,5},{4,0},{5,1},{8,10},{9,11},{10,... | collective-permute-start | bytes 589832 | tf_op jit(solution)/shard_map/ppermute | solution.py:66
  50.0 13.8 %collective-permute-start.2 = (bf16[48,2048]{1,0:T(8,128)(2,1)S(1)}, bf16[48,2048]{1,0:T(8,128)(2,1)S(1)}, u32[]{:S(2)}, u32[]{:S(2)}) collective-permute-start(bf16[48,2048]{1,0:T(8,128)(2,1)S(1)} %collective-permute-done), channel_id=1, source_target_pairs={{0,2},{1,3},{2,6},{3,7},{6,4},{7,5},{4,0},{5,1},{8,10},{9,11},{10,... | collective-permute-start | bytes 589832 | tf_op jit(solution)/shard_map/ppermute | solution.py:66
  56.1 17.0 %collective-permute-start.23 = (bf16[1,2,48,1792]{3,2,1,0:T(8,128)(2,1)S(1)}, bf16[1,2,48,1792]{3,2,1,0:T(8,128)(2,1)S(1)}, u32[]{:S(2)}, u32[]{:S(2)}) collective-permute-start(bf16[1,2,48,1792]{3,2,1,0:T(8,128)(2,1)S(1)} %dynamic-slice_convert_fusion.4), channel_id=1, source_target_pairs={{0,16},{8,24},{16,0},{24,8},{1,17},{9,25},{17,1},{25,9},{2,18},{10... | collective-permute-start | bytes 1032200 | tf_op jit(solution)/shard_map/ppermute | solution.py:62
  60.6 13.2 %collective-permute-start.8 = (bf16[2,1,48,1792]{3,2,1,0:T(8,128)(2,1)S(1)}, bf16[2,1,48,1792]{3,2,1,0:T(8,128)(2,1)S(1)}, u32[]{:S(2)}, u32[]{:S(2)}) collective-permute-start(bf16[2,1,48,1792]{3,2,1,0:T(8,128)(2,1)S(1)} %dynamic-slice_convert_fusion.5), channel_id=1, source_target_pairs={{0,8},{8,0},{16,24},{24,16},{1,9},{9,1},{17,25},{25,17},{2,10},{10... | collective-permute-start | bytes 1032200 | tf_op jit(solution)/shard_map/ppermute | solution.py:62
  80.1 47.1 %collective-permute-start.26 = (bf16[48,1792]{1,0:T(8,128)(2,1)S(1)}, bf16[48,1792]{1,0:T(8,128)(2,1)S(1)}, u32[]{:S(2)}, u32[]{:S(2)}) collective-permute-start(bf16[48,1792]{1,0:T(8,128)(2,1)S(1)} %fusion.21.refs_0_), channel_id=1, source_target_pairs={{0,16},{8,24},{16,0},{24,8},{1,17},{9,25},{17,1},{25,9},{2,18},{10... | collective-permute-start | bytes 516104 | tf_op jit(solution)/shard_map/ppermute | solution.py:62
  80.7 46.7 %collective-permute-start.25 = (bf16[48,1792]{1,0:T(8,128)(2,1)S(1)}, bf16[48,1792]{1,0:T(8,128)(2,1)S(1)}, u32[]{:S(2)}, u32[]{:S(2)}) collective-permute-start(bf16[48,1792]{1,0:T(8,128)(2,1)S(1)} %fusion.21.refs_0_), channel_id=1, source_target_pairs={{0,8},{8,0},{16,24},{24,16},{1,9},{9,1},{17,25},{25,17},{2,10},{10... | collective-permute-start | bytes 516104 | tf_op jit(solution)/shard_map/ppermute | solution.py:62
  81.3 48.7 %collective-permute-start.11 = (bf16[48,1792]{1,0:T(8,128)(2,1)S(1)}, bf16[48,1792]{1,0:T(8,128)(2,1)S(1)}, u32[]{:S(2)}, u32[]{:S(2)}) collective-permute-start(bf16[48,1792]{1,0:T(8,128)(2,1)S(1)} %fusion.20.refs_0_), channel_id=1, source_target_pairs={{0,16},{8,24},{16,0},{24,8},{1,17},{9,25},{17,1},{25,9},{2,18},{10... | collective-permute-start | bytes 516104 | tf_op jit(solution)/shard_map/ppermute | solution.py:62
  92.4 12.6 %collective-permute-start.33 = (bf16[1,2,144,896]{3,2,1,0:T(8,128)(2,1)S(1)}, bf16[1,2,144,896]{3,2,1,0:T(8,128)(2,1)S(1)}, u32[]{:S(2)}, u32[]{:S(2)}) collective-permute-start(bf16[1,2,144,896]{3,2,1,0:T(8,128)(2,1)S(1)} %dynamic-slice_convert_fusion), channel_id=1, source_target_pairs={{0,16},{8,24},{16,0},{24,8},{1,17},{9,25},{17,1},{25,9},{2,18},{10... | collective-permute-start | bytes 1548296 | tf_op jit(solution)/shard_map/ppermute | solution.py:62
  93.0 12.6 %collective-permute-start.28 = (bf16[2,1,144,896]{3,2,1,0:T(8,128)(2,1)S(1)}, bf16[2,1,144,896]{3,2,1,0:T(8,128)(2,1)S(1)}, u32[]{:S(2)}, u32[]{:S(2)}) collective-permute-start(bf16[2,1,144,896]{3,2,1,0:T(8,128)(2,1)S(1)} %dynamic-slice_convert_fusion.1), channel_id=1, source_target_pairs={{0,8},{8,0},{16,24},{24,16},{1,9},{9,1},{17,25},{25,17},{2,10},{10... | collective-permute-start | bytes 1548296 | tf_op jit(solution)/shard_map/ppermute | solution.py:62
  105.6 12.5 %collective-permute-start.13 = (bf16[2,1,144,896]{3,2,1,0:T(8,128)(2,1)S(1)}, bf16[2,1,144,896]{3,2,1,0:T(8,128)(2,1)S(1)}, u32[]{:S(2)}, u32[]{:S(2)}) collective-permute-start(bf16[2,1,144,896]{3,2,1,0:T(8,128)(2,1)S(1)} %dynamic-slice_convert_fusion.3), channel_id=1, source_target_pairs={{0,8},{8,0},{16,24},{24,16},{1,9},{9,1},{17,25},{25,17},{2,10},{10... | collective-permute-start | bytes 1548296 | tf_op jit(solution)/shard_map/ppermute | solution.py:62
  127.2 19.3 %collective-permute-start.36 = (bf16[144,896]{1,0:T(8,128)(2,1)S(1)}, bf16[144,896]{1,0:T(8,128)(2,1)S(1)}, u32[]{:S(2)}, u32[]{:S(2)}) collective-permute-start(bf16[144,896]{1,0:T(8,128)(2,1)S(1)} %fusion.17.refs_8_), channel_id=1, source_target_pairs={{0,16},{8,24},{16,0},{24,8},{1,17},{9,25},{17,1},{25,9},{2,18},{10... | collective-permute-start | bytes 774152 | tf_op jit(solution)/shard_map/ppermute | solution.py:62
  127.3 19.8 %collective-permute-start.35 = (bf16[144,896]{1,0:T(8,128)(2,1)S(1)}, bf16[144,896]{1,0:T(8,128)(2,1)S(1)}, u32[]{:S(2)}, u32[]{:S(2)}) collective-permute-start(bf16[144,896]{1,0:T(8,128)(2,1)S(1)} %fusion.17.refs_8_), channel_id=1, source_target_pairs={{0,8},{8,0},{16,24},{24,16},{1,9},{9,1},{17,25},{25,17},{2,10},{10... | collective-permute-start | bytes 774152 | tf_op jit(solution)/shard_map/ppermute | solution.py:62
  129.9 19.6 %collective-permute-start.31 = (bf16[144,896]{1,0:T(8,128)(2,1)S(1)}, bf16[144,896]{1,0:T(8,128)(2,1)S(1)}, u32[]{:S(2)}, u32[]{:S(2)}) collective-permute-start(bf16[144,896]{1,0:T(8,128)(2,1)S(1)} %fusion.16.refs_4_), channel_id=1, source_target_pairs={{0,16},{8,24},{16,0},{24,8},{1,17},{9,25},{17,1},{25,9},{2,18},{10... | collective-permute-start | bytes 774152 | tf_op jit(solution)/shard_map/ppermute | solution.py:62
  132.6 17.0 %collective-permute-start.30 = (bf16[144,896]{1,0:T(8,128)(2,1)S(1)}, bf16[144,896]{1,0:T(8,128)(2,1)S(1)}, u32[]{:S(2)}, u32[]{:S(2)}) collective-permute-start(bf16[144,896]{1,0:T(8,128)(2,1)S(1)} %fusion.16.refs_4_), channel_id=1, source_target_pairs={{0,8},{8,0},{16,24},{24,16},{1,9},{9,1},{17,25},{25,17},{2,10},{10... | collective-permute-start | bytes 774152 | tf_op jit(solution)/shard_map/ppermute | solution.py:62
  144.8 41.5 %collective-permute-start.10 = (bf16[48,1792]{1,0:T(8,128)(2,1)S(1)}, bf16[48,1792]{1,0:T(8,128)(2,1)}, u32[]{:S(2)}, u32[]{:S(2)}) collective-permute-start(bf16[48,1792]{1,0:T(8,128)(2,1)S(1)} %fusion.20.refs_0_), channel_id=1, source_target_pairs={{0,8},{8,0},{16,24},{24,16},{1,9},{9,1},{17,25},{25,17},{2,10},{10... | collective-permute-start | bytes 516104 | tf_op jit(solution)/shard_map/ppermute | solution.py:62
  146.5 41.3 %collective-permute-start.20 = (bf16[144,896]{1,0:T(8,128)(2,1)S(1)}, bf16[144,896]{1,0:T(8,128)(2,1)S(1)}, u32[]{:S(2)}, u32[]{:S(2)}) collective-permute-start(bf16[144,896]{1,0:T(8,128)(2,1)S(1)} %fusion.15.refs_8_), channel_id=1, source_target_pairs={{0,8},{8,0},{16,24},{24,16},{1,9},{9,1},{17,25},{25,17},{2,10},{10... | collective-permute-start | bytes 774152 | tf_op jit(solution)/shard_map/ppermute | solution.py:62
  147.1 41.3 %collective-permute-start.16 = (bf16[144,896]{1,0:T(8,128)(2,1)S(1)}, bf16[144,896]{1,0:T(8,128)(2,1)S(1)}, u32[]{:S(2)}, u32[]{:S(2)}) collective-permute-start(bf16[144,896]{1,0:T(8,128)(2,1)S(1)} %fusion.14.refs_4_), channel_id=1, source_target_pairs={{0,16},{8,24},{16,0},{24,8},{1,17},{9,25},{17,1},{25,9},{2,18},{10... | collective-permute-start | bytes 774152 | tf_op jit(solution)/shard_map/ppermute | solution.py:62
  149.5 25.7 %collective-permute-start.37 = (bf16[144,896]{1,0:T(8,128)(2,1)S(1)}, bf16[144,896]{1,0:T(8,128)(2,1)S(1)}, u32[]{:S(2)}, u32[]{:S(2)}) collective-permute-start(bf16[144,896]{1,0:T(8,128)(2,1)S(1)} %collective-permute-done.35.refs_9_), channel_id=1, source_target_pairs={{0,16},{8,24},{16,0},{24,8},{1,17},{9,25},{17,1},{25,9},{2,18},{10... | collective-permute-start | bytes 774152 | tf_op jit(solution)/shard_map/ppermute | solution.py:62
  149.6 26.3 %collective-permute-start.32 = (bf16[144,896]{1,0:T(8,128)(2,1)S(1)}, bf16[144,896]{1,0:T(8,128)(2,1)S(1)}, u32[]{:S(2)}, u32[]{:S(2)}) collective-permute-start(bf16[144,896]{1,0:T(8,128)(2,1)S(1)} %collective-permute-done.31.refs_6_), channel_id=1, source_target_pairs={{0,8},{8,0},{16,24},{24,16},{1,9},{9,1},{17,25},{25,17},{2,10},{10... | collective-permute-start | bytes 774152 | tf_op jit(solution)/shard_map/ppermute | solution.py:62
  175.2 24.5 %collective-permute-start.12 = (bf16[48,1792]{1,0:T(8,128)(2,1)S(1)}, bf16[48,1792]{1,0:T(8,128)(2,1)S(1)}, u32[]{:S(2)}, u32[]{:S(2)}) collective-permute-start(bf16[48,1792]{1,0:T(8,128)(2,1)S(1)} %collective-permute-done.11.refs_2_), channel_id=1, source_target_pairs={{0,8},{8,0},{16,24},{24,16},{1,9},{9,1},{17,25},{25,17},{2,10},{10... | collective-permute-start | bytes 516104 | tf_op jit(solution)/shard_map/ppermute | solution.py:62
  175.9 23.8 %collective-permute-start.21 = (bf16[144,896]{1,0:T(8,128)(2,1)S(1)}, bf16[144,896]{1,0:T(8,128)(2,1)S(1)}, u32[]{:S(2)}, u32[]{:S(2)}) collective-permute-start(bf16[144,896]{1,0:T(8,128)(2,1)S(1)} %fusion.15.refs_8_), channel_id=1, source_target_pairs={{0,16},{8,24},{16,0},{24,8},{1,17},{9,25},{17,1},{25,9},{2,18},{10... | collective-permute-start | bytes 774152 | tf_op jit(solution)/shard_map/ppermute | solution.py:62
  186.3 13.4 %collective-permute-start.15 = (bf16[144,896]{1,0:T(8,128)(2,1)S(1)}, bf16[144,896]{1,0:T(8,128)(2,1)S(1)}, u32[]{:S(2)}, u32[]{:S(2)}) collective-permute-start(bf16[144,896]{1,0:T(8,128)(2,1)S(1)} %fusion.14.refs_4_), channel_id=1, source_target_pairs={{0,8},{8,0},{16,24},{24,16},{1,9},{9,1},{17,25},{25,17},{2,10},{10... | collective-permute-start | bytes 774152 | tf_op jit(solution)/shard_map/ppermute | solution.py:62
  187.8 11.9 %collective-permute-start.22 = (bf16[144,896]{1,0:T(8,128)(2,1)S(1)}, bf16[144,896]{1,0:T(8,128)(2,1)S(1)}, u32[]{:S(2)}, u32[]{:S(2)}) collective-permute-start(bf16[144,896]{1,0:T(8,128)(2,1)S(1)} %collective-permute-done.20.refs_9_), channel_id=1, source_target_pairs={{0,16},{8,24},{16,0},{24,8},{1,17},{9,25},{17,1},{25,9},{2,18},{10... | collective-permute-start | bytes 774152 | tf_op jit(solution)/shard_map/ppermute | solution.py:62
  255.0 16.2 %collective-permute-start.42 = (bf16[96,1024]{1,0:T(8,128)(2,1)}, bf16[96,1024]{1,0:T(8,128)(2,1)}, u32[]{:S(2)}, u32[]{:S(2)}) collective-permute-start(bf16[96,1024]{1,0:T(8,128)(2,1)} %fusion.19), channel_id=1, source_target_pairs={{0,2},{1,3},{2,6},{3,7},{6,4},{7,5},{4,0},{5,1},{8,10},{9,11},{10,... | collective-permute-start | bytes 589832 | tf_op jit(solution)/shard_map/ppermute | solution.py:66
  261.2 20.6 %collective-permute-start.39 = (bf16[96,1024]{1,0:T(8,128)(2,1)S(1)}, bf16[96,1024]{1,0:T(8,128)(2,1)S(1)}, u32[]{:S(2)}, u32[]{:S(2)}) collective-permute-start(bf16[96,1024]{1,0:T(8,128)(2,1)S(1)} %fusion.18), channel_id=1, source_target_pairs={{0,2},{1,3},{2,6},{3,7},{6,4},{7,5},{4,0},{5,1},{8,10},{9,11},{10,... | collective-permute-start | bytes 589832 | tf_op jit(solution)/shard_map/ppermute | solution.py:66
  272.1 18.3 %collective-permute-start.43 = (bf16[96,1024]{1,0:T(8,128)(2,1)S(1)}, bf16[96,1024]{1,0:T(8,128)(2,1)S(1)}, u32[]{:S(2)}, u32[]{:S(2)}) collective-permute-start(bf16[96,1024]{1,0:T(8,128)(2,1)S(1)} %fusion.10), channel_id=1, source_target_pairs={{0,2},{1,3},{2,6},{3,7},{6,4},{7,5},{4,0},{5,1},{8,10},{9,11},{10,... | collective-permute-start | bytes 589832 | tf_op jit(solution)/shard_map/ppermute | solution.py:66
  281.9 15.8 %collective-permute-start.40 = (bf16[96,1024]{1,0:T(8,128)(2,1)S(1)}, bf16[96,1024]{1,0:T(8,128)(2,1)S(1)}, u32[]{:S(2)}, u32[]{:S(2)}) collective-permute-start(bf16[96,1024]{1,0:T(8,128)(2,1)S(1)} %fusion.13), channel_id=1, source_target_pairs={{0,2},{1,3},{2,6},{3,7},{6,4},{7,5},{4,0},{5,1},{8,10},{9,11},{10,... | collective-permute-start | bytes 589832 | tf_op jit(solution)/shard_map/ppermute | solution.py:66
  290.4 12.7 %collective-permute-start.44 = (bf16[96,1024]{1,0:T(8,128)(2,1)S(1)}, bf16[96,1024]{1,0:T(8,128)(2,1)S(1)}, u32[]{:S(2)}, u32[]{:S(2)}) collective-permute-start(bf16[96,1024]{1,0:T(8,128)(2,1)S(1)} %fusion.9), channel_id=1, source_target_pairs={{0,2},{1,3},{2,6},{3,7},{6,4},{7,5},{4,0},{5,1},{8,10},{9,11},{10,... | collective-permute-start | bytes 589832 | tf_op jit(solution)/shard_map/ppermute | solution.py:66
  (59 other events, 916.9 us)
Sparse Core Ops, SparseCore 0:
  244.8 57.4 all-gather.1

commit v4 on v3

v4 whole, which is shorter than its diff:
```python
import functools

import jax
import jax.numpy as jnp
from jax import lax
from jax.experimental import pallas as pl
from jax.experimental.pallas import tpu as pltpu
from jax.sharding import PartitionSpec as P

BLOCK = 128
BF16 = jnp.bfloat16
F32 = jnp.float32
VMEM_BYTES = 60 * 1024 * 1024
NT = (((1,), (1,)), ((), ()))
NN = (((1,), (0,)), ((), ()))


def params():
    return pltpu.CompilerParams(vmem_limit_bytes=VMEM_BYTES)


def after(x, *others):
    return lax.optimization_barrier((x, *others))[0]


def step_of(hid):
    return 512 if hid % 512 == 0 else 256


def chunk_of(size, most):
    return max(c for c in (128, 256, 512, 1024) if size % c == 0 and c <= most)


def ring_of(chips):
    return [0] + list(range(1, chips, 2)) + [c for c in range(chips - 1, 0, -1) if c % 2 == 0]


class Axes:
    def __init__(self, mesh):
        self.pipe = mesh.shape["pipe"]
        self.tensor = mesh.shape["tensor"]
        self.chips = self.tensor // 2
        self.ring = ring_of(self.chips)

    def slots(self):
        n = self.chips
        table = [[self.ring[(self.ring.index(c) - s) % n] for s in range(n)] for c in range(n)]
        return lax.dynamic_slice(jnp.array(table, jnp.int32), (lax.axis_index("tensor") // 2, 0), (1, n))[0]

    def rows(self, tok):
        chip = self.slots() * 2
        core = (lax.axis_index("tensor") % 2).astype(jnp.int32)
        mine, other = (chip + core) * tok, (chip + 1 - core) * tok
        place = lax.axis_index("pipe").astype(jnp.int32).reshape(1)
        return jnp.concatenate([mine[:1], other[:1], mine[1:], other[1:], place])

    def to_core(self, x):
        return lax.ppermute(x, "tensor", [(t, t ^ 1) for t in range(self.tensor)])

    def to_pipe(self, x, bit):
        return lax.ppermute(x, "pipe", [(i, i ^ bit) for i in range(self.pipe)])

    def to_next(self, x):
        pairs = [(self.ring[i], self.ring[(i + 1) % self.chips]) for i in range(self.chips)]
        return lax.ppermute(x, "tensor", [(2 * a + k, 2 * b + k) for a, b in pairs for k in range(2)])


def reduce_over_pipe(axes, partial):
    place = lax.axis_index("pipe")
    bits = axes.pipe.bit_length() - 1
    rows, cols = partial.shape
    left = partial.reshape((2,) * bits + (rows // axes.pipe, cols))
    for i in range(bits):
        axis = bits - 1 - i
        here = (place >> i) % 2
        send = lax.dynamic_slice_in_dim(left, 1 - here, 1, axis).astype(BF16)
        keep = lax.dynamic_slice_in_dim(left, here, 1, axis)
        left = keep + axes.to_pipe(send, 1 << i).astype(F32)
    held = {0: left.reshape(rows // axes.pipe, cols).astype(BF16)}
    for i in reversed(range(bits)):
        for r in list(held):
            held[r ^ (1 << i)] = axes.to_pipe(held[r], 1 << i)
    return [(held[r], r, 0) for r in range(axes.pipe)]


class Square:
    def __init__(self, axes, partial):
        self.axes, self.partial = axes, partial
        self.part = partial.shape[0] // 4
        self.half = self.part // 2

    def block(self, r, first, count):
        at = ((lax.axis_index("pipe") ^ r) * self.part + first, 0)
        return lax.dynamic_slice(self.partial, at, (count, self.partial.shape[1]))

    def send(self, for_1, for_2, others):
        for_1, for_2 = lax.optimization_barrier((for_1, for_2, *others))[:2] if others else (for_1, for_2)
        return self.axes.to_pipe(for_1, 1), self.axes.to_pipe(for_2, 2)

    def corner(self, others):
        half = self.half
        self.by = self.send(self.block(3, 0, half).astype(BF16), self.block(3, half, half).astype(BF16), others)

    def sides(self, others):
        half = self.half
        by_1, by_2 = [a.astype(F32) for a in self.by]
        for_1 = jnp.concatenate([self.block(1, 0, half), self.block(1, half, half) + by_2], axis=0).astype(BF16)
        for_2 = jnp.concatenate([self.block(2, 0, half) + by_1, self.block(2, half, half)], axis=0).astype(BF16)
        self.terms = self.send(for_1, for_2, others)

    def back(self, others, zero=0.0):
        mine = self.block(0, 0, self.part) + self.terms[0].astype(F32) + self.terms[1].astype(F32)
        self.mine = (mine + zero).astype(BF16)
        self.near = self.send(self.mine, self.mine, others)

    def across(self, others, zero=0.0):
        for_1, for_2 = self.near[1][self.half :], self.near[0][: self.half]
        self.far = self.send(for_1 + jnp.asarray(zero, BF16), for_2 + jnp.asarray(zero, BF16), others)

    def result(self):
        return [
            (self.mine, 0, 0),
            (self.near[0], 1, 0),
            (self.near[1], 2, 0),
            (self.far[1], 3, 0),
            (self.far[0], 3, self.half),
        ]


def mask_kernel(gate, up, gate_m, up_m, out):
    for j, (w, m) in enumerate(((gate, gate_m), (up, up_m))):

        @pl.when(pl.program_id(0) == j)
        def _(w=w, m=m):
            for i in range(out.shape[0] // BLOCK):
                rows = slice(i * BLOCK, (i + 1) * BLOCK)
                out[rows, :] = w[rows, :] * m[i : i + 1, :].astype(BF16)


def masked_pair(gate, up, gate_m, up_m, start, cols, step):
    width = gate.shape[0]
    first, steps = start // step, cols // step
    one = lambda j, k: (0, first + jnp.where(j == 0, k, steps - 1))
    two = lambda j, k: (0, first + jnp.where(j == 0, 0, k))
    return pl.pallas_call(
        mask_kernel,
        out_shape=jax.ShapeDtypeStruct((width, 2 * cols), BF16),
        grid=(2, steps),
        in_specs=[pl.BlockSpec((a.shape[0], step), i) for a, i in ((gate, one), (up, two), (gate_m, one), (up_m, two))],
        out_specs=pl.BlockSpec((width, step), lambda j, k: (0, j * steps + k)),
        compiler_params=params(),
        cost_estimate=pl.CostEstimate(flops=2 * width * cols, bytes_accessed=8 * width * cols, transcendentals=0),
        name="masked_pair",
    )(gate, up, gate_m, up_m)


def sigmoid(g):
    return 0.5 + 0.5 * jnp.tanh(0.5 * g)


def grads_kernel(cfg, at_rows, *refs):
    count = len(cfg["sources"])
    parts = refs[:count]
    gate_pre, up_pre, out, gate_out, up_out, hidden = refs[count:]
    place = at_rows[cfg["groups"]]
    tok = cfg["tok"]

    @pl.when(pl.program_id(1) == 0)
    def _():
        for (r, first), ref in zip(cfg["sources"], parts):
            to = (place ^ r) * cfg["part"] + first
            hidden[pl.ds(pl.multiple_of(to, 16), ref.shape[0]), :] = ref[...]
        for i in range(cfg["groups"]):
            at = pl.ds(pl.multiple_of(at_rows[i], 16), tok)
            g = gate_pre[at, :].astype(F32)
            u = up_pre[at, :].astype(F32)
            h = hidden[i * tok : (i + 1) * tok, :].astype(F32)
            sig = sigmoid(g)
            h = h * sig
            gate = (h * u * (1.0 + g * (1.0 - sig))).astype(BF16)
            out[at, :] = gate
            gate_out[at, :] = gate
            up_out[at, :] = (h * g).astype(BF16)

    @pl.when(pl.program_id(1) == 1)
    def _():
        out[...] = up_out[...]


def local_grads(axes, at_rows, sources, gate_pre, up_pre, tok, start, cols, step):
    tokens = gate_pre.shape[0]
    first, steps = start // step, cols // step
    specs = [pl.BlockSpec((a.shape[0], step), lambda k, j, _: (0, k)) for a, _, _ in sources]
    specs += [pl.BlockSpec((tokens, step), lambda k, j, _: (0, first + k))] * 2
    cfg = dict(sources=[(r, lo) for _, r, lo in sources], part=tokens // axes.pipe, groups=tokens // tok, tok=tok)
    return pl.pallas_call(
        functools.partial(grads_kernel, cfg),
        out_shape=[jax.ShapeDtypeStruct((tokens, n * cols), BF16) for n in (2, 1, 1)],
        grid_spec=pltpu.PrefetchScalarGridSpec(
            num_scalar_prefetch=1,
            grid=(steps, 2),
            in_specs=specs,
            out_specs=[pl.BlockSpec((tokens, step), lambda k, j, _: (0, j * steps + k))]
            + [pl.BlockSpec((tokens, step), lambda k, j, _: (0, k))] * 2,
            scratch_shapes=[pltpu.VMEM((tokens, step), BF16)],
        ),
        compiler_params=params(),
        cost_estimate=pl.CostEstimate(
            flops=20 * tokens * cols, bytes_accessed=10 * tokens * cols, transcendentals=2 * tokens * cols
        ),
        name="local_grads",
    )(at_rows, *[a for a, _, _ in sources], gate_pre, up_pre)


def down_kernel(cfg, at_rows, *refs):
    tokens = refs[:4]
    gate_pre, up_pre, mask = refs[4:7]
    out, done, rows, hidden = refs[-4:]
    tok = cfg["tok"]

    @pl.when(pl.program_id(0) == 0)
    def _():
        done[...] = jnp.zeros_like(done)
        at = 0
        for ref in tokens:
            rows[at : at + ref.shape[0], :] = ref[...]
            at += ref.shape[0]

    for i in range(cfg["groups"]):
        at = pl.ds(pl.multiple_of(at_rows[i], 16), tok)
        g = gate_pre[at, :].astype(F32)
        u = up_pre[at, :].astype(F32)
        hidden[i * tok : (i + 1) * tok, :] = (g * sigmoid(g) * u).astype(BF16)
    across = hidden[...].T
    chunk = cfg["chunk"]

    def tile(n):
        at = pl.ds(pl.multiple_of(n * chunk, chunk), chunk)
        term = lax.dot_general(across, rows[:, at], NN, preferred_element_type=F32)
        for i in range(cfg["step"] // BLOCK):
            part = slice(i * BLOCK, (i + 1) * BLOCK)
            out[part, at] = (term[part, :] * mask[i, :, at]).astype(BF16)

    pl.loop(0, cfg["width"] // chunk)(tile)


def down_grad(at_rows, out_grad, gate_pre, up_pre, mask, tok, before, first, last):
    tokens, hid = gate_pre.shape
    width = out_grad[0].shape[1]
    step = step_of(hid)
    cfg = dict(groups=tokens // tok, tok=tok, width=width, step=step, chunk=chunk_of(width, 1024))
    specs = [pl.BlockSpec(t.shape, lambda k, _: (0, 0), pipeline_mode=pl.Buffered(1)) for t in out_grad]
    specs += [pl.BlockSpec((tokens, step), lambda k, _: (0, first + k))] * 2
    specs += [pl.BlockSpec((step // BLOCK, 1, width), lambda k, _: (first + k, 0, 0))]
    arrays = [*out_grad, gate_pre, up_pre, mask]
    alias = {}
    if before is not None:
        specs.append(pl.BlockSpec(memory_space=pl.ANY))
        arrays.append(before)
        alias = {len(arrays): 0}
    cols = (last - first) * step
    return pl.pallas_call(
        functools.partial(down_kernel, cfg),
        out_shape=[jax.ShapeDtypeStruct((hid, width), BF16), jax.ShapeDtypeStruct((8, 128), F32)],
        grid_spec=pltpu.PrefetchScalarGridSpec(
            num_scalar_prefetch=1,
            grid=(last - first,),
            in_specs=specs,
            out_specs=[
                pl.BlockSpec((step, width), lambda k, _: (first + k, 0)),
                pl.BlockSpec((8, 128), lambda k, _: (0, 0)),
            ],
            scratch_shapes=[pltpu.VMEM((tokens, width), BF16), pltpu.VMEM((tokens, step), BF16)],
        ),
        input_output_aliases=alias,
        compiler_params=params(),
        cost_estimate=pl.CostEstimate(
            flops=2 * tokens * width * cols,
            bytes_accessed=2 * (tokens * width + 2 * tokens * cols + width * cols),
            transcendentals=tokens * cols,
        ),
        name="down_grad",
    )(at_rows, *arrays)


def masked(weight, mask):
    rows, cols = weight.shape
    return (weight.reshape(rows // BLOCK, BLOCK, cols) * mask.astype(BF16)[:, None, :]).reshape(rows, cols)


def dot_nt(a, b):
    return lax.dot_general(a, b, NT, preferred_element_type=F32)


def weight_grad(x, grad, mask):
    tokens, width = x.shape
    blocks = width // BLOCK
    out = lax.dot_general(
        x.reshape(tokens, blocks, BLOCK), grad, (((0,), (0,)), ((), ())), preferred_element_type=F32
    )
    return (out * mask[:, None, :]).astype(BF16).reshape(width, grad.shape[1])


def shards(axes, layer_input, out_grad, gate_pre, up_pre, gate_weight, up_weight, down_weight, gate_mask, up_mask, down_mask):
    tokens, hid = gate_pre.shape
    tok, width = out_grad.shape
    blocks = hid // BLOCK
    third = (blocks + 2) // 3 * BLOCK
    pieces = [(0, third), (third, third), (2 * third, hid - 2 * third)]
    step = 256 if third % 256 == 0 and hid % 256 == 0 else BLOCK
    at_rows = axes.rows(tok)
    gate_m = jnp.repeat(gate_mask, BLOCK, axis=1).astype(F32)
    up_m = jnp.repeat(up_mask, BLOCK, axis=1).astype(F32)
    down_m = jnp.repeat(down_mask, BLOCK, axis=1).astype(F32)

    near = [out_grad, axes.to_core(out_grad)]
    downs = [masked(down_weight[c : c + w], down_m[c // BLOCK : (c + w) // BLOCK]) for c, w in pieces]
    pairs = []
    half = tok // 2
    now, got = [out_grad[:half], out_grad[half:]], []
    for s in range(axes.chips - 1):
        if s and s <= len(pieces):
            now = lax.optimization_barrier((*now, pairs[s - 1]))[:2]
        now = [axes.to_next(a) for a in now]
        if s < len(pieces):
            c, w = pieces[s]
            m = after(gate_m, *got[-2:])
            pairs.append(masked_pair(gate_weight, up_weight, m, up_m, c, w, step))
        got += now
    for c, w in pieces[len(pairs) :]:
        pairs.append(masked_pair(gate_weight, up_weight, gate_m, up_m, c, w, step))
    far = jnp.concatenate(got, axis=0)
    far = [far, axes.to_core(far)]
    rows = after(jnp.concatenate(near + far, axis=0), *pairs)

    parts = [dot_nt(rows, d) for d in downs]
    x = lax.all_gather(after(layer_input, rows), "tensor", axis=0, tiled=True)
    down = functools.partial(down_grad, out_grad=near + far, gate_pre=gate_pre, up_pre=up_pre, mask=down_m[:, None, :], tok=tok)
    steps = hid // step_of(hid)
    if axes.pipe == 4:
        squares = [Square(axes, p) for p in parts]
        for i, sq in enumerate(squares):
            prev = squares[i - 1] if i else None
            sq.corner(prev.by if i else [])
            if not i:
                grad_down, done = down(after(at_rows, *sq.by), before=None, first=0, last=(steps + 1) // 2)
            sq.sides(prev.terms if i else [])
            sq.back(prev.near if i else [], 0.0 if i else done[0, 0])
            if not i:
                grad_down, done = down(after(at_rows, *sq.terms), before=grad_down, first=(steps + 1) // 2, last=steps)
            sq.across(prev.far if i else [], 0.0 if i else done[0, 0])
        sums = [sq.result() for sq in squares]
    else:
        sums = [reduce_over_pipe(axes, p) for p in parts]
        grad_down, _ = down(after(at_rows, *parts), before=None, first=0, last=steps)
    at_rows = at_rows + (x[0, 0].astype(F32) * 0.0).astype(jnp.int32)

    acc, gate_grads, up_grads = None, [], []
    for (c, w), sources, pair in zip(pieces, sums, pairs):
        both, gate, up = local_grads(axes, at_rows, sources, gate_pre, up_pre, tok, c, w, step)
        term = dot_nt(both, pair)
        acc = term if acc is None else acc + term
        acc, at_rows = lax.optimization_barrier((acc, at_rows))
        gate_grads.append(gate)
        up_grads.append(up)

    core = lax.axis_index("tensor") % 2
    slots = axes.slots()
    by_core = acc.reshape(axes.chips, 2, tok, width)
    pick = lambda a, i, axis: lax.dynamic_index_in_dim(a, i, axis, keepdims=False)
    total = pick(by_core, core, 1) + axes.to_core(pick(by_core, 1 - core, 1))
    grad_input = []
    for i in range(2):
        half = total[:, :, i * (width // 2) : (i + 1) * (width // 2)]
        run = pick(half, slots[1 % axes.chips], 0)
        for s in range(1, axes.chips):
            run = axes.to_next(run.astype(BF16)).astype(F32) + pick(half, slots[(s + 1) % axes.chips], 0)
        grad_input.append(run.astype(BF16))
    grad_gate = weight_grad(x, jnp.concatenate(gate_grads, axis=1), gate_m)
    grad_up = weight_grad(x, jnp.concatenate(up_grads, axis=1), up_m)
    return (jnp.concatenate(grad_input, axis=1), grad_gate, grad_up, grad_down)


def solution(mesh):
    in_specs = (
        P("tensor", "pipe"),
        P("tensor", "pipe"),
        P(None, "tensor"),
        P(None, "tensor"),
        P("pipe", "tensor"),
        P("pipe", "tensor"),
        P("tensor", "pipe"),
        P("pipe", "tensor"),
        P("pipe", "tensor"),
        P("tensor", "pipe"),
    )
    out_specs = (P("tensor", "pipe"), P("pipe", "tensor"), P("pipe", "tensor"), P("tensor", "pipe"))
    return jax.shard_map(
        functools.partial(shards, Axes(mesh)), mesh=mesh, in_specs=in_specs, out_specs=out_specs, check_vma=False
    )
```

time: 358 us -> 378 us (1.056)
  Pallas kernels: 40.1 us -> 97.8 us
  waiting for transfers between devices: 88.9 us -> 37.8 us
  local copies, waits for them, and re-layouts: 18 us -> 32.2 us
  starting transfers between devices: 53.3 us -> 47.4 us
    pallas_call x1 -> x5, Pallas kernels: 23.3 us -> 61.4 us  [the longest x3 33.3 us: masked_pair(): pl.pallas_call(mask_kernel, out_shape=jax.ShapeDtypeStruct((width, 2 * co...]
    ppermute x12, waiting for transfers between devices: 48.3 us -> 16.8 us  [to_next(): lax.ppermute(x, 'tensor', [(2 * a + k, 2 * b + k) for a, b in pairs for k...]
    pallas_call x2 -> x3, Pallas kernels: 16.8 us -> 36.4 us  [local_grads(): pl.pallas_call(functools.partial(grads_kernel, cfg), out_shape=[jax.Shape...]
    ppermute x30 -> x24, waiting for transfers between devices: 37.4 us -> 20.9 us  [to_pipe(): return lax.ppermute(x, 'pipe', [(i, i ^ bit) for i in range(self.pipe)])]
    ppermute x30 -> x24, starting transfers between devices: 38.2 us -> 24.7 us  [to_pipe(): return lax.ppermute(x, 'pipe', [(i, i ^ bit) for i in range(self.pipe)])]
    mul x3 -> x2, other arithmetic: 25.4 us -> 13.3 us  [masked(): weight.reshape(rows // BLOCK, BLOCK, cols) * mask.astype(BF16)[:, None, :]]
    ppermute x12, starting transfers between devices: 14.5 us -> 22.7 us  [to_next(): lax.ppermute(x, 'tensor', [(2 * a + k, 2 * b + k) for a, b in pairs for k...]
    convert_element_type x6 -> x3, other arithmetic: 0.27 us -> 5.73 us  [back(): self.mine = (mine + zero).astype(BF16)]
  transfers between devices with their start and end apart: 46 -> 40, of which waited for: 15 -> 15; matrix products, arithmetic and copies ran while one was open for 20% -> 33% of each run, Pallas kernels for 9% -> 23%
where the time goes in v4:
time: 378 us; the launch traced here: 373 us
  Pallas kernels  97.8 us (26%)
  matrix products  95.9 us (25%)
  starting transfers between devices  47.4 us (13%)
  other arithmetic  39 us (10%)
  waiting for transfers between devices  37.8 us (10%)
  local copies, waits for them, and re-layouts  32.2 us (9%)
  between operations  22.7 us (6%)
    dot_general x6, matrix products, dot_nt(): return lax.dot_general(a, b, NT, preferred_element_type=F32)  59.9 us
    pallas_call x3, Pallas kernels, local_grads(): pl.pallas_call(functools.partial(grads_kernel, cfg), out_shape=[jax.Shape...  36.4 us
    dot_general x2, matrix products, weight_grad(): lax.dot_general(x.reshape(tokens, blocks, BLOCK), grad, (((0,), (0,)), ((...  36 us
    pallas_call x3, Pallas kernels, masked_pair(): pl.pallas_call(mask_kernel, out_shape=jax.ShapeDtypeStruct((width, 2 * co...  33.3 us
    pallas_call x2, Pallas kernels, down_grad(): pl.pallas_call(functools.partial(down_kernel, cfg), out_shape=[jax.ShapeD...  28.1 us
    ppermute x24, starting transfers between devices, to_pipe(): return lax.ppermute(x, 'pipe', [(i, i ^ bit) for i in range(self.pipe)])  24.7 us
    ppermute x12, starting transfers between devices, to_next(): lax.ppermute(x, 'tensor', [(2 * a + k, 2 * b + k) for a, b in pairs for k...  22.7 us
    ppermute x24, waiting for transfers between devices, to_pipe(): return lax.ppermute(x, 'pipe', [(i, i ^ bit) for i in range(self.pipe)])  20.9 us
  transfers between devices with their start and end apart: 40, of which 15 were waited for; matrix products, arithmetic and copies ran while one was open for 33% of the time, Pallas kernels for 23%

profile of v4, /device:TPU:0, one launch (start us, length us, event | category | flops | bytes accessed | tf_op | source)
XLA Modules:
  0.0 372.9 jit_solution(3875121373440697417)
XLA Ops:
  8.3 3.1 collective-permute-start.2
  11.3 2.6 collective-permute-start.1
  17.3 11.5 %masked_pair.3 = bf16[2048,2560]{1,0:T(8,128)(2,1)} custom-call(bf16[2048,3584]{1,0:T(8,128)(2,1)} %gate.5, bf16[2048,3584]{1,0:T(8,128)(2,1)} %up.5, f32[16,3584]{1,0:T(8,128)} %bitcast.103, f32[16,3584]{1,0:T(8,128)} %bitcast.99), custom_call_target="tpu_custom_call" | custom-call | flops 5242880 | bytes 20971520 | tf_op jit(solution)/shard_map/masked_pair/pallas_call | solution.py:145
  30.2 11.5 %masked_pair.4 = bf16[2048,2560]{1,0:T(8,128)(2,1)} custom-call(bf16[2048,3584]{1,0:T(8,128)(2,1)} %gate.5, bf16[2048,3584]{1,0:T(8,128)(2,1)} %up.5, f32[16,3584]{1,0:T(8,128)} %bitcast.104, f32[16,3584]{1,0:T(8,128)} %bitcast.100), custom_call_target="tpu_custom_call" | custom-call | flops 5242880 | bytes 20971520 | tf_op jit(solution)/shard_map/masked_pair/pallas_call | solution.py:145
  43.6 2.6 collective-permute-start.6
  51.1 2.8 collective-permute-done.6
  55.5 4.5 %bitcast_multiply_fusion.2 = bf16[1024,2048]{1,0:T(8,128)(2,1)} fusion(bf16[3584,2048]{1,0:T(8,128)(2,1)} %param.18, bf16[8,2048]{1,0:T(8,128)(2,1)S(1)} %broadcast_bitcast_fusion), kind=kLoop, calls=%fused_computation.14 | loop fusion | flops 2097152 | bytes 8421376 | tf_op jit(solution)/shard_map/mul | solution.py:288
  60.0 8.8 %bitcast_multiply_fusion = (bf16[1280,2048]{1,0:T(8,128)(2,1)}, bf16[1280,2048]{1,0:T(8,128)(2,1)}) fusion(bf16[3584,2048]{1,0:T(8,128)(2,1)} %param.18, bf16[10,2048]{1,0:T(8,128)(2,1)S(1)} %bitcast.114, bf16[10,2048]{1,0:T(8,128)(2,1)S(1)} %bitcast.113), kind=kLoop, calls=%fused_computation.12 | loop fusion | flops 5242880 | bytes 21053440 | tf_op jit(solution)/shard_map/mul | solution.py:288
  70.7 10.3 %masked_pair.5 = bf16[2048,2048]{1,0:T(8,128)(2,1)} custom-call(bf16[2048,3584]{1,0:T(8,128)(2,1)} %gate.5, bf16[2048,3584]{1,0:T(8,128)(2,1)} %up.5, f32[16,3584]{1,0:T(8,128)} %bitcast.105, f32[16,3584]{1,0:T(8,128)} %bitcast.101), custom_call_target="tpu_custom_call" | custom-call | flops 4194304 | bytes 16777216 | tf_op jit(solution)/shard_map/masked_pair/pallas_call | solution.py:145
  82.1 10.5 %fusion.25 = f32[768,1280]{1,0:T(8,128)} fusion(bf16[768,2048]{1,0:T(8,128)(2,1)} %constant_dynamic-update-slice_fusion.6, bf16[1280,2048]{1,0:T(8,128)(2,1)} %get-tuple-element.92), kind=kOutput, calls=%fused_computation.99 | convolution fusion | flops 4026531840 | bytes 12320768 | tf_op jit(solution)/shard_map/dot_general | solution.py:292
  92.6 6.2 %fusion.23 = f32[768,1280]{1,0:T(8,128)} fusion(bf16[768,2048]{1,0:T(8,128)(2,1)S(1)} %copy-done.24, bf16[1280,2048]{1,0:T(8,128)(2,1)S(1)} %bitcast.98), kind=kOutput, calls=%fused_computation.97 | convolution fusion | flops 4026531840 | bytes 12320768 | tf_op jit(solution)/shard_map/dot_general | solution.py:292
  98.8 3.5 fusion.26
  110.6 2.9 collective-permute-done.10
  122.6 15.6 %down_grad.2 = (bf16[3584,2048]{1,0:T(8,128)(2,1)}, f32[8,128]{1,0:T(8,128)}) custom-call(s32[9]{0:T(128)} %concatenate.43.at_rows, bf16[96,2048]{1,0:T(8,128)(2,1)} %refs_0_.3, bf16[96,2048]{1,0:T(8,128)(2,1)} %copy-done.11, bf16[288,2048]{1,0:T(8,128)(2,1)} %copy-done.10, bf16[288,2048]{1,0:T(8,128)(2,1)} %copy-done.1, bf16[768,3584]{1,0:T(8,128)(2,1)} %refs_5_.9, ...), custom_call_target="tpu_custom_call" | custom-call | flops 6442450944 | bytes 17825792 | tf_op jit(solution)/shard_map/down_grad/pallas_call | solution.py:262
  150.1 3.1 add_convert_fusion.1.refs_0_
  156.3 12.5 %down_grad.3 = (bf16[3584,2048]{1,0:T(8,128)(2,1)}, f32[8,128]{1,0:T(8,128)}) custom-call(s32[9]{0:T(128)} %concatenate.43.at_rows, bf16[96,2048]{1,0:T(8,128)(2,1)} %refs_0_.3, bf16[96,2048]{1,0:T(8,128)(2,1)} %copy-done.11, bf16[288,2048]{1,0:T(8,128)(2,1)} %copy-done.10, bf16[288,2048]{1,0:T(8,128)(2,1)} %copy-done.1, ...), custom_call_target="tpu_custom_call", output_to_operand_aliasing={{0}: (8, {})} | custom-call | flops 4831838208 | bytes 14155776 | tf_op jit(solution)/shard_map/down_grad/pallas_call | solution.py:262
  179.3 3.0 collective-permute-done.26
  184.1 8.7 %collective-permute-done.20.refs_1_ = bf16[192,1280]{1,0:T(8,128)(2,1)S(1)} collective-permute-done((bf16[192,1280]{1,0:T(8,128)(2,1)S(1)}, bf16[192,1280]{1,0:T(8,128)(2,1)S(1)}, u32[]{:S(2)}, u32[]{:S(2)}) %collective-permute-start.20) | collective-permute-done | bytes 491552 | tf_op jit(solution)/shard_map/ppermute | solution.py:61
  214.5 12.9 %local_grads.3 = (bf16[768,2560]{1,0:T(8,128)(2,1)}, bf16[768,1280]{1,0:T(8,128)(2,1)}, bf16[768,1280]{1,0:T(8,128)(2,1)}) custom-call(s32[9]{0:T(128)} %broadcast_add_fusion.at_rows, bf16[192,1280]{1,0:T(8,128)(2,1)} %add_convert_fusion.1.refs_0_, bf16[192,1280]{1,0:T(8,128)(2,1)} %collective-permute-done.12.refs_1_, ...), custom_call_target="tpu_custom_call" | custom-call | flops 19660800 | bytes 9830400 | tf_op jit(solution)/shard_map/local_grads/pallas_call | solution.py:196
  227.4 14.0 %fusion.24 = f32[768,2048]{1,0:T(8,128)} fusion(bf16[768,2560]{1,0:T(8,128)(2,1)} %get-tuple-element.61, bf16[2048,2560]{1,0:T(8,128)(2,1)} %masked_pair.3), kind=kOutput, calls=%fused_computation.98 | convolution fusion | flops 8053063680 | bytes 20709376 | tf_op jit(solution)/shard_map/dot_general | solution.py:292
  241.4 12.9 %local_grads.4 = (bf16[768,2560]{1,0:T(8,128)(2,1)}, bf16[768,1280]{1,0:T(8,128)(2,1)}, bf16[768,1280]{1,0:T(8,128)(2,1)}) custom-call(s32[9]{0:T(128)} %broadcast_add_fusion.at_rows, bf16[192,1280]{1,0:T(8,128)(2,1)} %copy-done.8, bf16[192,1280]{1,0:T(8,128)(2,1)} %copy-done.13, bf16[192,1280]{1,0:T(8,128)(2,1)} %copy-done.14, bf16[96,1280]{1,0:T(8,128)(2,1)} %copy-done.20, ...), custom_call_target="tpu_custom_call" | custom-call | flops 19660800 | bytes 9830400 | tf_op jit(solution)/shard_map/local_grads/pallas_call | solution.py:196
  254.2 14.8 %convolution_add_fusion.1 = f32[768,2048]{1,0:T(8,128)} fusion(f32[768,2048]{1,0:T(8,128)} %fusion.24, bf16[768,2560]{1,0:T(8,128)(2,1)} %get-tuple-element.72, bf16[2048,2560]{1,0:T(8,128)(2,1)} %masked_pair.4), kind=kOutput, calls=%fused_computation.16 | convolution fusion | flops 8054636544 | bytes 27000832 | tf_op jit(solution)/shard_map/dot_general | solution.py:292
  270.4 10.7 %local_grads.5 = (bf16[768,2048]{1,0:T(8,128)(2,1)}, bf16[768,1024]{1,0:T(8,128)(2,1)}, bf16[768,1024]{1,0:T(8,128)(2,1)}) custom-call(s32[9]{0:T(128)} %broadcast_add_fusion.at_rows, bf16[192,1024]{1,0:T(8,128)(2,1)} %copy-done.12, bf16[192,1024]{1,0:T(8,128)(2,1)} %copy-done.15, bf16[192,1024]{1,0:T(8,128)(2,1)} %copy-done.16, ...), custom_call_target="tpu_custom_call" | custom-call | flops 15728640 | bytes 7864320 | tf_op jit(solution)/shard_map/local_grads/pallas_call | solution.py:196
  281.1 11.0 %convolution_add_fusion = f32[768,2048]{1,0:T(8,128)S(1)} fusion(f32[768,2048]{1,0:T(8,128)} %convolution_add_fusion.1, bf16[768,2048]{1,0:T(8,128)(2,1)} %get-tuple-element.83, bf16[2048,2048]{1,0:T(8,128)(2,1)} %masked_pair.5), kind=kOutput, calls=%fused_computation.15 | convolution fusion | flops 6444023808 | bytes 24117248 | tf_op jit(solution)/shard_map/dot_general | solution.py:292
  296.3 2.8 copy.24
  299.2 17.9 %multiply_convert_fusion.1 = bf16[16,128,3584]{2,1,0:T(8,128)(2,1)} fusion(f32[16,3584]{1,0:T(8,128)S(1)} %bitcast.106, bf16[768,16,128]{0,2,1:T(8,128)(2,1)} %bitcast.107, bf16[768,1024]{1,0:T(8,128)(2,1)} %get-tuple-element.87, bf16[768,1280]{1,0:T(8,128)(2,1)} %get-tuple-element.86, bf16[768,1280]{1,0:T(8,128)(2,1)} %get-tuple-element.85), kind=kOutput, calls=%fused_computation.1 | convolution fusion | flops 11305484288 | bytes 23560192 | tf_op jit(solution)/shard_map/dot_general | solution.py:298
  317.1 3.5 bitcast_add_fusion
  321.9 18.2 %multiply_convert_fusion = bf16[16,128,3584]{2,1,0:T(8,128)(2,1)} fusion(f32[16,3584]{1,0:T(8,128)S(1)} %bitcast.102, bf16[768,16,128]{0,2,1:T(8,128)(2,1)} %bitcast.108, bf16[768,1024]{1,0:T(8,128)(2,1)} %get-tuple-element.90, bf16[768,1280]{1,0:T(8,128)(2,1)} %get-tuple-element.89, bf16[768,1280]{1,0:T(8,128)(2,1)} %get-tuple-element.88), kind=kOutput, calls=%fused_computation | convolution fusion | flops 11305484288 | bytes 23560192 | tf_op jit(solution)/shard_map/dot_general | solution.py:298
  340.1 3.4 collective-permute-start.33
  344.1 4.7 %collective-permute-done.33 = bf16[96,1024]{1,0:T(8,128)(2,1)S(1)} collective-permute-done((bf16[96,1024]{1,0:T(8,128)(2,1)S(1)}, bf16[96,1024]{1,0:T(8,128)(2,1)S(1)}, u32[]{:S(2)}, u32[]{:S(2)}) %collective-permute-start.33) | collective-permute-done | bytes 196640 | tf_op jit(solution)/shard_map/ppermute | solution.py:65
  348.8 2.5 collective-permute-start.34
  361.9 3.1 collective-permute-done.35
  (199 shorter events, 94.3 us)
Async XLA Ops:
  7.2 205.1 %all-gather.2.cloned.1.call-start = ((), (), s32[]{:S(2)}) async-start(), calls=%async_computation | async-start | bytes 3538944 | tf_op jit(solution)/shard_map/all_gather | solution.py:337
  8.3 20.5 %collective-permute-start.2 = (bf16[48,2048]{1,0:T(8,128)(2,1)S(1)}, bf16[48,2048]{1,0:T(8,128)(2,1)S(1)}, u32[]{:S(2)}, u32[]{:S(2)}) collective-permute-start(bf16[48,2048]{1,0:T(8,128)(2,1)S(1)} %get-tuple-element.114), channel_id=1, source_target_pairs={{0,2},{1,3},{2,6},{3,7},{6,4},{7,5},{4,0},{5,1},{8,10},{9,11},{10,... | collective-permute-start | bytes 589832 | tf_op jit(solution)/shard_map/ppermute | solution.py:65
  11.3 17.5 %collective-permute-start.1 = (bf16[48,2048]{1,0:T(8,128)(2,1)S(1)}, bf16[48,2048]{1,0:T(8,128)(2,1)S(1)}, u32[]{:S(2)}, u32[]{:S(2)}) collective-permute-start(bf16[48,2048]{1,0:T(8,128)(2,1)S(1)} %get-tuple-element.115), channel_id=1, source_target_pairs={{0,2},{1,3},{2,6},{3,7},{6,4},{7,5},{4,0},{5,1},{8,10},{9,11},{10,... | collective-permute-start | bytes 589832 | tf_op jit(solution)/shard_map/ppermute | solution.py:65
  13.9 32.3 %collective-permute-start = (bf16[96,2048]{1,0:T(8,128)(2,1)}, bf16[96,2048]{1,0:T(8,128)(2,1)S(1)}, u32[]{:S(2)}, u32[]{:S(2)}) collective-permute-start(bf16[96,2048]{1,0:T(8,128)(2,1)} %refs_0_.3), channel_id=1, source_target_pairs={{0,1},{1,0},{2,3},{3,2},{4,5},{5,4},{6,7},{7,6},{8,9},{9,8},{10,11... | collective-permute-start | bytes 1179656 | tf_op jit(solution)/shard_map/ppermute | solution.py:58
  28.8 12.9 %collective-permute-start.3 = (bf16[48,2048]{1,0:T(8,128)(2,1)S(1)}, bf16[48,2048]{1,0:T(8,128)(2,1)S(1)}, u32[]{:S(2)}, u32[]{:S(2)}) collective-permute-start(bf16[48,2048]{1,0:T(8,128)(2,1)S(1)} %collective-permute-done.1), channel_id=1, source_target_pairs={{0,2},{1,3},{2,6},{3,7},{6,4},{7,5},{4,0},{5,1},{8,10},{9,11},{10,... | collective-permute-start | bytes 589832 | tf_op jit(solution)/shard_map/ppermute | solution.py:65
  29.3 12.4 %collective-permute-start.4 = (bf16[48,2048]{1,0:T(8,128)(2,1)S(1)}, bf16[48,2048]{1,0:T(8,128)(2,1)S(1)}, u32[]{:S(2)}, u32[]{:S(2)}) collective-permute-start(bf16[48,2048]{1,0:T(8,128)(2,1)S(1)} %collective-permute-done.2), channel_id=1, source_target_pairs={{0,2},{1,3},{2,6},{3,7},{6,4},{7,5},{4,0},{5,1},{8,10},{9,11},{10,... | collective-permute-start | bytes 589832 | tf_op jit(solution)/shard_map/ppermute | solution.py:65
  43.6 10.3 %collective-permute-start.6 = (bf16[48,2048]{1,0:T(8,128)(2,1)S(1)}, bf16[48,2048]{1,0:T(8,128)(2,1)S(1)}, u32[]{:S(2)}, u32[]{:S(2)}) collective-permute-start(bf16[48,2048]{1,0:T(8,128)(2,1)S(1)} %collective-permute-done.4), channel_id=1, source_target_pairs={{0,2},{1,3},{2,6},{3,7},{6,4},{7,5},{4,0},{5,1},{8,10},{9,11},{10,... | collective-permute-start | bytes 589832 | tf_op jit(solution)/shard_map/ppermute | solution.py:65
  54.6 26.3 %collective-permute-start.7 = (bf16[288,2048]{1,0:T(8,128)(2,1)S(1)}, bf16[288,2048]{1,0:T(8,128)(2,1)S(1)}, u32[]{:S(2)}, u32[]{:S(2)}) collective-permute-start(bf16[288,2048]{1,0:T(8,128)(2,1)S(1)} %get-tuple-element.116.refs_2_), channel_id=1, source_target_pairs={{0,1},{1,0},{2,3},{3,2},{4,5},{5,4},{6,7},{7,6},{8,9},{9,8},{10,11... | collective-permute-start | bytes 3538952 | tf_op jit(solution)/shard_map/ppermute | solution.py:58
  116.8 32.2 %collective-permute-start.11 = (bf16[192,1280]{1,0:T(8,128)(2,1)}, bf16[192,1280]{1,0:T(8,128)(2,1)}, u32[]{:S(2)}, u32[]{:S(2)}) collective-permute-start(bf16[192,1280]{1,0:T(8,128)(2,1)} %pad_maximum_fusion.1), channel_id=1, source_target_pairs={{0,16},{8,24},{16,0},{24,8},{1,17},{9,25},{17,1},{25,9},{2,18},{10... | collective-permute-start | bytes 1474568 | tf_op jit(solution)/shard_map/ppermute | solution.py:61
  119.2 29.9 %collective-permute-start.9 = (bf16[192,1280]{1,0:T(8,128)(2,1)}, bf16[192,1280]{1,0:T(8,128)(2,1)}, u32[]{:S(2)}, u32[]{:S(2)}) collective-permute-start(bf16[192,1280]{1,0:T(8,128)(2,1)} %pad_maximum_fusion), channel_id=1, source_target_pairs={{0,8},{8,0},{16,24},{24,16},{1,9},{9,1},{17,25},{25,17},{2,10},{10... | collective-permute-start | bytes 1474568 | tf_op jit(solution)/shard_map/ppermute | solution.py:61
  119.7 19.7 %collective-permute-start.16 = (bf16[96,1280]{1,0:T(8,128)(2,1)}, bf16[96,1280]{1,0:T(8,128)(2,1)}, u32[]{:S(2)}, u32[]{:S(2)}) collective-permute-start(bf16[96,1280]{1,0:T(8,128)(2,1)} %get-tuple-element.64), channel_id=1, source_target_pairs={{0,16},{8,24},{16,0},{24,8},{1,17},{9,25},{17,1},{25,9},{2,18},{10... | collective-permute-start | bytes 737288 | tf_op jit(solution)/shard_map/ppermute | solution.py:61
  120.3 19.2 %collective-permute-start.17 = (bf16[96,1280]{1,0:T(8,128)(2,1)}, bf16[96,1280]{1,0:T(8,128)(2,1)}, u32[]{:S(2)}, u32[]{:S(2)}) collective-permute-start(bf16[96,1280]{1,0:T(8,128)(2,1)} %get-tuple-element.65), channel_id=1, source_target_pairs={{0,8},{8,0},{16,24},{24,16},{1,9},{9,1},{17,25},{25,17},{2,10},{10... | collective-permute-start | bytes 737288 | tf_op jit(solution)/shard_map/ppermute | solution.py:61
  149.1 20.8 %collective-permute-start.18 = (bf16[192,1280]{1,0:T(8,128)(2,1)}, bf16[192,1280]{1,0:T(8,128)(2,1)}, u32[]{:S(2)}, u32[]{:S(2)}) collective-permute-start(bf16[192,1280]{1,0:T(8,128)(2,1)} %get-tuple-element.66), channel_id=1, source_target_pairs={{0,8},{8,0},{16,24},{24,16},{1,9},{9,1},{17,25},{25,17},{2,10},{10... | collective-permute-start | bytes 1474568 | tf_op jit(solution)/shard_map/ppermute | solution.py:61
  149.6 20.3 %collective-permute-start.19 = (bf16[192,1280]{1,0:T(8,128)(2,1)}, bf16[192,1280]{1,0:T(8,128)(2,1)}, u32[]{:S(2)}, u32[]{:S(2)}) collective-permute-start(bf16[192,1280]{1,0:T(8,128)(2,1)} %get-tuple-element.67), channel_id=1, source_target_pairs={{0,16},{8,24},{16,0},{24,8},{1,17},{9,25},{17,1},{25,9},{2,18},{10... | collective-permute-start | bytes 1474568 | tf_op jit(solution)/shard_map/ppermute | solution.py:61
  153.2 19.1 %collective-permute-start.13 = (bf16[192,1280]{1,0:T(8,128)(2,1)}, bf16[192,1280]{1,0:T(8,128)(2,1)}, u32[]{:S(2)}, u32[]{:S(2)}) collective-permute-start(bf16[192,1280]{1,0:T(8,128)(2,1)} %add_convert_fusion.1.refs_0_), channel_id=1, source_target_pairs={{0,16},{8,24},{16,0},{24,8},{1,17},{9,25},{17,1},{25,9},{2,18},{10... | collective-permute-start | bytes 1474568 | tf_op jit(solution)/shard_map/ppermute | solution.py:61
  154.7 17.6 %collective-permute-start.12 = (bf16[192,1280]{1,0:T(8,128)(2,1)}, bf16[192,1280]{1,0:T(8,128)(2,1)}, u32[]{:S(2)}, u32[]{:S(2)}) collective-permute-start(bf16[192,1280]{1,0:T(8,128)(2,1)} %add_convert_fusion.1.refs_0_), channel_id=1, source_target_pairs={{0,8},{8,0},{16,24},{24,16},{1,9},{9,1},{17,25},{25,17},{2,10},{10... | collective-permute-start | bytes 1474568 | tf_op jit(solution)/shard_map/ppermute | solution.py:61
  169.9 12.3 %collective-permute-start.26 = (bf16[192,1024]{1,0:T(8,128)(2,1)}, bf16[192,1024]{1,0:T(8,128)(2,1)S(1)}, u32[]{:S(2)}, u32[]{:S(2)}) collective-permute-start(bf16[192,1024]{1,0:T(8,128)(2,1)} %get-tuple-element.77), channel_id=1, source_target_pairs={{0,8},{8,0},{16,24},{24,16},{1,9},{9,1},{17,25},{25,17},{2,10},{10... | collective-permute-start | bytes 1179656 | tf_op jit(solution)/shard_map/ppermute | solution.py:61
  170.5 12.3 %collective-permute-start.27 = (bf16[192,1024]{1,0:T(8,128)(2,1)}, bf16[192,1024]{1,0:T(8,128)(2,1)S(1)}, u32[]{:S(2)}, u32[]{:S(2)}) collective-permute-start(bf16[192,1024]{1,0:T(8,128)(2,1)} %get-tuple-element.78), channel_id=1, source_target_pairs={{0,16},{8,24},{16,0},{24,8},{1,17},{9,25},{17,1},{25,9},{2,18},{10... | collective-permute-start | bytes 1179656 | tf_op jit(solution)/shard_map/ppermute | solution.py:61
  172.4 20.4 %collective-permute-start.20 = (bf16[192,1280]{1,0:T(8,128)(2,1)S(1)}, bf16[192,1280]{1,0:T(8,128)(2,1)S(1)}, u32[]{:S(2)}, u32[]{:S(2)}) collective-permute-start(bf16[192,1280]{1,0:T(8,128)(2,1)S(1)} %add_convert_fusion.refs_0_), channel_id=1, source_target_pairs={{0,8},{8,0},{16,24},{24,16},{1,9},{9,1},{17,25},{25,17},{2,10},{10... | collective-permute-start | bytes 1474568 | tf_op jit(solution)/shard_map/ppermute | solution.py:61
  174.0 19.4 %collective-permute-start.21 = (bf16[192,1280]{1,0:T(8,128)(2,1)S(1)}, bf16[192,1280]{1,0:T(8,128)(2,1)S(1)}, u32[]{:S(2)}, u32[]{:S(2)}) collective-permute-start(bf16[192,1280]{1,0:T(8,128)(2,1)S(1)} %add_convert_fusion.refs_0_), channel_id=1, source_target_pairs={{0,16},{8,24},{16,0},{24,8},{1,17},{9,25},{17,1},{25,9},{2,18},{10... | collective-permute-start | bytes 1474568 | tf_op jit(solution)/shard_map/ppermute | solution.py:61
  177.1 21.5 %collective-permute-start.14 = (bf16[96,1280]{1,0:T(8,128)(2,1)S(1)}, bf16[96,1280]{1,0:T(8,128)(2,1)S(1)}, u32[]{:S(2)}, u32[]{:S(2)}) collective-permute-start(bf16[96,1280]{1,0:T(8,128)(2,1)S(1)} %slice_add_fusion.1), channel_id=1, source_target_pairs={{0,16},{8,24},{16,0},{24,8},{1,17},{9,25},{17,1},{25,9},{2,18},{10... | collective-permute-start | bytes 737288 | tf_op jit(solution)/shard_map/ppermute | solution.py:61
  182.3 16.3 %collective-permute-start.15 = (bf16[96,1280]{1,0:T(8,128)(2,1)S(1)}, bf16[96,1280]{1,0:T(8,128)(2,1)S(1)}, u32[]{:S(2)}, u32[]{:S(2)}) collective-permute-start(bf16[96,1280]{1,0:T(8,128)(2,1)S(1)} %slice_add_fusion), channel_id=1, source_target_pairs={{0,8},{8,0},{16,24},{24,16},{1,9},{9,1},{17,25},{25,17},{2,10},{10... | collective-permute-start | bytes 737288 | tf_op jit(solution)/shard_map/ppermute | solution.py:61
  193.3 15.3 %collective-permute-start.28 = (bf16[192,1024]{1,0:T(8,128)(2,1)S(1)}, bf16[192,1024]{1,0:T(8,128)(2,1)S(1)}, u32[]{:S(2)}, u32[]{:S(2)}) collective-permute-start(bf16[192,1024]{1,0:T(8,128)(2,1)S(1)} %add_convert_fusion.2.refs_0_), channel_id=1, source_target_pairs={{0,8},{8,0},{16,24},{24,16},{1,9},{9,1},{17,25},{25,17},{2,10},{10... | collective-permute-start | bytes 1179656 | tf_op jit(solution)/shard_map/ppermute | solution.py:61
  194.8 14.6 %collective-permute-start.29 = (bf16[192,1024]{1,0:T(8,128)(2,1)S(1)}, bf16[192,1024]{1,0:T(8,128)(2,1)S(1)}, u32[]{:S(2)}, u32[]{:S(2)}) collective-permute-start(bf16[192,1024]{1,0:T(8,128)(2,1)S(1)} %add_convert_fusion.2.refs_0_), channel_id=1, source_target_pairs={{0,16},{8,24},{16,0},{24,8},{1,17},{9,25},{17,1},{25,9},{2,18},{10... | collective-permute-start | bytes 1179656 | tf_op jit(solution)/shard_map/ppermute | solution.py:61
  198.6 11.5 %collective-permute-start.22 = (bf16[96,1280]{1,0:T(8,128)(2,1)}, bf16[96,1280]{1,0:T(8,128)(2,1)S(1)}, u32[]{:S(2)}, u32[]{:S(2)}) collective-permute-start(bf16[96,1280]{1,0:T(8,128)(2,1)} %slice.148), channel_id=1, source_target_pairs={{0,16},{8,24},{16,0},{24,8},{1,17},{9,25},{17,1},{25,9},{2,18},{10... | collective-permute-start | bytes 737288 | tf_op jit(solution)/shard_map/ppermute | solution.py:61
  199.2 11.0 %collective-permute-start.23 = (bf16[96,1280]{1,0:T(8,128)(2,1)S(1)}, bf16[96,1280]{1,0:T(8,128)(2,1)S(1)}, u32[]{:S(2)}, u32[]{:S(2)}) collective-permute-start(bf16[96,1280]{1,0:T(8,128)(2,1)S(1)} %slice.147), channel_id=1, source_target_pairs={{0,8},{8,0},{16,24},{24,16},{1,9},{9,1},{17,25},{25,17},{2,10},{10... | collective-permute-start | bytes 737288 | tf_op jit(solution)/shard_map/ppermute | solution.py:61
  210.2 58.9 %collective-permute-start.30 = (bf16[96,1024]{1,0:T(8,128)(2,1)}, bf16[96,1024]{1,0:T(8,128)(2,1)S(1)}, u32[]{:S(2)}, u32[]{:S(2)}) collective-permute-start(bf16[96,1024]{1,0:T(8,128)(2,1)} %slice.151), channel_id=1, source_target_pairs={{0,16},{8,24},{16,0},{24,8},{1,17},{9,25},{17,1},{25,9},{2,18},{10... | collective-permute-start | bytes 589832 | tf_op jit(solution)/shard_map/ppermute | solution.py:61
  211.7 57.3 %collective-permute-start.31 = (bf16[96,1024]{1,0:T(8,128)(2,1)}, bf16[96,1024]{1,0:T(8,128)(2,1)S(1)}, u32[]{:S(2)}, u32[]{:S(2)}) collective-permute-start(bf16[96,1024]{1,0:T(8,128)(2,1)} %slice.150), channel_id=1, source_target_pairs={{0,8},{8,0},{16,24},{24,16},{1,9},{9,1},{17,25},{25,17},{2,10},{10... | collective-permute-start | bytes 589832 | tf_op jit(solution)/shard_map/ppermute | solution.py:61
  296.3 20.7 %collective-permute-start.32 = (f32[4,96,2048]{2,1,0:T(8,128)}, f32[4,96,2048]{2,1,0:T(8,128)}, u32[]{:S(2)}, u32[]{:S(2)}) collective-permute-start(f32[4,96,2048]{2,1,0:T(8,128)} %dynamic-slice_bitcast_fusion), channel_id=1, source_target_pairs={{0,1},{1,0},{2,3},{3,2},{4,5},{5,4},{6,7},{7,6},{8,9},{9,8},{10,11... | collective-permute-start | bytes 9437192 | tf_op jit(solution)/shard_map/ppermute | solution.py:58
  321.1 22.5 %collective-permute-start.36 = (bf16[96,1024]{1,0:T(8,128)(2,1)S(1)}, bf16[96,1024]{1,0:T(8,128)(2,1)S(1)}, u32[]{:S(2)}, u32[]{:S(2)}) collective-permute-start(bf16[96,1024]{1,0:T(8,128)(2,1)S(1)} %fusion.15), channel_id=1, source_target_pairs={{0,2},{1,3},{2,6},{3,7},{6,4},{7,5},{4,0},{5,1},{8,10},{9,11},{10,... | collective-permute-start | bytes 589832 | tf_op jit(solution)/shard_map/ppermute | solution.py:65
  343.6 9.4 %collective-permute-start.37 = (bf16[96,1024]{1,0:T(8,128)(2,1)S(1)}, bf16[96,1024]{1,0:T(8,128)(2,1)S(1)}, u32[]{:S(2)}, u32[]{:S(2)}) collective-permute-start(bf16[96,1024]{1,0:T(8,128)(2,1)S(1)} %fusion.10), channel_id=1, source_target_pairs={{0,2},{1,3},{2,6},{3,7},{6,4},{7,5},{4,0},{5,1},{8,10},{9,11},{10,... | collective-permute-start | bytes 589832 | tf_op jit(solution)/shard_map/ppermute | solution.py:65
  348.8 8.8 %collective-permute-start.34 = (bf16[96,1024]{1,0:T(8,128)(2,1)S(1)}, bf16[96,1024]{1,0:T(8,128)(2,1)S(1)}, u32[]{:S(2)}, u32[]{:S(2)}) collective-permute-start(bf16[96,1024]{1,0:T(8,128)(2,1)S(1)} %fusion.13), channel_id=1, source_target_pairs={{0,2},{1,3},{2,6},{3,7},{6,4},{7,5},{4,0},{5,1},{8,10},{9,11},{10,... | collective-permute-start | bytes 589832 | tf_op jit(solution)/shard_map/ppermute | solution.py:65
  (38 other events, 498.6 us)
Sparse Core Ops, SparseCore 0:
  102.4 39.6 all-gather.1

commit v5 on v4

v5 whole, which is shorter than its diff:
```python
import functools

import jax
import jax.numpy as jnp
from jax import lax
from jax.experimental import pallas as pl
from jax.experimental.pallas import tpu as pltpu
from jax.sharding import PartitionSpec as P

BLOCK = 128
BF16 = jnp.bfloat16
F32 = jnp.float32
VMEM_BYTES = 60 * 1024 * 1024
NT = (((1,), (1,)), ((), ()))
NN = (((1,), (0,)), ((), ()))


def params():
    return pltpu.CompilerParams(vmem_limit_bytes=VMEM_BYTES)


def after(x, *others):
    return lax.optimization_barrier((x, *others))[0]


def nothing(x):
    return x[(0,) * x.ndim].astype(F32) * 0.0


def step_of(hid):
    return 512 if hid % 512 == 0 else 256


def chunk_of(size, most):
    return max(c for c in (128, 256, 512, 1024) if size % c == 0 and c <= most)


def ring_of(chips):
    return [0] + list(range(1, chips, 2)) + [c for c in range(chips - 1, 0, -1) if c % 2 == 0]


class Axes:
    def __init__(self, mesh):
        self.pipe = mesh.shape["pipe"]
        self.tensor = mesh.shape["tensor"]
        self.chips = self.tensor // 2
        self.ring = ring_of(self.chips)

    def slots(self):
        n = self.chips
        table = [[self.ring[(self.ring.index(c) - s) % n] for s in range(n)] for c in range(n)]
        return lax.dynamic_slice(jnp.array(table, jnp.int32), (lax.axis_index("tensor") // 2, 0), (1, n))[0]

    def rows(self, tok):
        chip = self.slots() * 2
        core = (lax.axis_index("tensor") % 2).astype(jnp.int32)
        mine, other = (chip + core) * tok, (chip + 1 - core) * tok
        place = lax.axis_index("pipe").astype(jnp.int32).reshape(1)
        return jnp.concatenate([mine[:1], other[:1], mine[1:], other[1:], place])

    def to_core(self, x):
        return lax.ppermute(x, "tensor", [(t, t ^ 1) for t in range(self.tensor)])

    def to_pipe(self, x, bit):
        return lax.ppermute(x, "pipe", [(i, i ^ bit) for i in range(self.pipe)])

    def to_next(self, x):
        pairs = [(self.ring[i], self.ring[(i + 1) % self.chips]) for i in range(self.chips)]
        return lax.ppermute(x, "tensor", [(2 * a + k, 2 * b + k) for a, b in pairs for k in range(2)])


def reduce_over_pipe(axes, partial):
    place = lax.axis_index("pipe")
    bits = axes.pipe.bit_length() - 1
    rows, cols = partial.shape
    left = partial.reshape((2,) * bits + (rows // axes.pipe, cols))
    for i in range(bits):
        axis = bits - 1 - i
        here = (place >> i) % 2
        send = lax.dynamic_slice_in_dim(left, 1 - here, 1, axis).astype(BF16)
        keep = lax.dynamic_slice_in_dim(left, here, 1, axis)
        left = keep + axes.to_pipe(send, 1 << i).astype(F32)
    held = {0: left.reshape(rows // axes.pipe, cols).astype(BF16)}
    for i in reversed(range(bits)):
        for r in list(held):
            held[r ^ (1 << i)] = axes.to_pipe(held[r], 1 << i)
    return [(held[r], r, 0) for r in range(axes.pipe)]


class Square:
    def __init__(self, axes, partial):
        self.axes, self.partial = axes, partial
        self.part = partial.shape[0] // 4
        self.half = self.part // 2

    def block(self, r, first, count):
        at = ((lax.axis_index("pipe") ^ r) * self.part + first, 0)
        return lax.dynamic_slice(self.partial, at, (count, self.partial.shape[1]))

    def send(self, for_1, for_2, others):
        for_1, for_2 = lax.optimization_barrier((for_1, for_2, *others))[:2] if others else (for_1, for_2)
        return self.axes.to_pipe(for_1, 1), self.axes.to_pipe(for_2, 2)

    def corner(self, others):
        half = self.half
        self.by = self.send(self.block(3, 0, half).astype(BF16), self.block(3, half, half).astype(BF16), others)

    def sides(self, others):
        half = self.half
        by_1, by_2 = [a.astype(F32) for a in self.by]
        for_1 = jnp.concatenate([self.block(1, 0, half), self.block(1, half, half) + by_2], axis=0).astype(BF16)
        for_2 = jnp.concatenate([self.block(2, 0, half) + by_1, self.block(2, half, half)], axis=0).astype(BF16)
        self.terms = self.send(for_1, for_2, others)

    def back(self, others, zero=0.0):
        mine = self.block(0, 0, self.part) + self.terms[0].astype(F32) + self.terms[1].astype(F32)
        self.mine = (mine + zero).astype(BF16)
        self.near = self.send(self.mine, self.mine, others)

    def across(self, others, zero=0.0):
        for_1, for_2 = self.near[1][self.half :], self.near[0][: self.half]
        self.far = self.send(for_1 + jnp.asarray(zero, BF16), for_2 + jnp.asarray(zero, BF16), others)

    def back_at_once(self):
        mine = self.block(0, 0, self.part) + self.terms[0].astype(F32) + self.terms[1].astype(F32)
        self.mine = mine.astype(BF16)
        self.near = self.send(self.mine, self.mine, [])
        self.far = self.axes.to_pipe(self.mine, 3)

    def result(self):
        if not isinstance(self.far, tuple):
            return [(self.mine, 0, 0), (self.near[0], 1, 0), (self.near[1], 2, 0), (self.far, 3, 0)]
        return [
            (self.mine, 0, 0),
            (self.near[0], 1, 0),
            (self.near[1], 2, 0),
            (self.far[1], 3, 0),
            (self.far[0], 3, self.half),
        ]


def sigmoid(g):
    return 0.5 + 0.5 * jnp.tanh(0.5 * g)


def grads_kernel(cfg, at_rows, *refs):
    refs = list(refs)
    take = lambda n: [refs.pop(0) for _ in range(n)]
    parts = take(len(cfg["sources"]))
    gate_pre, up_pre, gate_w, up_w, gate_m, up_m = take(6)
    acc_in = take(1)[0] if cfg["acc_in"] else None
    gate_out, up_out, acc, hidden, both = refs
    step, tok, chunk = cfg["step"], cfg["tok"], cfg["chunk"]
    k = pl.program_id(0)
    place = at_rows[cfg["groups"]]

    for (r, first), ref in zip(cfg["sources"], parts):
        to = (place ^ r) * cfg["part"] + first
        hidden[pl.ds(pl.multiple_of(to, 16), ref.shape[0]), :] = ref[...]
    for i in range(cfg["groups"]):
        at = pl.ds(pl.multiple_of(at_rows[i], 16), tok)
        g = gate_pre[at, :].astype(F32)
        u = up_pre[at, :].astype(F32)
        h = hidden[i * tok : (i + 1) * tok, :].astype(F32)
        sig = sigmoid(g)
        h = h * sig
        gg = (h * u * (1.0 + g * (1.0 - sig))).astype(BF16)
        ug = (h * g).astype(BF16)
        gate_out[at, :] = gg
        up_out[at, :] = ug
        both[at, :step] = gg
        both[at, step:] = ug

    def tile(n, first):
        def masked(w, m):
            rows = []
            for i in range(chunk // BLOCK):
                at = pl.ds(pl.multiple_of(n * chunk + i * BLOCK, BLOCK), BLOCK)
                rows.append(w[at, :] * m[pl.ds(n * (chunk // BLOCK) + i, 1), :].astype(BF16))
            return jnp.concatenate(rows, axis=0)

        w = jnp.concatenate([masked(gate_w, gate_m), masked(up_w, up_m)], axis=1)
        to = pl.ds(pl.multiple_of(n * chunk, chunk), chunk)
        term = lax.dot_general(both[...], w, NT, preferred_element_type=F32)
        if not first:
            term += acc[:, to]
        elif acc_in is not None:
            term += acc_in[:, to]
        acc[:, to] = term

    tiles = cfg["width"] // chunk

    @pl.when(k == 0)
    def _():
        pl.loop(0, tiles)(lambda n: tile(n, True))

    @pl.when(k > 0)
    def _():
        pl.loop(0, tiles)(lambda n: tile(n, False))


def local_grads(axes, at_rows, sources, gate_pre, up_pre, gate_w, up_w, gate_m, up_m, acc, tok, start, cols):
    tokens, hid = gate_pre.shape
    width = gate_w.shape[0]
    step = step_of(hid)
    first = start // step
    col = lambda k, _: (0, first + k)
    one = lambda k, _: (0, 0)
    own = lambda k, _: (0, k)
    specs = [pl.BlockSpec((a.shape[0], step), own) for a, _, _ in sources]
    specs += [pl.BlockSpec((tokens, step), col)] * 2
    specs += [pl.BlockSpec((width, step), col)] * 2
    specs += [pl.BlockSpec((gate_m.shape[0], step), col)] * 2
    arrays = [a for a, _, _ in sources] + [gate_pre, up_pre, gate_w, up_w, gate_m, up_m]
    if acc is not None:
        specs.append(pl.BlockSpec((tokens, width), one, pipeline_mode=pl.Buffered(1)))
        arrays.append(acc)
    cfg = dict(
        sources=[(r, lo) for _, r, lo in sources], part=tokens // axes.pipe, groups=tokens // tok, tok=tok, step=step,
        width=width, chunk=chunk_of(width, 1024), acc_in=acc is not None,
    )
    return pl.pallas_call(
        functools.partial(grads_kernel, cfg),
        out_shape=[jax.ShapeDtypeStruct((tokens, cols), BF16)] * 2 + [jax.ShapeDtypeStruct((tokens, width), F32)],
        grid_spec=pltpu.PrefetchScalarGridSpec(
            num_scalar_prefetch=1,
            grid=(cols // step,),
            in_specs=specs,
            out_specs=[pl.BlockSpec((tokens, step), own)] * 2 + [pl.BlockSpec((tokens, width), one)],
            scratch_shapes=[pltpu.VMEM((tokens, step), BF16), pltpu.VMEM((tokens, 2 * step), BF16)],
        ),
        compiler_params=params(),
        cost_estimate=pl.CostEstimate(
            flops=4 * tokens * width * cols,
            bytes_accessed=4 * width * cols + 10 * tokens * cols + 8 * tokens * width,
            transcendentals=tokens * cols,
        ),
        name="local_grads",
    )(at_rows, *arrays)


def weights_kernel(cfg, x, gate, up, gate_m, up_m, *refs):
    *outs, done = refs[-3:]
    done[...] = jnp.zeros_like(done)
    chunk = cfg["chunk"]
    for g, m, out in ((gate, gate_m, outs[0]), (up, up_m, outs[1])):

        def tile(n, g=g, m=m, out=out):
            at = pl.ds(pl.multiple_of(n * chunk, chunk), chunk)
            term = lax.dot_general(x[at, :], g[...], NN, preferred_element_type=F32)
            for i in range(chunk // BLOCK):
                to = pl.ds(pl.multiple_of(n * chunk + i * BLOCK, BLOCK), BLOCK)
                row = m[pl.ds(n * (chunk // BLOCK) + i, 1), :]
                out[to, :] = (term[i * BLOCK : (i + 1) * BLOCK, :] * row).astype(BF16)

        pl.loop(0, cfg["width"] // chunk)(tile)


def weight_grads(x_t, gate, up, gate_m, up_m, before, shape, start, skip, steps):
    width, tokens = x_t.shape
    step = step_of(shape[1])
    first = start // step + skip
    col = lambda k: (0, first + k)
    specs = [
        pl.BlockSpec((width, tokens), lambda k: (0, 0), pipeline_mode=pl.Buffered(1)),
        pl.BlockSpec((tokens, step), lambda k: (0, skip + k)),
        pl.BlockSpec((tokens, step), lambda k: (0, skip + k)),
        pl.BlockSpec((gate_m.shape[0], step), col),
        pl.BlockSpec((gate_m.shape[0], step), col),
    ]
    arrays = [x_t, gate, up, gate_m, up_m]
    alias = {}
    if before is not None:
        specs += [pl.BlockSpec(memory_space=pl.ANY)] * 2
        arrays += list(before)
        alias = {5: 0, 6: 1}
    return pl.pallas_call(
        functools.partial(weights_kernel, dict(width=width, chunk=chunk_of(width, 1024))),
        out_shape=[jax.ShapeDtypeStruct(shape, BF16)] * 2 + [jax.ShapeDtypeStruct((8, 128), F32)],
        grid=(steps,),
        in_specs=specs,
        out_specs=[pl.BlockSpec((width, step), col)] * 2 + [pl.BlockSpec((8, 128), lambda k: (0, 0))],
        input_output_aliases=alias,
        compiler_params=params(),
        cost_estimate=pl.CostEstimate(
            flops=4 * tokens * width * steps * step,
            bytes_accessed=4 * (width + tokens) * steps * step + 2 * tokens * width,
            transcendentals=0,
        ),
        name="weight_grads",
    )(*arrays)


def down_kernel(cfg, at_rows, *refs):
    rows, gate_pre, up_pre, mask = refs[:4]
    out, done, hidden = refs[-3:]
    tok = cfg["tok"]
    done[...] = jnp.zeros_like(done)
    for i in range(cfg["groups"]):
        at = pl.ds(pl.multiple_of(at_rows[i], 16), tok)
        g = gate_pre[at, :].astype(F32)
        u = up_pre[at, :].astype(F32)
        hidden[i * tok : (i + 1) * tok, :] = (g * sigmoid(g) * u).astype(BF16)
    across = hidden[...].T
    chunk = cfg["chunk"]

    def tile(n):
        at = pl.ds(pl.multiple_of(n * chunk, chunk), chunk)
        term = lax.dot_general(across, rows[:, at], NN, preferred_element_type=F32)
        for i in range(cfg["step"] // BLOCK):
            part = slice(i * BLOCK, (i + 1) * BLOCK)
            out[part, at] = (term[part, :] * mask[i, :, at]).astype(BF16)

    pl.loop(0, cfg["width"] // chunk)(tile)


def down_grad(at_rows, rows, gate_pre, up_pre, mask, tok, before, first, last):
    tokens, hid = gate_pre.shape
    width = rows.shape[1]
    step = step_of(hid)
    cfg = dict(groups=tokens // tok, tok=tok, width=width, step=step, chunk=chunk_of(width, 1024))
    specs = [pl.BlockSpec(rows.shape, lambda k, _: (0, 0), pipeline_mode=pl.Buffered(1))]
    specs += [pl.BlockSpec((tokens, step), lambda k, _: (0, first + k))] * 2
    specs += [pl.BlockSpec((step // BLOCK, 1, width), lambda k, _: (first + k, 0, 0))]
    arrays = [rows, gate_pre, up_pre, mask]
    alias = {}
    if before is not None:
        specs.append(pl.BlockSpec(memory_space=pl.ANY))
        arrays.append(before)
        alias = {len(arrays): 0}
    cols = (last - first) * step
    return pl.pallas_call(
        functools.partial(down_kernel, cfg),
        out_shape=[jax.ShapeDtypeStruct((hid, width), BF16), jax.ShapeDtypeStruct((8, 128), F32)],
        grid_spec=pltpu.PrefetchScalarGridSpec(
            num_scalar_prefetch=1,
            grid=(last - first,),
            in_specs=specs,
            out_specs=[
                pl.BlockSpec((step, width), lambda k, _: (first + k, 0)),
                pl.BlockSpec((8, 128), lambda k, _: (0, 0)),
            ],
            scratch_shapes=[pltpu.VMEM((tokens, step), BF16)],
        ),
        input_output_aliases=alias,
        compiler_params=params(),
        cost_estimate=pl.CostEstimate(
            flops=2 * tokens * width * cols,
            bytes_accessed=2 * (tokens * width + 2 * tokens * cols + width * cols),
            transcendentals=tokens * cols,
        ),
        name="down_grad",
    )(at_rows, *arrays)


def masked(weight, mask):
    rows, cols = weight.shape
    return (weight.reshape(rows // BLOCK, BLOCK, cols) * mask.astype(BF16)[:, None, :]).reshape(rows, cols)


def dot_nt(a, b):
    return lax.dot_general(a, b, NT, preferred_element_type=F32)


def shards(axes, layer_input, out_grad, gate_pre, up_pre, gate_weight, up_weight, down_weight, gate_mask, up_mask, down_mask):
    tokens, hid = gate_pre.shape
    tok, width = out_grad.shape
    step = step_of(hid)
    steps = hid // step
    first = (steps + 1) // 2 * step
    pieces = [(0, first), (first, hid - first)]
    at_rows = axes.rows(tok)
    gate_m = jnp.repeat(gate_mask, BLOCK, axis=1).astype(F32)
    up_m = jnp.repeat(up_mask, BLOCK, axis=1).astype(F32)
    down_m = jnp.repeat(down_mask, BLOCK, axis=1).astype(F32)

    near = [out_grad, axes.to_core(out_grad)]
    downs = [masked(down_weight[c : c + w], down_m[c // BLOCK : (c + w) // BLOCK]) for c, w in pieces]
    half = tok // 2
    now, got = [out_grad[:half], out_grad[half:]], []
    for s in range(axes.chips - 1):
        if s == 2:
            now = lax.optimization_barrier((*now, downs[0]))[:2]
        now = [axes.to_next(a) for a in now]
        got += now
    rows = jnp.concatenate(near + got + [axes.to_core(a) for a in got], axis=0)

    x = lax.all_gather(after(layer_input, rows), "tensor", axis=0, tiled=True)
    down = functools.partial(down_grad, rows=rows, gate_pre=gate_pre, up_pre=up_pre, mask=down_m[:, None, :], tok=tok)
    if axes.pipe == 4:
        squares = []
        for i, d in enumerate(downs):
            prev = squares[i - 1] if i else None
            sq = Square(axes, dot_nt(after(rows, *prev.by) if i else rows, d))
            squares.append(sq)
            sq.corner(prev.by if i else [])
            if not i:
                grad_down, done = down(after(at_rows, *sq.by), before=None, first=0, last=(steps + 1) // 2)
            sq.sides(prev.terms if i else [])
            if i:
                sq.back_at_once()
                continue
            sq.back([], done[0, 0])
            grad_down, done = down(after(at_rows, *sq.terms), before=grad_down, first=(steps + 1) // 2, last=steps)
            sq.across([], done[0, 0])
        at_rows = at_rows + nothing(squares[-1].mine).astype(jnp.int32)
        sums = [sq.result() for sq in squares]
    else:
        parts = [dot_nt(rows, d) for d in downs]
        sums = [reduce_over_pipe(axes, p) for p in parts]
        grad_down, _ = down(after(at_rows, *parts), before=None, first=0, last=steps)
    x_t = x.T
    at_rows = at_rows + nothing(x_t).astype(jnp.int32)

    acc, grads = None, []
    for (c, w), sources in zip(pieces, sums):
        gate, up, acc = local_grads(
            axes, at_rows, sources, gate_pre, up_pre, gate_weight, up_weight, gate_m, up_m, acc, tok, c, w
        )
        grads.append((gate, up))

    core = lax.axis_index("tensor") % 2
    slots = axes.slots()
    by_core = acc.reshape(axes.chips, 2, tok, width)
    pick = lambda a, i, axis: lax.dynamic_index_in_dim(a, i, axis, keepdims=False)
    total = pick(by_core, core, 1) + axes.to_core(pick(by_core, 1 - core, 1))

    todo = [(c, g, skip, min(2, w // step - skip)) for (c, w), g in zip(pieces, grads) for skip in range(0, w // step, 2)]
    weights = None

    def weights_part(zero):
        nonlocal weights
        c, (gate, up), skip, count = todo.pop(0)
        weights = weight_grads(x_t, gate, up, gate_m, up_m + zero, weights, gate_weight.shape, c, skip, count)
        *weights, done = weights
        return done[0, 0]

    weights_part(0.0)
    run = pick(total, slots[1 % axes.chips], 0).astype(BF16)
    for s in range(1, axes.chips):
        zero = weights_part(nothing(run)) if todo else 0.0
        run = axes.to_next(run).astype(F32) + pick(total, slots[(s + 1) % axes.chips], 0) + zero
        run = run.astype(BF16)
    while todo:
        weights_part(0.0)
    return (run, weights[0], weights[1], grad_down)


def solution(mesh):
    in_specs = (
        P("tensor", "pipe"),
        P("tensor", "pipe"),
        P(None, "tensor"),
        P(None, "tensor"),
        P("pipe", "tensor"),
        P("pipe", "tensor"),
        P("tensor", "pipe"),
        P("pipe", "tensor"),
        P("pipe", "tensor"),
        P("tensor", "pipe"),
    )
    out_specs = (P("tensor", "pipe"), P("pipe", "tensor"), P("pipe", "tensor"), P("tensor", "pipe"))
    return jax.shard_map(
        functools.partial(shards, Axes(mesh)), mesh=mesh, in_specs=in_specs, out_specs=out_specs, check_vma=False
    )
```

time: 378 us -> 314 us (0.83)
  matrix products: 95.9 us -> 15.4 us
  Pallas kernels: 97.8 us -> 125 us
  starting transfers between devices: 47.4 us -> 25.7 us
  other arithmetic: 39 us -> 46.7 us
    dot_general x6 -> x2, matrix products: 59.9 us -> 15.4 us  [dot_nt(): return lax.dot_general(a, b, NT, preferred_element_type=F32)]
    dot_general x2 -> x0, matrix products: 36 us -> none  [weight_grad(): lax.dot_general(x.reshape(tokens, blocks, BLOCK), grad, (((0,), (0,)), ((...]
    pallas_call x3 -> x2, Pallas kernels: 36.4 us -> 51.5 us  [local_grads(): pl.pallas_call(functools.partial(grads_kernel, cfg), out_shape=[jax.Shape...]
    ppermute x12 -> x9, starting transfers between devices: 22.7 us -> 8.14 us  [to_next(): lax.ppermute(x, 'tensor', [(2 * a + k, 2 * b + k) for a, b in pairs for k...]
    pallas_call x3 -> x4, Pallas kernels: 33.3 us -> 46.3 us  [weight_grads(): pl.pallas_call(functools.partial(weights_kernel, dict(width=width, chunk=...]
    ppermute x24 -> x15, starting transfers between devices: 24.7 us -> 15.8 us  [to_pipe(): return lax.ppermute(x, 'pipe', [(i, i ^ bit) for i in range(self.pipe)])]
    convert_element_type x6 -> x4, other arithmetic: 0.25 us -> 8.23 us  [the longest x3 5.96 us: shards(): run = run.astype(BF16)]
    another operation x3 -> x2, local copies, waits for them, and re-layouts: 5.26 us -> 1.19 us
  transfers between devices with their start and end apart: 40 -> 33, of which waited for: 15 -> 11; matrix products, arithmetic and copies ran while one was open for 33% -> 21% of each run, Pallas kernels for 23% -> 32%
where the time goes in v5:
time: 314 us; the launch traced here: 312 us
  Pallas kernels  125 us (40%)
  other arithmetic  46.7 us (15%)
  waiting for transfers between devices  38.8 us (12%)
  local copies, waits for them, and re-layouts  34.9 us (11%)
  starting transfers between devices  25.7 us (8%)
  between operations  25.7 us (8%)
  matrix products  15.4 us (5%)
    pallas_call x2, Pallas kernels, local_grads(): pl.pallas_call(functools.partial(grads_kernel, cfg), out_shape=[jax.Shape...  51.5 us
    pallas_call x4, Pallas kernels, weight_grads(): pl.pallas_call(functools.partial(weights_kernel, dict(width=width, chunk=...  46.3 us
    pallas_call x2, Pallas kernels, down_grad(): pl.pallas_call(functools.partial(down_kernel, cfg), out_shape=[jax.ShapeD...  27.3 us
    ppermute x9, waiting for transfers between devices, to_next(): lax.ppermute(x, 'tensor', [(2 * a + k, 2 * b + k) for a, b in pairs for k...  19.6 us
    ppermute x15, waiting for transfers between devices, to_pipe(): return lax.ppermute(x, 'pipe', [(i, i ^ bit) for i in range(self.pipe)])  18.2 us
    ppermute x15, starting transfers between devices, to_pipe(): return lax.ppermute(x, 'pipe', [(i, i ^ bit) for i in range(self.pipe)])  15.8 us
    dot_general x2, matrix products, dot_nt(): return lax.dot_general(a, b, NT, preferred_element_type=F32)  15.4 us
    mul x2, other arithmetic, masked(): weight.reshape(rows // BLOCK, BLOCK, cols) * mask.astype(BF16)[:, None, :]  13.3 us
  transfers between devices with their start and end apart: 33, of which 11 were waited for; matrix products, arithmetic and copies ran while one was open for 21% of the time, Pallas kernels for 32%

profile of v5, /device:TPU:0, one launch (start us, length us, event | category | flops | bytes accessed | tf_op | source)
XLA Modules:
  0.0 312.5 jit_solution(11478163286381426998)
XLA Ops:
  8.8 2.6 collective-permute-start.2
  11.4 2.6 collective-permute-start.1
  17.5 7.4 %bitcast_multiply_fusion = bf16[2048,2048]{1,0:T(8,128)(2,1)} fusion(bf16[3584,2048]{1,0:T(8,128)(2,1)} %param.18, bf16[16,2048]{1,0:T(8,128)(2,1)S(1)} %bitcast.87), kind=kLoop, calls=%fused_computation | loop fusion | flops 4194304 | bytes 16842752 | tf_op jit(solution)/shard_map/mul | solution.py:358
  26.1 7.8 %collective-permute-done.4 = bf16[48,2048]{1,0:T(8,128)(2,1)S(1)} collective-permute-done((bf16[48,2048]{1,0:T(8,128)(2,1)}, bf16[48,2048]{1,0:T(8,128)(2,1)S(1)}, u32[]{:S(2)}, u32[]{:S(2)}) %collective-permute-start.4) | collective-permute-done | bytes 196640 | tf_op jit(solution)/shard_map/ppermute | solution.py:69
  33.8 3.2 %collective-permute-done.3 = bf16[48,2048]{1,0:T(8,128)(2,1)S(1)} collective-permute-done((bf16[48,2048]{1,0:T(8,128)(2,1)}, bf16[48,2048]{1,0:T(8,128)(2,1)S(1)}, u32[]{:S(2)}, u32[]{:S(2)}) %collective-permute-start.3) | collective-permute-done | bytes 196640 | tf_op jit(solution)/shard_map/ppermute | solution.py:69
  39.8 6.0 %collective-permute-done.5 = bf16[48,2048]{1,0:T(8,128)(2,1)S(1)} collective-permute-done((bf16[48,2048]{1,0:T(8,128)(2,1)S(1)}, bf16[48,2048]{1,0:T(8,128)(2,1)S(1)}, u32[]{:S(2)}, u32[]{:S(2)}) %collective-permute-start.5) | collective-permute-done | bytes 196640 | tf_op jit(solution)/shard_map/ppermute | solution.py:69
  45.8 2.2 collective-permute-done.6
  49.8 10.2 %fusion.10 = f32[768,2048]{1,0:T(8,128)S(1)} fusion(bf16[768,2048]{1,0:T(8,128)(2,1)S(1)} %constant_dynamic-update-slice_fusion.refs_0_, bf16[2048,2048]{1,0:T(8,128)(2,1)} %bitcast_multiply_fusion), kind=kOutput, calls=%fused_computation.65 | convolution fusion | flops 6442450944 | bytes 17825792 | tf_op jit(solution)/shard_map/dot_general | solution.py:362
  60.0 2.7 copy-done.4
  70.5 5.9 %bitcast_multiply_fusion.1 = bf16[1536,2048]{1,0:T(8,128)(2,1)} fusion(bf16[3584,2048]{1,0:T(8,128)(2,1)} %param.18, bf16[12,2048]{1,0:T(8,128)(2,1)S(1)} %bitcast.88), kind=kLoop, calls=%fused_computation.1 | loop fusion | flops 3145728 | bytes 12632064 | tf_op jit(solution)/shard_map/mul | solution.py:358
  78.9 2.5 concatenate.22.at_rows
  83.4 2.4 pad_maximum_fusion
  87.7 5.2 %fusion.11 = f32[768,1536]{1,0:T(8,128)S(1)} fusion(bf16[768,2048]{1,0:T(8,128)(2,1)S(1)} %constant_dynamic-update-slice_fusion.refs_0_, bf16[1536,2048]{1,0:T(8,128)(2,1)S(1)} %copy-done.1), kind=kOutput, calls=%fused_computation.66 | convolution fusion | flops 4831838208 | bytes 14155776 | tf_op jit(solution)/shard_map/dot_general | solution.py:362
  92.9 2.2 copy-done.5
  99.2 14.9 %down_grad.2 = (bf16[3584,2048]{1,0:T(8,128)(2,1)}, f32[8,128]{1,0:T(8,128)}) custom-call(s32[9]{0:T(128)} %concatenate.22.at_rows, bf16[768,2048]{1,0:T(8,128)(2,1)} %copy-done.3, bf16[768,3584]{1,0:T(8,128)(2,1)} %refs_4_.1, bf16[768,3584]{1,0:T(8,128)(2,1)} %refs_5_.3, f32[28,1,2048]{2,1,0:T(1,128)} %bitcast.85), custom_call_target="tpu_custom_call" | custom-call | flops 6442450944 | bytes 17825792 | tf_op jit(solution)/shard_map/down_grad/pallas_call | solution.py:332
  115.3 2.8 add_convert_fusion.refs_0_
  123.7 12.5 %down_grad.3 = (bf16[3584,2048]{1,0:T(8,128)(2,1)}, f32[8,128]{1,0:T(8,128)}) custom-call(s32[9]{0:T(128)} %concatenate.22.at_rows, bf16[768,2048]{1,0:T(8,128)(2,1)} %copy-done.3, bf16[768,3584]{1,0:T(8,128)(2,1)} %refs_4_.1, bf16[768,3584]{1,0:T(8,128)(2,1)} %refs_5_.3, f32[28,1,2048]{2,1,0:T(1,128)} %bitcast.86, ...), custom_call_target="tpu_custom_call", output_to_operand_aliasing={{0}: (5, {})} | custom-call | flops 4831838208 | bytes 14155776 | tf_op jit(solution)/shard_map/down_grad/pallas_call | solution.py:332
  141.7 2.4 slice_add_fusion
  144.7 6.5 %collective-permute-done.19 = bf16[192,1536]{1,0:T(8,128)(2,1)S(1)} collective-permute-done((bf16[192,1536]{1,0:T(8,128)(2,1)S(1)}, bf16[192,1536]{1,0:T(8,128)(2,1)S(1)}, u32[]{:S(2)}, u32[]{:S(2)}) %collective-permute-start.19) | collective-permute-done | bytes 589856 | tf_op jit(solution)/shard_map/ppermute | solution.py:65
  151.3 1.9 collective-permute-done.20
  153.2 2.3 add_convert_fusion.1.refs_0_
  160.9 3.2 %copy.37 = bf16[768,2048]{0,1:T(8,128)(2,1)S(1)} copy(bf16[768,2048]{1,0:T(8,128)(2,1)} %all-gather.2.cloned.1.call-done) | data formatting | bytes 6291456 | tf_op jit(solution)/shard_map/all_gather | solution.py:388
  165.9 8.5 %collective-permute-done.26.refs_3_ = bf16[96,2048]{1,0:T(8,128)(2,1)} collective-permute-done((bf16[96,2048]{1,0:T(8,128)(2,1)S(1)}, bf16[96,2048]{1,0:T(8,128)(2,1)}, u32[]{:S(2)}, u32[]{:S(2)}) %collective-permute-start.26) | collective-permute-done | bytes 393248 | tf_op jit(solution)/shard_map/ppermute | solution.py:65
  174.4 26.9 %local_grads.2 = (bf16[768,2048]{1,0:T(8,128)(2,1)}, bf16[768,2048]{1,0:T(8,128)(2,1)}, f32[768,2048]{1,0:T(8,128)}) custom-call(s32[9]{0:T(128)} %add_add_fusion.at_rows, bf16[192,2048]{1,0:T(8,128)(2,1)} %copy-done.7, bf16[192,2048]{1,0:T(8,128)(2,1)} %copy-done.8, bf16[192,2048]{1,0:T(8,128)(2,1)} %collective-permute-done.25.refs_2_, ...), custom_call_target="tpu_custom_call" | custom-call | flops 12884901888 | bytes 45088768 | tf_op jit(solution)/shard_map/local_grads/pallas_call | solution.py:222
  201.4 24.6 %local_grads.3 = (bf16[768,1536]{1,0:T(8,128)(2,1)}, bf16[768,1536]{1,0:T(8,128)(2,1)}, f32[768,2048]{1,0:T(8,128)}) custom-call(s32[9]{0:T(128)} %add_add_fusion.at_rows, bf16[192,1536]{1,0:T(8,128)(2,1)} %add_convert_fusion.1.refs_0_, bf16[192,1536]{1,0:T(8,128)(2,1)} %collective-permute-done.21.refs_1_, ...), custom_call_target="tpu_custom_call" | custom-call | flops 9663676416 | bytes 36962304 | tf_op jit(solution)/shard_map/local_grads/pallas_call | solution.py:222
  226.0 3.9 %dynamic-slice_bitcast_fusion = f32[4,96,2048]{2,1,0:T(8,128)} fusion(f32[4,2,96,2048]{3,2,1,0:T(8,128)} %bitcast.81, s32[]{:T(128)S(6)} %select_n.77), kind=kLoop, calls=%fused_computation.3 | loop fusion | bytes 6291460 | tf_op jit(solution)/shard_map/jit(dynamic_index_in_dim)/squeeze | solution.py:425
  238.4 13.0 %weight_grads.4 = (bf16[2048,3584]{1,0:T(8,128)(2,1)}, bf16[2048,3584]{1,0:T(8,128)(2,1)}, f32[8,128]{1,0:T(8,128)}) custom-call(bf16[2048,768]{1,0:T(8,128)(2,1)} %bitcast.77, bf16[768,2048]{1,0:T(8,128)(2,1)} %get-tuple-element.50.gate, bf16[768,2048]{1,0:T(8,128)(2,1)} %get-tuple-element.51.up, f32[16,3584]{1,0:T(8,128)} %get-tuple-element.94.refs_9_.refs_8_.gate_m, ...), custom_call_target="tpu_custom_call" | custom-call | flops 6442450944 | bytes 14680064 | tf_op jit(solution)/shard_map/weight_grads/pallas_call | solution.py:277
  251.4 3.6 %bitcast_add_fusion = f32[4,96,2048]{2,1,0:T(8,128)S(1)} fusion(f32[4,96,2048]{2,1,0:T(8,128)} %collective-permute-done.28, f32[4,2,96,2048]{3,2,1,0:T(8,128)} %bitcast.82, s32[]{:T(128)S(6)} %select_n.76), kind=kLoop, calls=%fused_computation.2 | loop fusion | flops 786432 | bytes 9437188 | tf_op jit(solution)/shard_map/add | solution.py:426
  257.0 12.6 %weight_grads.5 = (bf16[2048,3584]{1,0:T(8,128)(2,1)}, bf16[2048,3584]{1,0:T(8,128)(2,1)}, f32[8,128]{1,0:T(8,128)}) custom-call(bf16[2048,768]{1,0:T(8,128)(2,1)} %bitcast.78, bf16[768,2048]{1,0:T(8,128)(2,1)} %get-tuple-element.50.gate, bf16[768,2048]{1,0:T(8,128)(2,1)} %get-tuple-element.51.up, ...), custom_call_target="tpu_custom_call", output_to_operand_aliasing={{0}: (5, {}), {1}: (6, {})} | custom-call | flops 6442450944 | bytes 14680064 | tf_op jit(solution)/shard_map/weight_grads/pallas_call | solution.py:277
  275.2 12.6 %weight_grads.6 = (bf16[2048,3584]{1,0:T(8,128)(2,1)}, bf16[2048,3584]{1,0:T(8,128)(2,1)}, f32[8,128]{1,0:T(8,128)}) custom-call(bf16[2048,768]{1,0:T(8,128)(2,1)} %bitcast.79, bf16[768,1536]{1,0:T(8,128)(2,1)} %get-tuple-element.55.gate, bf16[768,1536]{1,0:T(8,128)(2,1)} %get-tuple-element.56.up, ...), custom_call_target="tpu_custom_call", output_to_operand_aliasing={{0}: (5, {}), {1}: (6, {})} | custom-call | flops 6442450944 | bytes 14680064 | tf_op jit(solution)/shard_map/weight_grads/pallas_call | solution.py:277
  293.3 8.2 %weight_grads.7 = (bf16[2048,3584]{1,0:T(8,128)(2,1)}, bf16[2048,3584]{1,0:T(8,128)(2,1)}, f32[8,128]{1,0:T(8,128)}) custom-call(bf16[2048,768]{1,0:T(8,128)(2,1)} %bitcast.80, bf16[768,1536]{1,0:T(8,128)(2,1)} %get-tuple-element.55.gate, bf16[768,1536]{1,0:T(8,128)(2,1)} %get-tuple-element.56.up, ...), custom_call_target="tpu_custom_call", output_to_operand_aliasing={{0}: (5, {}), {1}: (6, {})} | custom-call | flops 3221225472 | bytes 8912896 | tf_op jit(solution)/shard_map/weight_grads/pallas_call | solution.py:277
  303.1 2.5 fusion.1
  (143 shorter events, 61.0 us)
Async XLA Ops:
  7.2 153.7 %all-gather.2.cloned.1.call-start = ((), (), s32[]{:S(2)}) async-start(), calls=%async_computation | async-start | bytes 3538944 | tf_op jit(solution)/shard_map/all_gather | solution.py:388
  7.2 30.6 %collective-permute-start = (bf16[96,2048]{1,0:T(8,128)(2,1)}, bf16[96,2048]{1,0:T(8,128)(2,1)S(1)}, u32[]{:S(2)}, u32[]{:S(2)}) collective-permute-start(bf16[96,2048]{1,0:T(8,128)(2,1)} %param.13), channel_id=1, source_target_pairs={{0,1},{1,0},{2,3},{3,2},{4,5},{5,4},{6,7},{7,6},{8,9},{9,8},{10,11... | collective-permute-start | bytes 1179656 | tf_op jit(solution)/shard_map/ppermute | solution.py:62
  8.8 16.2 %collective-permute-start.2 = (bf16[48,2048]{1,0:T(8,128)(2,1)S(1)}, bf16[48,2048]{1,0:T(8,128)(2,1)}, u32[]{:S(2)}, u32[]{:S(2)}) collective-permute-start(bf16[48,2048]{1,0:T(8,128)(2,1)S(1)} %get-tuple-element.78), channel_id=1, source_target_pairs={{0,2},{1,3},{2,6},{3,7},{6,4},{7,5},{4,0},{5,1},{8,10},{9,11},{10,... | collective-permute-start | bytes 589832 | tf_op jit(solution)/shard_map/ppermute | solution.py:69
  11.4 14.0 %collective-permute-start.1 = (bf16[48,2048]{1,0:T(8,128)(2,1)S(1)}, bf16[48,2048]{1,0:T(8,128)(2,1)}, u32[]{:S(2)}, u32[]{:S(2)}) collective-permute-start(bf16[48,2048]{1,0:T(8,128)(2,1)S(1)} %get-tuple-element.79), channel_id=1, source_target_pairs={{0,2},{1,3},{2,6},{3,7},{6,4},{7,5},{4,0},{5,1},{8,10},{9,11},{10,... | collective-permute-start | bytes 589832 | tf_op jit(solution)/shard_map/ppermute | solution.py:69
  25.0 8.9 %collective-permute-start.4 = (bf16[48,2048]{1,0:T(8,128)(2,1)}, bf16[48,2048]{1,0:T(8,128)(2,1)S(1)}, u32[]{:S(2)}, u32[]{:S(2)}) collective-permute-start(bf16[48,2048]{1,0:T(8,128)(2,1)} %collective-permute-done.2), channel_id=1, source_target_pairs={{0,2},{1,3},{2,6},{3,7},{6,4},{7,5},{4,0},{5,1},{8,10},{9,11},{10,... | collective-permute-start | bytes 589832 | tf_op jit(solution)/shard_map/ppermute | solution.py:69
  25.4 11.6 %collective-permute-start.3 = (bf16[48,2048]{1,0:T(8,128)(2,1)}, bf16[48,2048]{1,0:T(8,128)(2,1)S(1)}, u32[]{:S(2)}, u32[]{:S(2)}) collective-permute-start(bf16[48,2048]{1,0:T(8,128)(2,1)} %collective-permute-done.1), channel_id=1, source_target_pairs={{0,2},{1,3},{2,6},{3,7},{6,4},{7,5},{4,0},{5,1},{8,10},{9,11},{10,... | collective-permute-start | bytes 589832 | tf_op jit(solution)/shard_map/ppermute | solution.py:69
  25.5 23.1 %collective-permute-start.8 = (bf16[48,2048]{1,0:T(8,128)(2,1)}, bf16[48,2048]{1,0:T(8,128)(2,1)S(1)}, u32[]{:S(2)}, u32[]{:S(2)}) collective-permute-start(bf16[48,2048]{1,0:T(8,128)(2,1)} %collective-permute-done.2), channel_id=1, source_target_pairs={{0,1},{1,0},{2,3},{3,2},{4,5},{5,4},{6,7},{7,6},{8,9},{9,8},{10,11... | collective-permute-start | bytes 589832 | tf_op jit(solution)/shard_map/ppermute | solution.py:62
  25.6 22.4 %collective-permute-start.7 = (bf16[48,2048]{1,0:T(8,128)(2,1)}, bf16[48,2048]{1,0:T(8,128)(2,1)S(1)}, u32[]{:S(2)}, u32[]{:S(2)}) collective-permute-start(bf16[48,2048]{1,0:T(8,128)(2,1)} %collective-permute-done.1), channel_id=1, source_target_pairs={{0,1},{1,0},{2,3},{3,2},{4,5},{5,4},{6,7},{7,6},{8,9},{9,8},{10,11... | collective-permute-start | bytes 589832 | tf_op jit(solution)/shard_map/ppermute | solution.py:62
  37.0 8.7 %collective-permute-start.5 = (bf16[48,2048]{1,0:T(8,128)(2,1)S(1)}, bf16[48,2048]{1,0:T(8,128)(2,1)S(1)}, u32[]{:S(2)}, u32[]{:S(2)}) collective-permute-start(bf16[48,2048]{1,0:T(8,128)(2,1)S(1)} %collective-permute-done.3), channel_id=1, source_target_pairs={{0,2},{1,3},{2,6},{3,7},{6,4},{7,5},{4,0},{5,1},{8,10},{9,11},{10,... | collective-permute-start | bytes 589832 | tf_op jit(solution)/shard_map/ppermute | solution.py:69
  37.0 11.0 %collective-permute-start.6 = (bf16[48,2048]{1,0:T(8,128)(2,1)S(1)}, bf16[48,2048]{1,0:T(8,128)(2,1)S(1)}, u32[]{:S(2)}, u32[]{:S(2)}) collective-permute-start(bf16[48,2048]{1,0:T(8,128)(2,1)S(1)} %collective-permute-done.4), channel_id=1, source_target_pairs={{0,2},{1,3},{2,6},{3,7},{6,4},{7,5},{4,0},{5,1},{8,10},{9,11},{10,... | collective-permute-start | bytes 589832 | tf_op jit(solution)/shard_map/ppermute | solution.py:69
  37.8 10.9 %collective-permute-start.10 = (bf16[48,2048]{1,0:T(8,128)(2,1)S(1)}, bf16[48,2048]{1,0:T(8,128)(2,1)S(1)}, u32[]{:S(2)}, u32[]{:S(2)}) collective-permute-start(bf16[48,2048]{1,0:T(8,128)(2,1)S(1)} %collective-permute-done.4), channel_id=1, source_target_pairs={{0,1},{1,0},{2,3},{3,2},{4,5},{5,4},{6,7},{7,6},{8,9},{9,8},{10,11... | collective-permute-start | bytes 589832 | tf_op jit(solution)/shard_map/ppermute | solution.py:62
  45.8 2.9 collective-permute-start.9
  48.0 1.7 collective-permute-start.12
  63.8 17.7 %collective-permute-start.14 = (bf16[96,2048]{1,0:T(8,128)(2,1)}, bf16[96,2048]{1,0:T(8,128)(2,1)}, u32[]{:S(2)}, u32[]{:S(2)}) collective-permute-start(bf16[96,2048]{1,0:T(8,128)(2,1)} %get-tuple-element.70), channel_id=1, source_target_pairs={{0,16},{8,24},{16,0},{24,8},{1,17},{9,25},{17,1},{25,9},{2,18},{10... | collective-permute-start | bytes 1179656 | tf_op jit(solution)/shard_map/ppermute | solution.py:65
  65.3 16.1 %collective-permute-start.13 = (bf16[96,2048]{1,0:T(8,128)(2,1)}, bf16[96,2048]{1,0:T(8,128)(2,1)}, u32[]{:S(2)}, u32[]{:S(2)}) collective-permute-start(bf16[96,2048]{1,0:T(8,128)(2,1)} %get-tuple-element.71), channel_id=1, source_target_pairs={{0,8},{8,0},{16,24},{24,16},{1,9},{9,1},{17,25},{25,17},{2,10},{10... | collective-permute-start | bytes 1179656 | tf_op jit(solution)/shard_map/ppermute | solution.py:65
  85.8 29.4 %collective-permute-start.17 = (bf16[192,2048]{1,0:T(8,128)(2,1)}, bf16[192,2048]{1,0:T(8,128)(2,1)}, u32[]{:S(2)}, u32[]{:S(2)}) collective-permute-start(bf16[192,2048]{1,0:T(8,128)(2,1)} %pad_maximum_fusion), channel_id=1, source_target_pairs={{0,8},{8,0},{16,24},{24,16},{1,9},{9,1},{17,25},{25,17},{2,10},{10... | collective-permute-start | bytes 2359304 | tf_op jit(solution)/shard_map/ppermute | solution.py:65
  87.2 28.1 %collective-permute-start.18 = (bf16[192,2048]{1,0:T(8,128)(2,1)}, bf16[192,2048]{1,0:T(8,128)(2,1)}, u32[]{:S(2)}, u32[]{:S(2)}) collective-permute-start(bf16[192,2048]{1,0:T(8,128)(2,1)} %pad_maximum_fusion.1), channel_id=1, source_target_pairs={{0,16},{8,24},{16,0},{24,8},{1,17},{9,25},{17,1},{25,9},{2,18},{10... | collective-permute-start | bytes 2359304 | tf_op jit(solution)/shard_map/ppermute | solution.py:65
  95.2 23.4 %collective-permute-start.15 = (bf16[96,1536]{1,0:T(8,128)(2,1)S(1)}, bf16[96,1536]{1,0:T(8,128)(2,1)S(1)}, u32[]{:S(2)}, u32[]{:S(2)}) collective-permute-start(bf16[96,1536]{1,0:T(8,128)(2,1)S(1)} %get-tuple-element.38), channel_id=1, source_target_pairs={{0,16},{8,24},{16,0},{24,8},{1,17},{9,25},{17,1},{25,9},{2,18},{10... | collective-permute-start | bytes 884744 | tf_op jit(solution)/shard_map/ppermute | solution.py:65
  96.8 21.8 %collective-permute-start.16 = (bf16[96,1536]{1,0:T(8,128)(2,1)S(1)}, bf16[96,1536]{1,0:T(8,128)(2,1)S(1)}, u32[]{:S(2)}, u32[]{:S(2)}) collective-permute-start(bf16[96,1536]{1,0:T(8,128)(2,1)S(1)} %get-tuple-element.39), channel_id=1, source_target_pairs={{0,8},{8,0},{16,24},{24,16},{1,9},{9,1},{17,25},{25,17},{2,10},{10... | collective-permute-start | bytes 884744 | tf_op jit(solution)/shard_map/ppermute | solution.py:65
  118.1 20.5 %collective-permute-start.24 = (bf16[192,2048]{1,0:T(8,128)(2,1)S(1)}, bf16[192,2048]{1,0:T(8,128)(2,1)S(1)}, u32[]{:S(2)}, u32[]{:S(2)}) collective-permute-start(bf16[192,2048]{1,0:T(8,128)(2,1)S(1)} %add_convert_fusion.refs_0_), channel_id=1, source_target_pairs={{0,8},{8,0},{16,24},{24,16},{1,9},{9,1},{17,25},{25,17},{2,10},{10... | collective-permute-start | bytes 2359304 | tf_op jit(solution)/shard_map/ppermute | solution.py:65
  120.1 21.7 %collective-permute-start.25 = (bf16[192,2048]{1,0:T(8,128)(2,1)S(1)}, bf16[192,2048]{1,0:T(8,128)(2,1)}, u32[]{:S(2)}, u32[]{:S(2)}) collective-permute-start(bf16[192,2048]{1,0:T(8,128)(2,1)S(1)} %add_convert_fusion.refs_0_), channel_id=1, source_target_pairs={{0,16},{8,24},{16,0},{24,8},{1,17},{9,25},{17,1},{25,9},{2,18},{10... | collective-permute-start | bytes 2359304 | tf_op jit(solution)/shard_map/ppermute | solution.py:65
  120.6 30.6 %collective-permute-start.19 = (bf16[192,1536]{1,0:T(8,128)(2,1)S(1)}, bf16[192,1536]{1,0:T(8,128)(2,1)S(1)}, u32[]{:S(2)}, u32[]{:S(2)}) collective-permute-start(bf16[192,1536]{1,0:T(8,128)(2,1)S(1)} %get-tuple-element.40), channel_id=1, source_target_pairs={{0,8},{8,0},{16,24},{24,16},{1,9},{9,1},{17,25},{25,17},{2,10},{10... | collective-permute-start | bytes 1769480 | tf_op jit(solution)/shard_map/ppermute | solution.py:65
  122.1 31.1 %collective-permute-start.20 = (bf16[192,1536]{1,0:T(8,128)(2,1)S(1)}, bf16[192,1536]{1,0:T(8,128)(2,1)S(1)}, u32[]{:S(2)}, u32[]{:S(2)}) collective-permute-start(bf16[192,1536]{1,0:T(8,128)(2,1)S(1)} %get-tuple-element.41), channel_id=1, source_target_pairs={{0,16},{8,24},{16,0},{24,8},{1,17},{9,25},{17,1},{25,9},{2,18},{10... | collective-permute-start | bytes 1769480 | tf_op jit(solution)/shard_map/ppermute | solution.py:65
  141.3 33.2 %collective-permute-start.26 = (bf16[96,2048]{1,0:T(8,128)(2,1)S(1)}, bf16[96,2048]{1,0:T(8,128)(2,1)}, u32[]{:S(2)}, u32[]{:S(2)}) collective-permute-start(bf16[96,2048]{1,0:T(8,128)(2,1)S(1)} %slice_add_fusion.1), channel_id=1, source_target_pairs={{0,16},{8,24},{16,0},{24,8},{1,17},{9,25},{17,1},{25,9},{2,18},{10... | collective-permute-start | bytes 1179656 | tf_op jit(solution)/shard_map/ppermute | solution.py:65
  144.2 30.2 %collective-permute-start.27 = (bf16[96,2048]{1,0:T(8,128)(2,1)}, bf16[96,2048]{1,0:T(8,128)(2,1)}, u32[]{:S(2)}, u32[]{:S(2)}) collective-permute-start(bf16[96,2048]{1,0:T(8,128)(2,1)} %slice_add_fusion), channel_id=1, source_target_pairs={{0,8},{8,0},{16,24},{24,16},{1,9},{9,1},{17,25},{25,17},{2,10},{10... | collective-permute-start | bytes 1179656 | tf_op jit(solution)/shard_map/ppermute | solution.py:65
  156.7 44.6 %collective-permute-start.23 = (bf16[192,1536]{1,0:T(8,128)(2,1)}, bf16[192,1536]{1,0:T(8,128)(2,1)}, u32[]{:S(2)}, u32[]{:S(2)}) collective-permute-start(bf16[192,1536]{1,0:T(8,128)(2,1)} %add_convert_fusion.1.refs_0_), channel_id=1, source_target_pairs={{0,24},{8,16},{16,8},{24,0},{1,25},{9,17},{17,9},{25,1},{2,26},{10... | collective-permute-start | bytes 1769480 | tf_op jit(solution)/shard_map/ppermute | solution.py:65
  158.1 43.2 %collective-permute-start.22 = (bf16[192,1536]{1,0:T(8,128)(2,1)}, bf16[192,1536]{1,0:T(8,128)(2,1)}, u32[]{:S(2)}, u32[]{:S(2)}) collective-permute-start(bf16[192,1536]{1,0:T(8,128)(2,1)} %add_convert_fusion.1.refs_0_), channel_id=1, source_target_pairs={{0,16},{8,24},{16,0},{24,8},{1,17},{9,25},{17,1},{25,9},{2,18},{10... | collective-permute-start | bytes 1769480 | tf_op jit(solution)/shard_map/ppermute | solution.py:65
  159.8 41.6 %collective-permute-start.21 = (bf16[192,1536]{1,0:T(8,128)(2,1)}, bf16[192,1536]{1,0:T(8,128)(2,1)}, u32[]{:S(2)}, u32[]{:S(2)}) collective-permute-start(bf16[192,1536]{1,0:T(8,128)(2,1)} %add_convert_fusion.1.refs_0_), channel_id=1, source_target_pairs={{0,8},{8,0},{16,24},{24,16},{1,9},{9,1},{17,25},{25,17},{2,10},{10... | collective-permute-start | bytes 1769480 | tf_op jit(solution)/shard_map/ppermute | solution.py:65
  230.0 21.5 %collective-permute-start.28 = (f32[4,96,2048]{2,1,0:T(8,128)}, f32[4,96,2048]{2,1,0:T(8,128)}, u32[]{:S(2)}, u32[]{:S(2)}) collective-permute-start(f32[4,96,2048]{2,1,0:T(8,128)} %dynamic-slice_bitcast_fusion), channel_id=1, source_target_pairs={{0,1},{1,0},{2,3},{3,2},{4,5},{5,4},{6,7},{7,6},{8,9},{9,8},{10,11... | collective-permute-start | bytes 9437192 | tf_op jit(solution)/shard_map/ppermute | solution.py:62
  255.6 15.1 %collective-permute-start.29 = (bf16[96,2048]{1,0:T(8,128)(2,1)S(1)}, bf16[96,2048]{1,0:T(8,128)(2,1)}, u32[]{:S(2)}, u32[]{:S(2)}) collective-permute-start(bf16[96,2048]{1,0:T(8,128)(2,1)S(1)} %fusion.6), channel_id=1, source_target_pairs={{0,2},{1,3},{2,6},{3,7},{6,4},{7,5},{4,0},{5,1},{8,10},{9,11},{10,... | collective-permute-start | bytes 1179656 | tf_op jit(solution)/shard_map/ppermute | solution.py:69
  273.0 16.0 %collective-permute-start.30 = (bf16[96,2048]{1,0:T(8,128)(2,1)S(1)}, bf16[96,2048]{1,0:T(8,128)(2,1)}, u32[]{:S(2)}, u32[]{:S(2)}) collective-permute-start(bf16[96,2048]{1,0:T(8,128)(2,1)S(1)} %fusion.5), channel_id=1, source_target_pairs={{0,2},{1,3},{2,6},{3,7},{6,4},{7,5},{4,0},{5,1},{8,10},{9,11},{10,... | collective-permute-start | bytes 1179656 | tf_op jit(solution)/shard_map/ppermute | solution.py:69
  291.2 12.0 %collective-permute-start.31 = (bf16[96,2048]{1,0:T(8,128)(2,1)S(1)}, bf16[96,2048]{1,0:T(8,128)(2,1)}, u32[]{:S(2)}, u32[]{:S(2)}) collective-permute-start(bf16[96,2048]{1,0:T(8,128)(2,1)S(1)} %fusion.3), channel_id=1, source_target_pairs={{0,2},{1,3},{2,6},{3,7},{6,4},{7,5},{4,0},{5,1},{8,10},{9,11},{10,... | collective-permute-start | bytes 1179656 | tf_op jit(solution)/shard_map/ppermute | solution.py:69
  (15 other events, 133.9 us)
Sparse Core Ops, SparseCore 0:
  81.5 34.5 all-gather.1

commit v6 on v5

--- a/solution.py
+++ b/solution.py
@@ -112,31 +112,13 @@
         for_2 = jnp.concatenate([self.block(2, 0, half) + by_1, self.block(2, half, half)], axis=0).astype(BF16)
         self.terms = self.send(for_1, for_2, others)
 
-    def back(self, others, zero=0.0):
+    def back(self, zero=0.0):
         mine = self.block(0, 0, self.part) + self.terms[0].astype(F32) + self.terms[1].astype(F32)
         self.mine = (mine + zero).astype(BF16)
-        self.near = self.send(self.mine, self.mine, others)
-
-    def across(self, others, zero=0.0):
-        for_1, for_2 = self.near[1][self.half :], self.near[0][: self.half]
-        self.far = self.send(for_1 + jnp.asarray(zero, BF16), for_2 + jnp.asarray(zero, BF16), others)
-
-    def back_at_once(self):
-        mine = self.block(0, 0, self.part) + self.terms[0].astype(F32) + self.terms[1].astype(F32)
-        self.mine = mine.astype(BF16)
-        self.near = self.send(self.mine, self.mine, [])
-        self.far = self.axes.to_pipe(self.mine, 3)
+        self.others = [(self.axes.to_pipe(self.mine, r), r, 0) for r in (1, 2, 3)]
 
     def result(self):
-        if not isinstance(self.far, tuple):
-            return [(self.mine, 0, 0), (self.near[0], 1, 0), (self.near[1], 2, 0), (self.far, 3, 0)]
-        return [
-            (self.mine, 0, 0),
-            (self.near[0], 1, 0),
-            (self.near[1], 2, 0),
-            (self.far[1], 3, 0),
-            (self.far[0], 3, self.half),
-        ]
+        return [(self.mine, 0, 0), *self.others]
 
 
 def sigmoid(g):
@@ -144,14 +126,12 @@
 
 
 def grads_kernel(cfg, at_rows, *refs):
-    refs = list(refs)
-    take = lambda n: [refs.pop(0) for _ in range(n)]
-    parts = take(len(cfg["sources"]))
-    gate_pre, up_pre, gate_w, up_w, gate_m, up_m = take(6)
-    acc_in = take(1)[0] if cfg["acc_in"] else None
-    gate_out, up_out, acc, hidden, both = refs
+    count = len(cfg["sources"])
+    parts = refs[:count]
+    gate_pre, up_pre, gate_w, up_w, gate_m, up_m = refs[count : count + 6]
+    acc_in = refs[count + 6 : count + 10] if cfg["acc_in"] else None
+    out, *acc, hidden, both = refs[-7:]
     step, tok, chunk = cfg["step"], cfg["tok"], cfg["chunk"]
-    k = pl.program_id(0)
     place = at_rows[cfg["groups"]]
 
     for (r, first), ref in zip(cfg["sources"], parts):
@@ -159,47 +139,41 @@
         hidden[pl.ds(pl.multiple_of(to, 16), ref.shape[0]), :] = ref[...]
     for i in range(cfg["groups"]):
         at = pl.ds(pl.multiple_of(at_rows[i], 16), tok)
+        rows = slice(i * tok, (i + 1) * tok)
         g = gate_pre[at, :].astype(F32)
         u = up_pre[at, :].astype(F32)
-        h = hidden[i * tok : (i + 1) * tok, :].astype(F32)
+        h = hidden[rows, :].astype(F32)
         sig = sigmoid(g)
         h = h * sig
         gg = (h * u * (1.0 + g * (1.0 - sig))).astype(BF16)
         ug = (h * g).astype(BF16)
-        gate_out[at, :] = gg
-        up_out[at, :] = ug
-        both[at, :step] = gg
-        both[at, step:] = ug
-
-    def tile(n, first):
-        def masked(w, m):
-            rows = []
-            for i in range(chunk // BLOCK):
-                at = pl.ds(pl.multiple_of(n * chunk + i * BLOCK, BLOCK), BLOCK)
-                rows.append(w[at, :] * m[pl.ds(n * (chunk // BLOCK) + i, 1), :].astype(BF16))
-            return jnp.concatenate(rows, axis=0)
-
-        w = jnp.concatenate([masked(gate_w, gate_m), masked(up_w, up_m)], axis=1)
-        to = pl.ds(pl.multiple_of(n * chunk, chunk), chunk)
+        out[at, :step] = gg
+        out[at, step:] = ug
+        both[rows, :step] = gg
+        both[rows, step:] = ug
+
+    @pl.when(pl.program_id(0) == 0)
+    def _():
+        for i, ref in enumerate(acc):
+            ref[...] = jnp.zeros_like(ref) if acc_in is None else acc_in[i][...]
+
+    def masked(w, m, at):
+        rows = [
+            w[at + i : at + i + BLOCK, :] * m[(at + i) // BLOCK : (at + i) // BLOCK + 1, :].astype(BF16)
+            for i in range(0, chunk, BLOCK)
+        ]
+        return jnp.concatenate(rows, axis=0)
+
+    for at in range(0, cfg["width"], chunk):
+        w = jnp.concatenate([masked(gate_w, gate_m, at), masked(up_w, up_m, at)], axis=1)
         term = lax.dot_general(both[...], w, NT, preferred_element_type=F32)
-        if not first:
-            term += acc[:, to]
-        elif acc_in is not None:
-            term += acc_in[:, to]
-        acc[:, to] = term
-
-    tiles = cfg["width"] // chunk
-
-    @pl.when(k == 0)
-    def _():
-        pl.loop(0, tiles)(lambda n: tile(n, True))
-
-    @pl.when(k > 0)
-    def _():
-        pl.loop(0, tiles)(lambda n: tile(n, False))
-
-
-def local_grads(axes, at_rows, sources, gate_pre, up_pre, gate_w, up_w, gate_m, up_m, acc, tok, start, cols):
+        lo = 0
+        for ref in acc:
+            ref[:, at : at + chunk] += term[lo : lo + ref.shape[0], :]
+            lo += ref.shape[0]
+
+
+def local_grads(axes, at_rows, sources, gate_pre, up_pre, gate_w, up_w, gate_m, up_m, acc, tok, start, cols, ties):
     tokens, hid = gate_pre.shape
     width = gate_w.shape[0]
     step = step_of(hid)
@@ -207,26 +181,30 @@
     col = lambda k, _: (0, first + k)
     one = lambda k, _: (0, 0)
     own = lambda k, _: (0, k)
+    groups = [tok, tok, tokens // 2 - tok, tokens // 2 - tok]
     specs = [pl.BlockSpec((a.shape[0], step), own) for a, _, _ in sources]
     specs += [pl.BlockSpec((tokens, step), col)] * 2
     specs += [pl.BlockSpec((width, step), col)] * 2
     specs += [pl.BlockSpec((gate_m.shape[0], step), col)] * 2
     arrays = [a for a, _, _ in sources] + [gate_pre, up_pre, gate_w, up_w, gate_m, up_m]
     if acc is not None:
-        specs.append(pl.BlockSpec((tokens, width), one, pipeline_mode=pl.Buffered(1)))
-        arrays.append(acc)
+        specs += [pl.BlockSpec((n, width), one, pipeline_mode=pl.Buffered(1)) for n in groups]
+        arrays += acc
+    specs += [pl.BlockSpec(memory_space=pl.ANY)] * len(ties)
+    arrays += ties
     cfg = dict(
         sources=[(r, lo) for _, r, lo in sources], part=tokens // axes.pipe, groups=tokens // tok, tok=tok, step=step,
         width=width, chunk=chunk_of(width, 1024), acc_in=acc is not None,
     )
-    return pl.pallas_call(
+    out = pl.pallas_call(
         functools.partial(grads_kernel, cfg),
-        out_shape=[jax.ShapeDtypeStruct((tokens, cols), BF16)] * 2 + [jax.ShapeDtypeStruct((tokens, width), F32)],
+        out_shape=[jax.ShapeDtypeStruct((tokens, 2 * cols), BF16)]
+        + [jax.ShapeDtypeStruct((n, width), F32) for n in groups],
         grid_spec=pltpu.PrefetchScalarGridSpec(
             num_scalar_prefetch=1,
             grid=(cols // step,),
             in_specs=specs,
-            out_specs=[pl.BlockSpec((tokens, step), own)] * 2 + [pl.BlockSpec((tokens, width), one)],
+            out_specs=[pl.BlockSpec((tokens, 2 * step), own)] + [pl.BlockSpec((n, width), one) for n in groups],
             scratch_shapes=[pltpu.VMEM((tokens, step), BF16), pltpu.VMEM((tokens, 2 * step), BF16)],
         ),
         compiler_params=params(),
@@ -237,45 +215,43 @@
         ),
         name="local_grads",
     )(at_rows, *arrays)
-
-
-def weights_kernel(cfg, x, gate, up, gate_m, up_m, *refs):
-    *outs, done = refs[-3:]
+    return out[0], list(out[1:])
+
+
+def weights_kernel(cfg, x, grads, gate_m, up_m, *refs):
+    gate_out, up_out, done = refs[-3:]
     done[...] = jnp.zeros_like(done)
-    chunk = cfg["chunk"]
-    for g, m, out in ((gate, gate_m, outs[0]), (up, up_m, outs[1])):
-
-        def tile(n, g=g, m=m, out=out):
-            at = pl.ds(pl.multiple_of(n * chunk, chunk), chunk)
-            term = lax.dot_general(x[at, :], g[...], NN, preferred_element_type=F32)
-            for i in range(chunk // BLOCK):
-                to = pl.ds(pl.multiple_of(n * chunk + i * BLOCK, BLOCK), BLOCK)
-                row = m[pl.ds(n * (chunk // BLOCK) + i, 1), :]
-                out[to, :] = (term[i * BLOCK : (i + 1) * BLOCK, :] * row).astype(BF16)
-
-        pl.loop(0, cfg["width"] // chunk)(tile)
-
-
-def weight_grads(x_t, gate, up, gate_m, up_m, before, shape, start, skip, steps):
+    chunk, step = cfg["chunk"], cfg["step"]
+    for at in range(0, cfg["width"], chunk):
+        term = lax.dot_general(x[at : at + chunk, :], grads[...], NN, preferred_element_type=F32)
+        for i in range(0, chunk, BLOCK):
+            rows = slice(at + i, at + i + BLOCK)
+            block = (at + i) // BLOCK
+            gate_out[rows, :] = (term[i : i + BLOCK, :step] * gate_m[block : block + 1, :]).astype(BF16)
+            up_out[rows, :] = (term[i : i + BLOCK, step:] * up_m[block : block + 1, :]).astype(BF16)
+
+
+def weight_grads(x_t, grads, gate_m, up_m, before, shape, start, skip, steps, ties):
     width, tokens = x_t.shape
     step = step_of(shape[1])
     first = start // step + skip
     col = lambda k: (0, first + k)
     specs = [
         pl.BlockSpec((width, tokens), lambda k: (0, 0), pipeline_mode=pl.Buffered(1)),
-        pl.BlockSpec((tokens, step), lambda k: (0, skip + k)),
-        pl.BlockSpec((tokens, step), lambda k: (0, skip + k)),
+        pl.BlockSpec((tokens, 2 * step), lambda k: (0, skip + k)),
         pl.BlockSpec((gate_m.shape[0], step), col),
         pl.BlockSpec((gate_m.shape[0], step), col),
     ]
-    arrays = [x_t, gate, up, gate_m, up_m]
+    arrays = [x_t, grads, gate_m, up_m]
     alias = {}
     if before is not None:
         specs += [pl.BlockSpec(memory_space=pl.ANY)] * 2
         arrays += list(before)
-        alias = {5: 0, 6: 1}
-    return pl.pallas_call(
-        functools.partial(weights_kernel, dict(width=width, chunk=chunk_of(width, 1024))),
+        alias = {4: 0, 5: 1}
+    specs += [pl.BlockSpec(memory_space=pl.ANY)] * len(ties)
+    arrays += ties
+    *out, done = pl.pallas_call(
+        functools.partial(weights_kernel, dict(width=width, chunk=chunk_of(width, 512), step=step)),
         out_shape=[jax.ShapeDtypeStruct(shape, BF16)] * 2 + [jax.ShapeDtypeStruct((8, 128), F32)],
         grid=(steps,),
         in_specs=specs,
@@ -289,6 +265,7 @@
         ),
         name="weight_grads",
     )(*arrays)
+    return out, done
 
 
 def down_kernel(cfg, at_rows, *refs):
@@ -304,17 +281,15 @@
     across = hidden[...].T
     chunk = cfg["chunk"]
 
-    def tile(n):
-        at = pl.ds(pl.multiple_of(n * chunk, chunk), chunk)
+    for lo in range(0, cfg["width"], chunk):
+        at = slice(lo, lo + chunk)
         term = lax.dot_general(across, rows[:, at], NN, preferred_element_type=F32)
         for i in range(cfg["step"] // BLOCK):
             part = slice(i * BLOCK, (i + 1) * BLOCK)
             out[part, at] = (term[part, :] * mask[i, :, at]).astype(BF16)
 
-    pl.loop(0, cfg["width"] // chunk)(tile)
-
-
-def down_grad(at_rows, rows, gate_pre, up_pre, mask, tok, before, first, last):
+
+def down_grad(at_rows, rows, gate_pre, up_pre, mask, tok, before, first, last, ties):
     tokens, hid = gate_pre.shape
     width = rows.shape[1]
     step = step_of(hid)
@@ -328,6 +303,8 @@
         specs.append(pl.BlockSpec(memory_space=pl.ANY))
         arrays.append(before)
         alias = {len(arrays): 0}
+    specs += [pl.BlockSpec(memory_space=pl.ANY)] * len(ties)
+    arrays += ties
     cols = (last - first) * step
     return pl.pallas_call(
         functools.partial(down_kernel, cfg),
@@ -367,8 +344,8 @@
     tok, width = out_grad.shape
     step = step_of(hid)
     steps = hid // step
-    first = (steps + 1) // 2 * step
-    pieces = [(0, first), (first, hid - first)]
+    counts = [2, steps - 4, 2] if steps > 4 else [steps]
+    pieces = [(sum(counts[:i]) * step, n * step) for i, n in enumerate(counts)]
     at_rows = axes.rows(tok)
     gate_m = jnp.repeat(gate_mask, BLOCK, axis=1).astype(F32)
     up_m = jnp.repeat(up_mask, BLOCK, axis=1).astype(F32)
@@ -379,14 +356,15 @@
     half = tok // 2
     now, got = [out_grad[:half], out_grad[half:]], []
     for s in range(axes.chips - 1):
-        if s == 2:
-            now = lax.optimization_barrier((*now, downs[0]))[:2]
+        if s == 1:
+            now[1] = after(now[1], *downs)
         now = [axes.to_next(a) for a in now]
         got += now
     rows = jnp.concatenate(near + got + [axes.to_core(a) for a in got], axis=0)
 
     x = lax.all_gather(after(layer_input, rows), "tensor", axis=0, tiled=True)
     down = functools.partial(down_grad, rows=rows, gate_pre=gate_pre, up_pre=up_pre, mask=down_m[:, None, :], tok=tok)
+    half_steps = (steps + 1) // 2
     if axes.pipe == 4:
         squares = []
         for i, d in enumerate(downs):
@@ -394,55 +372,58 @@
             sq = Square(axes, dot_nt(after(rows, *prev.by) if i else rows, d))
             squares.append(sq)
             sq.corner(prev.by if i else [])
+            sq.sides(prev.terms if i else [])
             if not i:
-                grad_down, done = down(after(at_rows, *sq.by), before=None, first=0, last=(steps + 1) // 2)
-            sq.sides(prev.terms if i else [])
-            if i:
-                sq.back_at_once()
-                continue
-            sq.back([], done[0, 0])
-            grad_down, done = down(after(at_rows, *sq.terms), before=grad_down, first=(steps + 1) // 2, last=steps)
-            sq.across([], done[0, 0])
-        at_rows = at_rows + nothing(squares[-1].mine).astype(jnp.int32)
+                grad_down, done = down(at_rows, before=None, first=0, last=half_steps, ties=list(sq.by))
+            sq.back(0.0 if i else done[0, 0])
         sums = [sq.result() for sq in squares]
     else:
-        parts = [dot_nt(rows, d) for d in downs]
-        sums = [reduce_over_pipe(axes, p) for p in parts]
-        grad_down, _ = down(after(at_rows, *parts), before=None, first=0, last=steps)
+        sums = [reduce_over_pipe(axes, dot_nt(rows, d)) for d in downs]
+        grad_down, done = down(at_rows, before=None, first=0, last=half_steps, ties=[])
     x_t = x.T
-    at_rows = at_rows + nothing(x_t).astype(jnp.int32)
-
-    acc, grads = None, []
-    for (c, w), sources in zip(pieces, sums):
-        gate, up, acc = local_grads(
-            axes, at_rows, sources, gate_pre, up_pre, gate_weight, up_weight, gate_m, up_m, acc, tok, c, w
+
+    acc, grads, weights, waits = None, [], None, []
+    for i, ((c, w), sources) in enumerate(zip(pieces, sums)):
+        if i + 1 < len(sums):
+            waits = waits + [sums[i + 1][0][0]]
+        both, acc = local_grads(
+            axes, at_rows, sources, gate_pre, up_pre, gate_weight, up_weight, gate_m, up_m, acc, tok, c, w, waits
         )
-        grads.append((gate, up))
-
-    core = lax.axis_index("tensor") % 2
-    slots = axes.slots()
-    by_core = acc.reshape(axes.chips, 2, tok, width)
-    pick = lambda a, i, axis: lax.dynamic_index_in_dim(a, i, axis, keepdims=False)
-    total = pick(by_core, core, 1) + axes.to_core(pick(by_core, 1 - core, 1))
-
-    todo = [(c, g, skip, min(2, w // step - skip)) for (c, w), g in zip(pieces, grads) for skip in range(0, w // step, 2)]
-    weights = None
-
-    def weights_part(zero):
-        nonlocal weights
-        c, (gate, up), skip, count = todo.pop(0)
-        weights = weight_grads(x_t, gate, up, gate_m, up_m + zero, weights, gate_weight.shape, c, skip, count)
-        *weights, done = weights
-        return done[0, 0]
-
-    weights_part(0.0)
-    run = pick(total, slots[1 % axes.chips], 0).astype(BF16)
+        grads.append(both)
+        waits = []
+        if not i:
+            weights, ready = weight_grads(
+                x_t, both, gate_m, up_m, None, gate_weight.shape, c, 0, w // step, []
+            )
+            waits = [ready]
+
+    todo = [(i, skip) for i in reversed(range(1, len(pieces))) for skip in range(0, pieces[i][1] // step, 2)]
+    todo.insert(1, None)
+
+    def next_part(ties):
+        nonlocal weights, grad_down
+        part = todo.pop(0)
+        if part is None:
+            grad_down, _ = down(at_rows, before=grad_down, first=half_steps, last=steps, ties=ties)
+            return
+        i, skip = part
+        c, w = pieces[i]
+        weights, _ = weight_grads(
+            x_t, grads[i], gate_m, up_m, weights, gate_weight.shape, c, skip, min(2, w // step - skip), ties
+        )
+
+    near_own, near_other, far_own, far_other = acc
+    far_there, near_there = axes.to_core(far_other), axes.to_core(near_other)
+    next_part([])
+    run = (far_own[:tok] + far_there[:tok]).astype(BF16)
     for s in range(1, axes.chips):
-        zero = weights_part(nothing(run)) if todo else 0.0
-        run = axes.to_next(run).astype(F32) + pick(total, slots[(s + 1) % axes.chips], 0) + zero
-        run = run.astype(BF16)
+        if todo:
+            next_part([run])
+        at = slice(s * tok, (s + 1) * tok)
+        term = far_own[at] + far_there[at] if s < axes.chips - 1 else near_own + near_there
+        run = (axes.to_next(run).astype(F32) + term).astype(BF16)
     while todo:
-        weights_part(0.0)
+        next_part([])
     return (run, weights[0], weights[1], grad_down)
 
 

time: 314 us -> 306 us (0.975)
  waiting for transfers between devices: 38.8 us -> 58.7 us
  other arithmetic: 46.7 us -> 29.5 us
  local copies, waits for them, and re-layouts: 34.9 us -> 22 us
  starting transfers between devices: 25.7 us -> 37.2 us
  between operations: 25.7 us -> 14.9 us
    ppermute x15 -> x21, waiting for transfers between devices: 18.2 us -> 36.5 us  [to_pipe(): return lax.ppermute(x, 'pipe', [(i, i ^ bit) for i in range(self.pipe)])]
    add x7 -> x0, other arithmetic: 10.4 us -> none  [the longest x1 3.56 us: shards(): total = pick(by_core, core, 1) + axes.to_core(pick(by_core, 1 - core, 1))]
    ppermute x15 -> x21, starting transfers between devices: 15.8 us -> 25.5 us  [to_pipe(): return lax.ppermute(x, 'pipe', [(i, i ^ bit) for i in range(self.pipe)])]
    slice x11 -> x1, local copies, waits for them, and re-layouts: 9.22 us -> 1.38 us  [shards(): sq.back(0.0 if i else done[0, 0])]
    pallas_call x2 -> x3, Pallas kernels: 51.5 us -> 59.1 us  [local_grads(): pl.pallas_call(functools.partial(grads_kernel, cfg), out_shape=[jax.Shape...]
    pallas_call x4, Pallas kernels: 46.3 us -> 40.8 us  [weight_grads(): pl.pallas_call(functools.partial(weights_kernel, dict(width=width, chunk=...]
    ppermute x8 -> x9, waiting for transfers between devices: 1 us -> 5.23 us  [to_core(): return lax.ppermute(x, 'tensor', [(t, t ^ 1) for t in range(self.tensor)])]
    squeeze x1 -> x0, local copies, waits for them, and re-layouts: 3.92 us -> none  [shards(): lax.dynamic_index_in_dim(a, i, axis, keepdims=False)]
  transfers between devices with their start and end apart: 33 -> 40, of which waited for: 11 -> 15; matrix products, arithmetic and copies ran while one was open for 21% -> 19% of each run, Pallas kernels for 32% -> 35%
where the time goes in v6:
time: 306 us; the launch traced here: 302 us
  Pallas kernels  124 us (41%)
  waiting for transfers between devices  58.7 us (19%)
  starting transfers between devices  37.2 us (12%)
  other arithmetic  29.5 us (10%)
  local copies, waits for them, and re-layouts  22 us (7%)
  matrix products  16.3 us (5%)
  between operations  14.9 us (5%)
    pallas_call x3, Pallas kernels, local_grads(): pl.pallas_call(functools.partial(grads_kernel, cfg), out_shape=[jax.Shape...  59.1 us
    pallas_call x4, Pallas kernels, weight_grads(): pl.pallas_call(functools.partial(weights_kernel, dict(width=width, chunk=...  40.8 us
    ppermute x21, waiting for transfers between devices, to_pipe(): return lax.ppermute(x, 'pipe', [(i, i ^ bit) for i in range(self.pipe)])  36.5 us
    ppermute x21, starting transfers between devices, to_pipe(): return lax.ppermute(x, 'pipe', [(i, i ^ bit) for i in range(self.pipe)])  25.5 us
    pallas_call x2, Pallas kernels, down_grad(): pl.pallas_call(functools.partial(down_kernel, cfg), out_shape=[jax.ShapeD...  23.9 us
    ppermute x9, waiting for transfers between devices, to_next(): lax.ppermute(x, 'tensor', [(2 * a + k, 2 * b + k) for a, b in pairs for k...  16.9 us
    dot_general x3, matrix products, dot_nt(): return lax.dot_general(a, b, NT, preferred_element_type=F32)  16.3 us
    mul x2, other arithmetic, masked(): weight.reshape(rows // BLOCK, BLOCK, cols) * mask.astype(BF16)[:, None, :]  11.8 us
  transfers between devices with their start and end apart: 40, of which 15 were waited for; matrix products, arithmetic and copies ran while one was open for 19% of the time, Pallas kernels for 35%

profile of v6, /device:TPU:0, one launch (start us, length us, event | category | flops | bytes accessed | tf_op | source)
XLA Modules:
  0.0 302.4 jit_solution(16546563879390978490)
XLA Ops:
  7.7 1.7 fusion.6
  9.5 2.6 collective-permute-start.1
  12.0 2.6 collective-permute-start.2
  19.3 5.9 %bitcast_multiply_fusion = bf16[1536,2048]{1,0:T(8,128)(2,1)} fusion(bf16[3584,2048]{1,0:T(8,128)(2,1)} %param.17, bf16[12,2048]{1,0:T(8,128)(2,1)S(1)} %bitcast.47), kind=kLoop, calls=%fused_computation | loop fusion | flops 3145728 | bytes 12632064 | tf_op jit(solution)/shard_map/mul | solution.py:335
  25.2 5.9 %bitcast_multiply_fusion.1 = (bf16[1024,2048]{1,0:T(8,128)(2,1)}, bf16[1024,2048]{1,0:T(8,128)(2,1)}) fusion(bf16[3584,2048]{1,0:T(8,128)(2,1)} %param.17, bf16[8,2048]{1,0:T(8,128)(2,1)S(1)} %get-tuple-element.112, bf16[8,2048]{1,0:T(8,128)(2,1)S(1)} %get-tuple-element.113), kind=kLoop, calls=%fused_computation.1 | loop fusion | flops 4194304 | bytes 16842752 | tf_op jit(solution)/shard_map/mul | solution.py:335
  33.0 7.8 %collective-permute-done.3 = bf16[48,2048]{1,0:T(8,128)(2,1)S(1)} collective-permute-done((bf16[48,2048]{1,0:T(8,128)(2,1)}, bf16[48,2048]{1,0:T(8,128)(2,1)S(1)}, u32[]{:S(2)}, u32[]{:S(2)}) %collective-permute-start.3) | collective-permute-done | bytes 196640 | tf_op jit(solution)/shard_map/ppermute | solution.py:69
  45.5 2.6 collective-permute-done.5
  48.1 4.6 %collective-permute-done.6 = bf16[48,2048]{1,0:T(8,128)(2,1)S(1)} collective-permute-done((bf16[48,2048]{1,0:T(8,128)(2,1)S(1)}, bf16[48,2048]{1,0:T(8,128)(2,1)S(1)}, u32[]{:S(2)}, u32[]{:S(2)}) %collective-permute-start.6) | collective-permute-done | bytes 196640 | tf_op jit(solution)/shard_map/ppermute | solution.py:69
  54.5 3.6 %fusion.9 = f32[768,1024]{1,0:T(8,128)S(1)} fusion(bf16[768,2048]{1,0:T(8,128)(2,1)S(1)} %constant_dynamic-update-slice_fusion.refs_0_, bf16[1024,2048]{1,0:T(8,128)(2,1)S(1)} %copy-done.1), kind=kOutput, calls=%fused_computation.67 | convolution fusion | flops 3221225472 | bytes 10485760 | tf_op jit(solution)/shard_map/dot_general | solution.py:339
  63.7 2.0 concatenate.30.at_rows
  65.7 2.4 collective-permute-done.13.refs_4_
  69.2 7.4 %fusion.10 = f32[768,1536]{1,0:T(8,128)S(1)} fusion(bf16[768,2048]{1,0:T(8,128)(2,1)S(1)} %constant_dynamic-update-slice_fusion.refs_0_, bf16[1536,2048]{1,0:T(8,128)(2,1)} %bitcast_multiply_fusion), kind=kOutput, calls=%fused_computation.68 | convolution fusion | flops 4831838208 | bytes 14155776 | tf_op jit(solution)/shard_map/dot_general | solution.py:339
  85.6 13.2 %down_grad.2 = (bf16[3584,2048]{1,0:T(8,128)(2,1)}, f32[8,128]{1,0:T(8,128)}) custom-call(s32[9]{0:T(128)} %concatenate.30.at_rows, bf16[768,2048]{1,0:T(8,128)(2,1)} %copy-done.2, bf16[768,3584]{1,0:T(8,128)(2,1)} %refs_1_.3, bf16[768,3584]{1,0:T(8,128)(2,1)} %refs_2_.3, f32[28,1,2048]{2,1,0:T(1,128)} %bitcast.45, ...), custom_call_target="tpu_custom_call" | custom-call | flops 6442450944 | bytes 17825792 | tf_op jit(solution)/shard_map/down_grad/pallas_call | solution.py:309
  100.2 5.3 %fusion.11 = f32[768,1024]{1,0:T(8,128)S(1)} fusion(bf16[768,2048]{1,0:T(8,128)(2,1)S(1)} %copy-done.3, bf16[1024,2048]{1,0:T(8,128)(2,1)} %get-tuple-element.82), kind=kOutput, calls=%fused_computation.69 | convolution fusion | flops 3221225472 | bytes 10485760 | tf_op jit(solution)/shard_map/dot_general | solution.py:339
  109.0 1.7 collective-permute-start.21
  111.2 2.1 add_convert_fusion.2.refs_0_
  118.5 7.7 %collective-permute-done.21 = bf16[192,1536]{1,0:T(8,128)(2,1)S(1)} collective-permute-done((bf16[192,1536]{1,0:T(8,128)(2,1)S(1)}, bf16[192,1536]{1,0:T(8,128)(2,1)S(1)}, u32[]{:S(2)}, u32[]{:S(2)}) %collective-permute-start.21) | collective-permute-done | bytes 589856 | tf_op jit(solution)/shard_map/ppermute | solution.py:65
  130.0 4.5 %collective-permute-done.31.refs_1_ = bf16[192,1024]{1,0:T(8,128)(2,1)S(1)} collective-permute-done((bf16[192,1024]{1,0:T(8,128)(2,1)S(1)}, bf16[192,1024]{1,0:T(8,128)(2,1)S(1)}, u32[]{:S(2)}, u32[]{:S(2)}) %collective-permute-start.31) | collective-permute-done | bytes 393248 | tf_op jit(solution)/shard_map/ppermute | solution.py:65
  135.9 7.7 %collective-permute-done.32.refs_2_ = bf16[192,1024]{1,0:T(8,128)(2,1)S(1)} collective-permute-done((bf16[192,1024]{1,0:T(8,128)(2,1)S(1)}, bf16[192,1024]{1,0:T(8,128)(2,1)S(1)}, u32[]{:S(2)}, u32[]{:S(2)}) %collective-permute-start.32) | collective-permute-done | bytes 393248 | tf_op jit(solution)/shard_map/ppermute | solution.py:65
  146.6 16.3 %local_grads.3 = (bf16[768,2048]{1,0:T(8,128)(2,1)}, f32[96,2048]{1,0:T(8,128)}, f32[96,2048]{1,0:T(8,128)}, f32[288,2048]{1,0:T(8,128)}, f32[288,2048]{1,0:T(8,128)}) custom-call(s32[9]{0:T(128)} %concatenate.30.at_rows, bf16[192,1024]{1,0:T(8,128)(2,1)} %copy-done.10, bf16[192,1024]{1,0:T(8,128)(2,1)} %copy-done.19, bf16[192,1024]{1,0:T(8,128)(2,1)} %copy-done.20, ...), custom_call_target="tpu_custom_call" | custom-call | flops 6442450944 | bytes 28835840 | tf_op jit(solution)/shard_map/local_grads/pallas_call | solution.py:199
  162.9 12.1 %collective-permute-done.24 = bf16[192,1024]{1,0:T(8,128)(2,1)} collective-permute-done((bf16[192,1024]{1,0:T(8,128)(2,1)}, bf16[192,1024]{1,0:T(8,128)(2,1)}, u32[]{:S(2)}, u32[]{:S(2)}) %collective-permute-start.24) | collective-permute-done | bytes 393248 | tf_op jit(solution)/shard_map/ppermute | solution.py:65
  178.8 4.7 %copy.30 = bf16[768,2048]{0,1:T(8,128)(2,1)} copy(bf16[768,2048]{1,0:T(8,128)(2,1)} %all-gather.2.cloned.1.call-done) | data formatting | bytes 6291456 | tf_op jit(solution)/shard_map/all_gather | solution.py:365
  183.5 10.9 %weight_grads.4 = (bf16[2048,3584]{1,0:T(8,128)(2,1)}, bf16[2048,3584]{1,0:T(8,128)(2,1)}, f32[8,128]{1,0:T(8,128)}) custom-call(bf16[2048,768]{1,0:T(8,128)(2,1)} %bitcast.37, bf16[768,2048]{1,0:T(8,128)(2,1)} %get-tuple-element.60.grads, f32[16,3584]{1,0:T(8,128)} %get-tuple-element.115.refs_8_.gate_m, f32[16,3584]{1,0:T(8,128)} %get-tuple-element.114.refs_9_.up_m), custom_call_target="tpu_custom_call" | custom-call | flops 6442450944 | bytes 14680064 | tf_op jit(solution)/shard_map/weight_grads/pallas_call | solution.py:253
  196.9 23.8 %local_grads.4 = (bf16[768,3072]{1,0:T(8,128)(2,1)}, f32[96,2048]{1,0:T(8,128)}, f32[96,2048]{1,0:T(8,128)}, f32[288,2048]{1,0:T(8,128)}, f32[288,2048]{1,0:T(8,128)}) custom-call(s32[9]{0:T(128)} %concatenate.30.at_rows, bf16[192,1536]{1,0:T(8,128)(2,1)} %copy-done, bf16[192,1536]{1,0:T(8,128)(2,1)} %copy-done.16, bf16[192,1536]{1,0:T(8,128)(2,1)} %copy-done.17, ...), custom_call_target="tpu_custom_call" | custom-call | flops 9663676416 | bytes 36962304 | tf_op jit(solution)/shard_map/local_grads/pallas_call | solution.py:199
  221.8 18.9 %local_grads.5 = (bf16[768,2048]{1,0:T(8,128)(2,1)}, f32[96,2048]{1,0:T(8,128)}, f32[96,2048]{1,0:T(8,128)}, f32[288,2048]{1,0:T(8,128)}, f32[288,2048]{1,0:T(8,128)}) custom-call(s32[9]{0:T(128)} %concatenate.30.at_rows, bf16[192,1024]{1,0:T(8,128)(2,1)} %copy-done.4, bf16[192,1024]{1,0:T(8,128)(2,1)} %copy-done.22, bf16[192,1024]{1,0:T(8,128)(2,1)} %copy-done.23, ...), custom_call_target="tpu_custom_call" | custom-call | flops 6442450944 | bytes 28835840 | tf_op jit(solution)/shard_map/local_grads/pallas_call | solution.py:199
  241.3 4.2 %collective-permute-done.34 = f32[288,2048]{1,0:T(8,128)S(1)} collective-permute-done((f32[288,2048]{1,0:T(8,128)}, f32[288,2048]{1,0:T(8,128)S(1)}, u32[]{:S(2)}, u32[]{:S(2)}) %collective-permute-start.34) | collective-permute-done | bytes 2359328 | tf_op jit(solution)/shard_map/ppermute | solution.py:62
  245.5 1.8 fusion.4.refs_5_
  247.4 11.5 %weight_grads.5 = (bf16[2048,3584]{1,0:T(8,128)(2,1)}, bf16[2048,3584]{1,0:T(8,128)(2,1)}, f32[8,128]{1,0:T(8,128)}) custom-call(bf16[2048,768]{1,0:T(8,128)(2,1)} %bitcast.38, bf16[768,2048]{1,0:T(8,128)(2,1)} %get-tuple-element.71.grads, f32[16,3584]{1,0:T(8,128)} %get-tuple-element.115.refs_8_.gate_m, ...), custom_call_target="tpu_custom_call", output_to_operand_aliasing={{0}: (4, {}), {1}: (5, {})} | custom-call | flops 6442450944 | bytes 14680064 | tf_op jit(solution)/shard_map/weight_grads/pallas_call | solution.py:253
  261.6 10.8 %down_grad.3 = (bf16[3584,2048]{1,0:T(8,128)(2,1)}, f32[8,128]{1,0:T(8,128)}) custom-call(s32[9]{0:T(128)} %concatenate.30.at_rows, bf16[768,2048]{1,0:T(8,128)(2,1)} %copy-done.2, bf16[768,3584]{1,0:T(8,128)(2,1)} %refs_1_.3, bf16[768,3584]{1,0:T(8,128)(2,1)} %refs_2_.3, f32[28,1,2048]{2,1,0:T(1,128)} %bitcast.46, ...), custom_call_target="tpu_custom_call", output_to_operand_aliasing={{0}: (5, {})} | custom-call | flops 4831838208 | bytes 14155776 | tf_op jit(solution)/shard_map/down_grad/pallas_call | solution.py:309
  273.6 2.4 collective-permute-start.37
  276.0 11.0 %weight_grads.6 = (bf16[2048,3584]{1,0:T(8,128)(2,1)}, bf16[2048,3584]{1,0:T(8,128)(2,1)}, f32[8,128]{1,0:T(8,128)}) custom-call(bf16[2048,768]{1,0:T(8,128)(2,1)} %bitcast.39, bf16[768,3072]{1,0:T(8,128)(2,1)} %get-tuple-element.70.grads, f32[16,3584]{1,0:T(8,128)} %get-tuple-element.115.refs_8_.gate_m, ...), custom_call_target="tpu_custom_call", output_to_operand_aliasing={{0}: (4, {}), {1}: (5, {})} | custom-call | flops 6442450944 | bytes 14680064 | tf_op jit(solution)/shard_map/weight_grads/pallas_call | solution.py:253
  286.9 7.5 %weight_grads.7 = (bf16[2048,3584]{1,0:T(8,128)(2,1)}, bf16[2048,3584]{1,0:T(8,128)(2,1)}, f32[8,128]{1,0:T(8,128)}) custom-call(bf16[2048,768]{1,0:T(8,128)(2,1)} %bitcast.40, bf16[768,3072]{1,0:T(8,128)(2,1)} %get-tuple-element.70.grads, f32[16,3584]{1,0:T(8,128)} %get-tuple-element.115.refs_8_.gate_m, ...), custom_call_target="tpu_custom_call", output_to_operand_aliasing={{0}: (4, {}), {1}: (5, {})} | custom-call | flops 3221225472 | bytes 8912896 | tf_op jit(solution)/shard_map/weight_grads/pallas_call | solution.py:253
  (178 shorter events, 60.4 us)
Async XLA Ops:
  7.2 171.6 %all-gather.2.cloned.1.call-start = ((), (), s32[]{:S(2)}) async-start(), calls=%async_computation | async-start | bytes 3538944 | tf_op jit(solution)/shard_map/all_gather | solution.py:365
  7.2 33.5 %collective-permute-start = (bf16[96,2048]{1,0:T(8,128)(2,1)}, bf16[96,2048]{1,0:T(8,128)(2,1)}, u32[]{:S(2)}, u32[]{:S(2)}) collective-permute-start(bf16[96,2048]{1,0:T(8,128)(2,1)} %param.12), channel_id=1, source_target_pairs={{0,1},{1,0},{2,3},{3,2},{4,5},{5,4},{6,7},{7,6},{8,9},{9,8},{10,11... | collective-permute-start | bytes 1179656 | tf_op jit(solution)/shard_map/ppermute | solution.py:62
  9.5 22.3 %collective-permute-start.1 = (bf16[48,2048]{1,0:T(8,128)(2,1)S(1)}, bf16[48,2048]{1,0:T(8,128)(2,1)}, u32[]{:S(2)}, u32[]{:S(2)}) collective-permute-start(bf16[48,2048]{1,0:T(8,128)(2,1)S(1)} %get-tuple-element.103), channel_id=1, source_target_pairs={{0,2},{1,3},{2,6},{3,7},{6,4},{7,5},{4,0},{5,1},{8,10},{9,11},{10,... | collective-permute-start | bytes 589832 | tf_op jit(solution)/shard_map/ppermute | solution.py:69
  12.0 20.3 %collective-permute-start.2 = (bf16[48,2048]{1,0:T(8,128)(2,1)}, bf16[48,2048]{1,0:T(8,128)(2,1)}, u32[]{:S(2)}, u32[]{:S(2)}) collective-permute-start(bf16[48,2048]{1,0:T(8,128)(2,1)} %get-tuple-element.102), channel_id=1, source_target_pairs={{0,2},{1,3},{2,6},{3,7},{6,4},{7,5},{4,0},{5,1},{8,10},{9,11},{10,... | collective-permute-start | bytes 589832 | tf_op jit(solution)/shard_map/ppermute | solution.py:69
  31.8 8.9 %collective-permute-start.3 = (bf16[48,2048]{1,0:T(8,128)(2,1)}, bf16[48,2048]{1,0:T(8,128)(2,1)S(1)}, u32[]{:S(2)}, u32[]{:S(2)}) collective-permute-start(bf16[48,2048]{1,0:T(8,128)(2,1)} %collective-permute-done.1), channel_id=1, source_target_pairs={{0,2},{1,3},{2,6},{3,7},{6,4},{7,5},{4,0},{5,1},{8,10},{9,11},{10,... | collective-permute-start | bytes 589832 | tf_op jit(solution)/shard_map/ppermute | solution.py:69
  32.3 12.6 %collective-permute-start.4 = (bf16[48,2048]{1,0:T(8,128)(2,1)}, bf16[48,2048]{1,0:T(8,128)(2,1)S(1)}, u32[]{:S(2)}, u32[]{:S(2)}) collective-permute-start(bf16[48,2048]{1,0:T(8,128)(2,1)} %collective-permute-done.2), channel_id=1, source_target_pairs={{0,2},{1,3},{2,6},{3,7},{6,4},{7,5},{4,0},{5,1},{8,10},{9,11},{10,... | collective-permute-start | bytes 589832 | tf_op jit(solution)/shard_map/ppermute | solution.py:69
  32.4 20.4 %collective-permute-start.7 = (bf16[48,2048]{1,0:T(8,128)(2,1)}, bf16[48,2048]{1,0:T(8,128)(2,1)S(1)}, u32[]{:S(2)}, u32[]{:S(2)}) collective-permute-start(bf16[48,2048]{1,0:T(8,128)(2,1)} %collective-permute-done.1), channel_id=1, source_target_pairs={{0,1},{1,0},{2,3},{3,2},{4,5},{5,4},{6,7},{7,6},{8,9},{9,8},{10,11... | collective-permute-start | bytes 589832 | tf_op jit(solution)/shard_map/ppermute | solution.py:62
  32.5 20.9 %collective-permute-start.8 = (bf16[48,2048]{1,0:T(8,128)(2,1)}, bf16[48,2048]{1,0:T(8,128)(2,1)S(1)}, u32[]{:S(2)}, u32[]{:S(2)}) collective-permute-start(bf16[48,2048]{1,0:T(8,128)(2,1)} %collective-permute-done.2), channel_id=1, source_target_pairs={{0,1},{1,0},{2,3},{3,2},{4,5},{5,4},{6,7},{7,6},{8,9},{9,8},{10,11... | collective-permute-start | bytes 589832 | tf_op jit(solution)/shard_map/ppermute | solution.py:62
  40.7 12.7 %collective-permute-start.9 = (bf16[48,2048]{1,0:T(8,128)(2,1)S(1)}, bf16[48,2048]{1,0:T(8,128)(2,1)S(1)}, u32[]{:S(2)}, u32[]{:S(2)}) collective-permute-start(bf16[48,2048]{1,0:T(8,128)(2,1)S(1)} %collective-permute-done.3), channel_id=1, source_target_pairs={{0,1},{1,0},{2,3},{3,2},{4,5},{5,4},{6,7},{7,6},{8,9},{9,8},{10,11... | collective-permute-start | bytes 589832 | tf_op jit(solution)/shard_map/ppermute | solution.py:62
  77.8 22.3 %collective-permute-start.15 = (bf16[96,1536]{1,0:T(8,128)(2,1)}, bf16[96,1536]{1,0:T(8,128)(2,1)}, u32[]{:S(2)}, u32[]{:S(2)}) collective-permute-start(bf16[96,1536]{1,0:T(8,128)(2,1)} %get-tuple-element.45), channel_id=1, source_target_pairs={{0,8},{8,0},{16,24},{24,16},{1,9},{9,1},{17,25},{25,17},{2,10},{10... | collective-permute-start | bytes 884744 | tf_op jit(solution)/shard_map/ppermute | solution.py:65
  78.2 21.9 %collective-permute-start.16 = (bf16[96,1536]{1,0:T(8,128)(2,1)}, bf16[96,1536]{1,0:T(8,128)(2,1)}, u32[]{:S(2)}, u32[]{:S(2)}) collective-permute-start(bf16[96,1536]{1,0:T(8,128)(2,1)} %get-tuple-element.46), channel_id=1, source_target_pairs={{0,16},{8,24},{16,0},{24,8},{1,17},{9,25},{17,1},{25,9},{2,18},{10... | collective-permute-start | bytes 884744 | tf_op jit(solution)/shard_map/ppermute | solution.py:65
  81.9 27.0 %collective-permute-start.19 = (bf16[192,1024]{1,0:T(8,128)(2,1)}, bf16[192,1024]{1,0:T(8,128)(2,1)}, u32[]{:S(2)}, u32[]{:S(2)}) collective-permute-start(bf16[192,1024]{1,0:T(8,128)(2,1)} %pad_maximum_fusion.4), channel_id=1, source_target_pairs={{0,8},{8,0},{16,24},{24,16},{1,9},{9,1},{17,25},{25,17},{2,10},{10... | collective-permute-start | bytes 1179656 | tf_op jit(solution)/shard_map/ppermute | solution.py:65
  84.3 24.7 %collective-permute-start.20 = (bf16[192,1024]{1,0:T(8,128)(2,1)}, bf16[192,1024]{1,0:T(8,128)(2,1)S(1)}, u32[]{:S(2)}, u32[]{:S(2)}) collective-permute-start(bf16[192,1024]{1,0:T(8,128)(2,1)} %pad_maximum_fusion.5), channel_id=1, source_target_pairs={{0,16},{8,24},{16,0},{24,8},{1,17},{9,25},{17,1},{25,9},{2,18},{10... | collective-permute-start | bytes 1179656 | tf_op jit(solution)/shard_map/ppermute | solution.py:65
  105.7 8.0 %collective-permute-start.18 = (bf16[96,1024]{1,0:T(8,128)(2,1)S(1)}, bf16[96,1024]{1,0:T(8,128)(2,1)S(1)}, u32[]{:S(2)}, u32[]{:S(2)}) collective-permute-start(bf16[96,1024]{1,0:T(8,128)(2,1)S(1)} %get-tuple-element.49), channel_id=1, source_target_pairs={{0,8},{8,0},{16,24},{24,16},{1,9},{9,1},{17,25},{25,17},{2,10},{10... | collective-permute-start | bytes 589832 | tf_op jit(solution)/shard_map/ppermute | solution.py:65
  106.1 9.1 %collective-permute-start.17 = (bf16[96,1024]{1,0:T(8,128)(2,1)S(1)}, bf16[96,1024]{1,0:T(8,128)(2,1)S(1)}, u32[]{:S(2)}, u32[]{:S(2)}) collective-permute-start(bf16[96,1024]{1,0:T(8,128)(2,1)S(1)} %get-tuple-element.48), channel_id=1, source_target_pairs={{0,16},{8,24},{16,0},{24,8},{1,17},{9,25},{17,1},{25,9},{2,18},{10... | collective-permute-start | bytes 589832 | tf_op jit(solution)/shard_map/ppermute | solution.py:65
  109.0 17.2 %collective-permute-start.21 = (bf16[192,1536]{1,0:T(8,128)(2,1)S(1)}, bf16[192,1536]{1,0:T(8,128)(2,1)S(1)}, u32[]{:S(2)}, u32[]{:S(2)}) collective-permute-start(bf16[192,1536]{1,0:T(8,128)(2,1)S(1)} %pad_maximum_fusion), channel_id=1, source_target_pairs={{0,8},{8,0},{16,24},{24,16},{1,9},{9,1},{17,25},{25,17},{2,10},{10... | collective-permute-start | bytes 1769480 | tf_op jit(solution)/shard_map/ppermute | solution.py:65
  110.7 16.3 %collective-permute-start.22 = (bf16[192,1536]{1,0:T(8,128)(2,1)S(1)}, bf16[192,1536]{1,0:T(8,128)(2,1)S(1)}, u32[]{:S(2)}, u32[]{:S(2)}) collective-permute-start(bf16[192,1536]{1,0:T(8,128)(2,1)S(1)} %pad_maximum_fusion.1), channel_id=1, source_target_pairs={{0,16},{8,24},{16,0},{24,8},{1,17},{9,25},{17,1},{25,9},{2,18},{10... | collective-permute-start | bytes 1769480 | tf_op jit(solution)/shard_map/ppermute | solution.py:65
  113.2 21.3 %collective-permute-start.31 = (bf16[192,1024]{1,0:T(8,128)(2,1)S(1)}, bf16[192,1024]{1,0:T(8,128)(2,1)S(1)}, u32[]{:S(2)}, u32[]{:S(2)}) collective-permute-start(bf16[192,1024]{1,0:T(8,128)(2,1)S(1)} %add_convert_fusion.2.refs_0_), channel_id=1, source_target_pairs={{0,8},{8,0},{16,24},{24,16},{1,9},{9,1},{17,25},{25,17},{2,10},{10... | collective-permute-start | bytes 1179656 | tf_op jit(solution)/shard_map/ppermute | solution.py:65
  113.7 29.9 %collective-permute-start.32 = (bf16[192,1024]{1,0:T(8,128)(2,1)S(1)}, bf16[192,1024]{1,0:T(8,128)(2,1)S(1)}, u32[]{:S(2)}, u32[]{:S(2)}) collective-permute-start(bf16[192,1024]{1,0:T(8,128)(2,1)S(1)} %add_convert_fusion.2.refs_0_), channel_id=1, source_target_pairs={{0,16},{8,24},{16,0},{24,8},{1,17},{9,25},{17,1},{25,9},{2,18},{10... | collective-permute-start | bytes 1179656 | tf_op jit(solution)/shard_map/ppermute | solution.py:65
  115.2 29.7 %collective-permute-start.33 = (bf16[192,1024]{1,0:T(8,128)(2,1)S(1)}, bf16[192,1024]{1,0:T(8,128)(2,1)S(1)}, u32[]{:S(2)}, u32[]{:S(2)}) collective-permute-start(bf16[192,1024]{1,0:T(8,128)(2,1)S(1)} %add_convert_fusion.2.refs_0_), channel_id=1, source_target_pairs={{0,24},{8,16},{16,8},{24,0},{1,25},{9,17},{17,9},{25,1},{2,26},{10... | collective-permute-start | bytes 1179656 | tf_op jit(solution)/shard_map/ppermute | solution.py:65
  127.2 67.2 %collective-permute-start.28 = (bf16[192,1536]{1,0:T(8,128)(2,1)S(1)}, bf16[192,1536]{1,0:T(8,128)(2,1)S(1)}, u32[]{:S(2)}, u32[]{:S(2)}) collective-permute-start(bf16[192,1536]{1,0:T(8,128)(2,1)S(1)} %add_convert_fusion.refs_10_.refs_0_), channel_id=1, source_target_pairs={{0,8},{8,0},{16,24},{24,16},{1,9},{9,1},{17,25},{25,17},{2,10},{10... | collective-permute-start | bytes 1769480 | tf_op jit(solution)/shard_map/ppermute | solution.py:65
  128.4 67.5 %collective-permute-start.29 = (bf16[192,1536]{1,0:T(8,128)(2,1)S(1)}, bf16[192,1536]{1,0:T(8,128)(2,1)S(1)}, u32[]{:S(2)}, u32[]{:S(2)}) collective-permute-start(bf16[192,1536]{1,0:T(8,128)(2,1)S(1)} %add_convert_fusion.refs_10_.refs_0_), channel_id=1, source_target_pairs={{0,16},{8,24},{16,0},{24,8},{1,17},{9,25},{17,1},{25,9},{2,18},{10... | collective-permute-start | bytes 1769480 | tf_op jit(solution)/shard_map/ppermute | solution.py:65
  134.6 61.3 %collective-permute-start.30 = (bf16[192,1536]{1,0:T(8,128)(2,1)S(1)}, bf16[192,1536]{1,0:T(8,128)(2,1)S(1)}, u32[]{:S(2)}, u32[]{:S(2)}) collective-permute-start(bf16[192,1536]{1,0:T(8,128)(2,1)S(1)} %add_convert_fusion.refs_10_.refs_0_), channel_id=1, source_target_pairs={{0,24},{8,16},{16,8},{24,0},{1,25},{9,17},{17,9},{25,1},{2,26},{10... | collective-permute-start | bytes 1769480 | tf_op jit(solution)/shard_map/ppermute | solution.py:65
  143.6 31.4 %collective-permute-start.24 = (bf16[192,1024]{1,0:T(8,128)(2,1)}, bf16[192,1024]{1,0:T(8,128)(2,1)}, u32[]{:S(2)}, u32[]{:S(2)}) collective-permute-start(bf16[192,1024]{1,0:T(8,128)(2,1)} %pad_maximum_fusion.3), channel_id=1, source_target_pairs={{0,16},{8,24},{16,0},{24,8},{1,17},{9,25},{17,1},{25,9},{2,18},{10... | collective-permute-start | bytes 1179656 | tf_op jit(solution)/shard_map/ppermute | solution.py:65
  144.9 30.1 %collective-permute-start.23 = (bf16[192,1024]{1,0:T(8,128)(2,1)}, bf16[192,1024]{1,0:T(8,128)(2,1)}, u32[]{:S(2)}, u32[]{:S(2)}) collective-permute-start(bf16[192,1024]{1,0:T(8,128)(2,1)} %pad_maximum_fusion.2), channel_id=1, source_target_pairs={{0,8},{8,0},{16,24},{24,16},{1,9},{9,1},{17,25},{25,17},{2,10},{10... | collective-permute-start | bytes 1179656 | tf_op jit(solution)/shard_map/ppermute | solution.py:65
  176.6 44.1 %collective-permute-start.25 = (bf16[192,1024]{1,0:T(8,128)(2,1)S(1)}, bf16[192,1024]{1,0:T(8,128)(2,1)S(1)}, u32[]{:S(2)}, u32[]{:S(2)}) collective-permute-start(bf16[192,1024]{1,0:T(8,128)(2,1)S(1)} %add_convert_fusion.3.refs_15_.refs_0_), channel_id=1, source_target_pairs={{0,8},{8,0},{16,24},{24,16},{1,9},{9,1},{17,25},{25,17},{2,10},{10... | collective-permute-start | bytes 1179656 | tf_op jit(solution)/shard_map/ppermute | solution.py:65
  177.9 42.9 %collective-permute-start.26 = (bf16[192,1024]{1,0:T(8,128)(2,1)S(1)}, bf16[192,1024]{1,0:T(8,128)(2,1)S(1)}, u32[]{:S(2)}, u32[]{:S(2)}) collective-permute-start(bf16[192,1024]{1,0:T(8,128)(2,1)S(1)} %add_convert_fusion.3.refs_15_.refs_0_), channel_id=1, source_target_pairs={{0,16},{8,24},{16,0},{24,8},{1,17},{9,25},{17,1},{25,9},{2,18},{10... | collective-permute-start | bytes 1179656 | tf_op jit(solution)/shard_map/ppermute | solution.py:65
  194.4 26.4 %collective-permute-start.27 = (bf16[192,1024]{1,0:T(8,128)(2,1)S(1)}, bf16[192,1024]{1,0:T(8,128)(2,1)S(1)}, u32[]{:S(2)}, u32[]{:S(2)}) collective-permute-start(bf16[192,1024]{1,0:T(8,128)(2,1)S(1)} %add_convert_fusion.3.refs_15_.refs_0_), channel_id=1, source_target_pairs={{0,24},{8,16},{16,8},{24,0},{1,25},{9,17},{17,9},{25,1},{2,26},{10... | collective-permute-start | bytes 1179656 | tf_op jit(solution)/shard_map/ppermute | solution.py:65
  240.8 53.6 %collective-permute-start.38 = (f32[96,2048]{1,0:T(8,128)}, f32[96,2048]{1,0:T(8,128)S(1)}, u32[]{:S(2)}, u32[]{:S(2)}) collective-permute-start(f32[96,2048]{1,0:T(8,128)} %get-tuple-element.69), channel_id=1, source_target_pairs={{0,1},{1,0},{2,3},{3,2},{4,5},{5,4},{6,7},{7,6},{8,9},{9,8},{10,11... | collective-permute-start | bytes 2359304 | tf_op jit(solution)/shard_map/ppermute | solution.py:62
  247.3 12.2 %collective-permute-start.35 = (bf16[96,2048]{1,0:T(8,128)(2,1)S(1)}, bf16[96,2048]{1,0:T(8,128)(2,1)}, u32[]{:S(2)}, u32[]{:S(2)}) collective-permute-start(bf16[96,2048]{1,0:T(8,128)(2,1)S(1)} %fusion.4.refs_5_), channel_id=1, source_target_pairs={{0,2},{1,3},{2,6},{3,7},{6,4},{7,5},{4,0},{5,1},{8,10},{9,11},{10,... | collective-permute-start | bytes 1179656 | tf_op jit(solution)/shard_map/ppermute | solution.py:69
  260.9 11.5 %collective-permute-start.36 = (bf16[96,2048]{1,0:T(8,128)(2,1)S(1)}, bf16[96,2048]{1,0:T(8,128)(2,1)S(1)}, u32[]{:S(2)}, u32[]{:S(2)}) collective-permute-start(bf16[96,2048]{1,0:T(8,128)(2,1)S(1)} %fusion.3.refs_2_), channel_id=1, source_target_pairs={{0,2},{1,3},{2,6},{3,7},{6,4},{7,5},{4,0},{5,1},{8,10},{9,11},{10,... | collective-permute-start | bytes 1179656 | tf_op jit(solution)/shard_map/ppermute | solution.py:69
  273.6 20.8 %collective-permute-start.37 = (bf16[96,2048]{1,0:T(8,128)(2,1)S(1)}, bf16[96,2048]{1,0:T(8,128)(2,1)S(1)}, u32[]{:S(2)}, u32[]{:S(2)}) collective-permute-start(bf16[96,2048]{1,0:T(8,128)(2,1)S(1)} %fusion.1.refs_2_), channel_id=1, source_target_pairs={{0,2},{1,3},{2,6},{3,7},{6,4},{7,5},{4,0},{5,1},{8,10},{9,11},{10,... | collective-permute-start | bytes 1179656 | tf_op jit(solution)/shard_map/ppermute | solution.py:69
  (38 other events, 363.4 us)
Sparse Core Ops, SparseCore 0:
  65.8 35.7 all-gather.1

commit v7 on v6

--- a/solution.py
+++ b/solution.py
@@ -99,6 +99,7 @@
 
     def send(self, for_1, for_2, others):
         for_1, for_2 = lax.optimization_barrier((for_1, for_2, *others))[:2] if others else (for_1, for_2)
+        self.sent = (for_1, for_2)
         return self.axes.to_pipe(for_1, 1), self.axes.to_pipe(for_2, 2)
 
     def corner(self, others):
@@ -352,30 +353,41 @@
     down_m = jnp.repeat(down_mask, BLOCK, axis=1).astype(F32)
 
     near = [out_grad, axes.to_core(out_grad)]
-    downs = [masked(down_weight[c : c + w], down_m[c // BLOCK : (c + w) // BLOCK]) for c, w in pieces]
+    down_part = lambda c, w, m: masked(down_weight[c : c + w], m[c // BLOCK : (c + w) // BLOCK])
+    downs = [down_part(*pieces[0], down_m)]
     half = tok // 2
     now, got = [out_grad[:half], out_grad[half:]], []
     for s in range(axes.chips - 1):
         if s == 1:
+            later = after(down_m, now[0])
             now[1] = after(now[1], *downs)
+            downs += [down_part(c, w, later) for c, w in pieces[1:]]
+        if s == 2:
+            now[1] = after(now[1], *downs[1:])
         now = [axes.to_next(a) for a in now]
         got += now
+    if len(downs) < len(pieces):
+        downs += [down_part(c, w, down_m) for c, w in pieces[1:]]
     rows = jnp.concatenate(near + got + [axes.to_core(a) for a in got], axis=0)
 
     x = lax.all_gather(after(layer_input, rows), "tensor", axis=0, tiled=True)
     down = functools.partial(down_grad, rows=rows, gate_pre=gate_pre, up_pre=up_pre, mask=down_m[:, None, :], tok=tok)
     half_steps = (steps + 1) // 2
     if axes.pipe == 4:
-        squares = []
+        squares, waits = [], []
         for i, d in enumerate(downs):
             prev = squares[i - 1] if i else None
-            sq = Square(axes, dot_nt(after(rows, *prev.by) if i else rows, d))
+            sq = Square(axes, dot_nt(after(rows, *waits) if i else rows, d))
             squares.append(sq)
             sq.corner(prev.by if i else [])
+            waits = sq.sent
             sq.sides(prev.terms if i else [])
-            if not i:
-                grad_down, done = down(at_rows, before=None, first=0, last=half_steps, ties=list(sq.by))
-            sq.back(0.0 if i else done[0, 0])
+            if i == 0 and len(downs) > 2:
+                first_sides = sq.sent
+            if i == 1:
+                waits = first_sides if len(downs) > 2 else []
+                grad_down, done = down(at_rows, before=None, first=0, last=half_steps, ties=[prev.mine, sq.sent[1]])
+            sq.back(done[0, 0] if i == 1 else 0.0)
         sums = [sq.result() for sq in squares]
     else:
         sums = [reduce_over_pipe(axes, dot_nt(rows, d)) for d in downs]
@@ -386,6 +398,8 @@
     for i, ((c, w), sources) in enumerate(zip(pieces, sums)):
         if i + 1 < len(sums):
             waits = waits + [sums[i + 1][0][0]]
+            if i + 2 < len(sums) and axes.pipe == 4:
+                waits.append(squares[i + 2].sent[0])
         both, acc = local_grads(
             axes, at_rows, sources, gate_pre, up_pre, gate_weight, up_weight, gate_m, up_m, acc, tok, c, w, waits
         )
@@ -393,7 +407,7 @@
         waits = []
         if not i:
             weights, ready = weight_grads(
-                x_t, both, gate_m, up_m, None, gate_weight.shape, c, 0, w // step, []
+                x_t, both, gate_m, up_m, None, gate_weight.shape, c, 0, w // step, [sums[-1][0][0]]
             )
             waits = [ready]
 

time: 306 us -> 288 us (0.941)
  waiting for transfers between devices: 58.7 us -> 46.2 us
  local copies, waits for them, and re-layouts: 22 us -> 18.3 us
    ppermute x9, waiting for transfers between devices: 16.9 us -> 9.3 us  [to_next(): lax.ppermute(x, 'tensor', [(2 * a + k, 2 * b + k) for a, b in pairs for k...]
    ppermute x21, waiting for transfers between devices: 36.5 us -> 31.4 us  [to_pipe(): return lax.ppermute(x, 'pipe', [(i, i ^ bit) for i in range(self.pipe)])]
    unnamed x75 -> x69, local copies, waits for them, and re-layouts: 6.81 us -> 7.9 us
  transfers between devices with their start and end apart: 40 -> 40, of which waited for: 15 -> 12; matrix products, arithmetic and copies ran while one was open for 19% -> 18% of each run, Pallas kernels for 35% -> 37%
where the time goes in v7:
time: 288 us; the launch traced here: 282 us
  Pallas kernels  124 us (43%)
  waiting for transfers between devices  46.2 us (16%)
  starting transfers between devices  36.6 us (13%)
  other arithmetic  27.2 us (9%)
  local copies, waits for them, and re-layouts  18.3 us (6%)
  matrix products  15 us (5%)
  between operations  14.9 us (5%)
    pallas_call x3, Pallas kernels, local_grads(): pl.pallas_call(functools.partial(grads_kernel, cfg), out_shape=[jax.Shape...  59.1 us
    pallas_call x4, Pallas kernels, weight_grads(): pl.pallas_call(functools.partial(weights_kernel, dict(width=width, chunk=...  40.9 us
    ppermute x21, waiting for transfers between devices, to_pipe(): return lax.ppermute(x, 'pipe', [(i, i ^ bit) for i in range(self.pipe)])  31.4 us
    ppermute x21, starting transfers between devices, to_pipe(): return lax.ppermute(x, 'pipe', [(i, i ^ bit) for i in range(self.pipe)])  23.6 us
    pallas_call x2, Pallas kernels, down_grad(): pl.pallas_call(functools.partial(down_kernel, cfg), out_shape=[jax.ShapeD...  23.6 us
    dot_general x3, matrix products, dot_nt(): return lax.dot_general(a, b, NT, preferred_element_type=F32)  15 us
    mul x2, other arithmetic, masked(): weight.reshape(rows // BLOCK, BLOCK, cols) * mask.astype(BF16)[:, None, :]  11.1 us
    ppermute x9, starting transfers between devices, to_next(): lax.ppermute(x, 'tensor', [(2 * a + k, 2 * b + k) for a, b in pairs for k...  10.7 us
  transfers between devices with their start and end apart: 40, of which 12 were waited for; matrix products, arithmetic and copies ran while one was open for 18% of the time, Pallas kernels for 37%

profile of v7, /device:TPU:0, one launch (start us, length us, event | category | flops | bytes accessed | tf_op | source)
XLA Modules:
  0.0 281.9 jit_solution(7256170845044158897)
XLA Ops:
  8.8 2.6 collective-permute-start.1
  11.4 2.6 collective-permute-start.2
  19.4 5.1 %bitcast_multiply_fusion.1 = (bf16[1024,2048]{1,0:T(8,128)(2,1)}, bf16[1024,2048]{1,0:T(8,128)(2,1)S(1)}) fusion(bf16[3584,2048]{1,0:T(8,128)(2,1)} %param.17, bf16[8,2048]{1,0:T(8,128)(2,1)S(1)} %slice.99, bf16[8,2048]{1,0:T(8,128)(2,1)S(1)} %broadcast_bitcast_fusion), kind=kLoop, calls=%fused_computation.1 | loop fusion | flops 4194304 | bytes 16842752 | tf_op jit(solution)/shard_map/mul | solution.py:336
  25.0 2.9 %collective-permute-start.3 = (bf16[48,2048]{1,0:T(8,128)(2,1)}, bf16[48,2048]{1,0:T(8,128)(2,1)S(1)}, u32[]{:S(2)}, u32[]{:S(2)}) collective-permute-start(bf16[48,2048]{1,0:T(8,128)(2,1)} %collective-permute-done.1), channel_id=1, source_target_pairs={{0,2},{1,3},{2,6},{3,7},{6,4},{7,5},{4,0},{5,1},{8,10},{9,11},{10,... | collective-permute-start | bytes 589832 | tf_op jit(solution)/shard_map/ppermute | solution.py:69
  28.0 5.9 %bitcast_multiply_fusion = bf16[1536,2048]{1,0:T(8,128)(2,1)} fusion(bf16[3584,2048]{1,0:T(8,128)(2,1)} %param.17, bf16[12,2048]{1,0:T(8,128)(2,1)S(1)} %slice.98), kind=kLoop, calls=%fused_computation | loop fusion | flops 3145728 | bytes 12632064 | tf_op jit(solution)/shard_map/mul | solution.py:336
  34.5 2.1 collective-permute-done.3
  39.8 6.5 %collective-permute-done.5 = bf16[48,2048]{1,0:T(8,128)(2,1)S(1)} collective-permute-done((bf16[48,2048]{1,0:T(8,128)(2,1)S(1)}, bf16[48,2048]{1,0:T(8,128)(2,1)S(1)}, u32[]{:S(2)}, u32[]{:S(2)}) %collective-permute-start.5) | collective-permute-done | bytes 196640 | tf_op jit(solution)/shard_map/ppermute | solution.py:69
  48.5 3.5 %fusion.7 = f32[768,1024]{1,0:T(8,128)S(1)} fusion(bf16[768,2048]{1,0:T(8,128)(2,1)S(1)} %constant_dynamic-update-slice_fusion.refs_0_, bf16[1024,2048]{1,0:T(8,128)(2,1)S(1)} %get-tuple-element.87), kind=kOutput, calls=%fused_computation.64 | convolution fusion | flops 3221225472 | bytes 10485760 | tf_op jit(solution)/shard_map/dot_general | solution.py:340
  52.0 1.7 copy-done.10
  57.6 8.0 %fusion.9 = f32[768,1536]{1,0:T(8,128)S(1)} fusion(bf16[768,2048]{1,0:T(8,128)(2,1)S(1)} %constant_dynamic-update-slice_fusion.refs_0_, bf16[1536,2048]{1,0:T(8,128)(2,1)} %bitcast_multiply_fusion), kind=kOutput, calls=%fused_computation.66 | convolution fusion | flops 4831838208 | bytes 14155776 | tf_op jit(solution)/shard_map/dot_general | solution.py:340
  65.8 2.4 add_convert_fusion.8
  72.4 3.6 %fusion.8 = f32[768,1024]{1,0:T(8,128)S(1)} fusion(bf16[768,2048]{1,0:T(8,128)(2,1)S(1)} %constant_dynamic-update-slice_fusion.refs_0_, bf16[1024,2048]{1,0:T(8,128)(2,1)S(1)} %copy-done.1), kind=kOutput, calls=%fused_computation.65 | convolution fusion | flops 3221225472 | bytes 10485760 | tf_op jit(solution)/shard_map/dot_general | solution.py:340
  76.1 9.2 %collective-permute-done.15 = bf16[96,1536]{1,0:T(8,128)(2,1)S(1)} collective-permute-done((bf16[96,1536]{1,0:T(8,128)(2,1)S(1)}, bf16[96,1536]{1,0:T(8,128)(2,1)S(1)}, u32[]{:S(2)}, u32[]{:S(2)}) %collective-permute-start.15) | collective-permute-done | bytes 294944 | tf_op jit(solution)/shard_map/ppermute | solution.py:65
  85.6 1.5 collective-permute-start.18
  90.2 1.6 collective-permute-start.31
  91.8 12.8 %down_grad.2 = (bf16[3584,2048]{1,0:T(8,128)(2,1)}, f32[8,128]{1,0:T(8,128)}) custom-call(s32[9]{0:T(128)} %concatenate.30.at_rows, bf16[768,2048]{1,0:T(8,128)(2,1)} %copy-done.2, bf16[768,3584]{1,0:T(8,128)(2,1)} %refs_1_.3, bf16[768,3584]{1,0:T(8,128)(2,1)} %refs_2_.3, f32[28,1,2048]{2,1,0:T(1,128)} %bitcast.39, bf16[192,1024]{1,0:T(8,128)(2,1)} %copy-done.14, ...), custom_call_target="tpu_custom_call" | custom-call | flops 6442450944 | bytes 17825792 | tf_op jit(solution)/shard_map/down_grad/pallas_call | solution.py:310
  106.2 1.7 collective-permute-start.33
  109.9 2.1 add_convert_fusion.refs_10_.refs_0_
  116.0 9.2 %collective-permute-done.32.refs_2_ = bf16[192,1024]{1,0:T(8,128)(2,1)S(1)} collective-permute-done((bf16[192,1024]{1,0:T(8,128)(2,1)}, bf16[192,1024]{1,0:T(8,128)(2,1)S(1)}, u32[]{:S(2)}, u32[]{:S(2)}) %collective-permute-start.32) | collective-permute-done | bytes 393248 | tf_op jit(solution)/shard_map/ppermute | solution.py:65
  128.0 16.3 %local_grads.3 = (bf16[768,2048]{1,0:T(8,128)(2,1)}, f32[96,2048]{1,0:T(8,128)}, f32[96,2048]{1,0:T(8,128)}, f32[288,2048]{1,0:T(8,128)}, f32[288,2048]{1,0:T(8,128)}) custom-call(s32[9]{0:T(128)} %concatenate.30.at_rows, bf16[192,1024]{1,0:T(8,128)(2,1)} %copy-done.14, bf16[192,1024]{1,0:T(8,128)(2,1)} %collective-permute-done.31.refs_1_, ...), custom_call_target="tpu_custom_call" | custom-call | flops 6442450944 | bytes 28835840 | tf_op jit(solution)/shard_map/local_grads/pallas_call | solution.py:200
  144.4 11.9 %collective-permute-done.24 = bf16[192,1024]{1,0:T(8,128)(2,1)S(1)} collective-permute-done((bf16[192,1024]{1,0:T(8,128)(2,1)}, bf16[192,1024]{1,0:T(8,128)(2,1)S(1)}, u32[]{:S(2)}, u32[]{:S(2)}) %collective-permute-start.24) | collective-permute-done | bytes 393248 | tf_op jit(solution)/shard_map/ppermute | solution.py:65
  159.1 4.6 %copy.27 = bf16[768,2048]{0,1:T(8,128)(2,1)} copy(bf16[768,2048]{1,0:T(8,128)(2,1)} %all-gather.2.cloned.1.call-done) | data formatting | bytes 6291456 | tf_op jit(solution)/shard_map/all_gather | solution.py:373
  163.7 11.0 %weight_grads.4 = (bf16[2048,3584]{1,0:T(8,128)(2,1)}, bf16[2048,3584]{1,0:T(8,128)(2,1)}, f32[8,128]{1,0:T(8,128)}) custom-call(bf16[2048,768]{1,0:T(8,128)(2,1)} %bitcast.35, bf16[768,2048]{1,0:T(8,128)(2,1)} %get-tuple-element.64.grads, f32[16,3584]{1,0:T(8,128)} %get-tuple-element.117.refs_8_.gate_m, f32[16,3584]{1,0:T(8,128)} %get-tuple-element.116.refs_9_.up_m, ...), custom_call_target="tpu_custom_call" | custom-call | flops 6442450944 | bytes 14680064 | tf_op jit(solution)/shard_map/weight_grads/pallas_call | solution.py:254
  174.7 2.2 collective-permute-start.27
  177.9 23.8 %local_grads.4 = (bf16[768,3072]{1,0:T(8,128)(2,1)}, f32[96,2048]{1,0:T(8,128)}, f32[96,2048]{1,0:T(8,128)}, f32[288,2048]{1,0:T(8,128)}, f32[288,2048]{1,0:T(8,128)}) custom-call(s32[9]{0:T(128)} %concatenate.30.at_rows, bf16[192,1536]{1,0:T(8,128)(2,1)} %copy-done, bf16[192,1536]{1,0:T(8,128)(2,1)} %copy-done.20, bf16[192,1536]{1,0:T(8,128)(2,1)} %copy-done.21, ...), custom_call_target="tpu_custom_call" | custom-call | flops 9663676416 | bytes 36962304 | tf_op jit(solution)/shard_map/local_grads/pallas_call | solution.py:200
  202.7 19.0 %local_grads.5 = (bf16[768,2048]{1,0:T(8,128)(2,1)}, f32[96,2048]{1,0:T(8,128)}, f32[96,2048]{1,0:T(8,128)}, f32[288,2048]{1,0:T(8,128)}, f32[288,2048]{1,0:T(8,128)}) custom-call(s32[9]{0:T(128)} %concatenate.30.at_rows, bf16[192,1024]{1,0:T(8,128)(2,1)} %copy-done.3, bf16[192,1024]{1,0:T(8,128)(2,1)} %copy-done.25, bf16[192,1024]{1,0:T(8,128)(2,1)} %copy-done.26, ...), custom_call_target="tpu_custom_call" | custom-call | flops 6442450944 | bytes 28835840 | tf_op jit(solution)/shard_map/local_grads/pallas_call | solution.py:200
  222.3 4.2 %collective-permute-done.34 = f32[288,2048]{1,0:T(8,128)S(1)} collective-permute-done((f32[288,2048]{1,0:T(8,128)}, f32[288,2048]{1,0:T(8,128)S(1)}, u32[]{:S(2)}, u32[]{:S(2)}) %collective-permute-start.34) | collective-permute-done | bytes 2359328 | tf_op jit(solution)/shard_map/ppermute | solution.py:62
  226.5 1.8 fusion.4.refs_5_
  228.4 11.5 %weight_grads.5 = (bf16[2048,3584]{1,0:T(8,128)(2,1)}, bf16[2048,3584]{1,0:T(8,128)(2,1)}, f32[8,128]{1,0:T(8,128)}) custom-call(bf16[2048,768]{1,0:T(8,128)(2,1)} %bitcast.36, bf16[768,2048]{1,0:T(8,128)(2,1)} %get-tuple-element.75.grads, f32[16,3584]{1,0:T(8,128)} %get-tuple-element.117.refs_8_.gate_m, ...), custom_call_target="tpu_custom_call", output_to_operand_aliasing={{0}: (4, {}), {1}: (5, {})} | custom-call | flops 6442450944 | bytes 14680064 | tf_op jit(solution)/shard_map/weight_grads/pallas_call | solution.py:254
  242.6 10.8 %down_grad.3 = (bf16[3584,2048]{1,0:T(8,128)(2,1)}, f32[8,128]{1,0:T(8,128)}) custom-call(s32[9]{0:T(128)} %concatenate.30.at_rows, bf16[768,2048]{1,0:T(8,128)(2,1)} %copy-done.2, bf16[768,3584]{1,0:T(8,128)(2,1)} %refs_1_.3, bf16[768,3584]{1,0:T(8,128)(2,1)} %refs_2_.3, f32[28,1,2048]{2,1,0:T(1,128)} %bitcast.40, ...), custom_call_target="tpu_custom_call", output_to_operand_aliasing={{0}: (5, {})} | custom-call | flops 4831838208 | bytes 14155776 | tf_op jit(solution)/shard_map/down_grad/pallas_call | solution.py:310
  255.5 11.0 %weight_grads.6 = (bf16[2048,3584]{1,0:T(8,128)(2,1)}, bf16[2048,3584]{1,0:T(8,128)(2,1)}, f32[8,128]{1,0:T(8,128)}) custom-call(bf16[2048,768]{1,0:T(8,128)(2,1)} %bitcast.37, bf16[768,3072]{1,0:T(8,128)(2,1)} %get-tuple-element.74.grads, f32[16,3584]{1,0:T(8,128)} %get-tuple-element.117.refs_8_.gate_m, ...), custom_call_target="tpu_custom_call", output_to_operand_aliasing={{0}: (4, {}), {1}: (5, {})} | custom-call | flops 6442450944 | bytes 14680064 | tf_op jit(solution)/shard_map/weight_grads/pallas_call | solution.py:254
  266.5 7.5 %weight_grads.7 = (bf16[2048,3584]{1,0:T(8,128)(2,1)}, bf16[2048,3584]{1,0:T(8,128)(2,1)}, f32[8,128]{1,0:T(8,128)}) custom-call(bf16[2048,768]{1,0:T(8,128)(2,1)} %bitcast.38, bf16[768,3072]{1,0:T(8,128)(2,1)} %get-tuple-element.74.grads, f32[16,3584]{1,0:T(8,128)} %get-tuple-element.117.refs_8_.gate_m, ...), custom_call_target="tpu_custom_call", output_to_operand_aliasing={{0}: (4, {}), {1}: (5, {})} | custom-call | flops 3221225472 | bytes 8912896 | tf_op jit(solution)/shard_map/weight_grads/pallas_call | solution.py:254
  (168 shorter events, 46.5 us)
Async XLA Ops:
  7.2 151.9 %all-gather.2.cloned.1.call-start = ((), (), s32[]{:S(2)}) async-start(), calls=%async_computation | async-start | bytes 3538944 | tf_op jit(solution)/shard_map/all_gather | solution.py:373
  7.2 29.7 %collective-permute-start = (bf16[96,2048]{1,0:T(8,128)(2,1)}, bf16[96,2048]{1,0:T(8,128)(2,1)}, u32[]{:S(2)}, u32[]{:S(2)}) collective-permute-start(bf16[96,2048]{1,0:T(8,128)(2,1)} %param.12), channel_id=1, source_target_pairs={{0,1},{1,0},{2,3},{3,2},{4,5},{5,4},{6,7},{7,6},{8,9},{9,8},{10,11... | collective-permute-start | bytes 1179656 | tf_op jit(solution)/shard_map/ppermute | solution.py:62
  8.8 10.5 %collective-permute-start.1 = (bf16[48,2048]{1,0:T(8,128)(2,1)S(1)}, bf16[48,2048]{1,0:T(8,128)(2,1)}, u32[]{:S(2)}, u32[]{:S(2)}) collective-permute-start(bf16[48,2048]{1,0:T(8,128)(2,1)S(1)} %get-tuple-element.107), channel_id=1, source_target_pairs={{0,2},{1,3},{2,6},{3,7},{6,4},{7,5},{4,0},{5,1},{8,10},{9,11},{10,... | collective-permute-start | bytes 589832 | tf_op jit(solution)/shard_map/ppermute | solution.py:69
  11.4 13.1 %collective-permute-start.2 = (bf16[48,2048]{1,0:T(8,128)(2,1)S(1)}, bf16[48,2048]{1,0:T(8,128)(2,1)}, u32[]{:S(2)}, u32[]{:S(2)}) collective-permute-start(bf16[48,2048]{1,0:T(8,128)(2,1)S(1)} %get-tuple-element.106), channel_id=1, source_target_pairs={{0,2},{1,3},{2,6},{3,7},{6,4},{7,5},{4,0},{5,1},{8,10},{9,11},{10,... | collective-permute-start | bytes 589832 | tf_op jit(solution)/shard_map/ppermute | solution.py:69
  25.0 11.6 %collective-permute-start.3 = (bf16[48,2048]{1,0:T(8,128)(2,1)}, bf16[48,2048]{1,0:T(8,128)(2,1)S(1)}, u32[]{:S(2)}, u32[]{:S(2)}) collective-permute-start(bf16[48,2048]{1,0:T(8,128)(2,1)} %collective-permute-done.1), channel_id=1, source_target_pairs={{0,2},{1,3},{2,6},{3,7},{6,4},{7,5},{4,0},{5,1},{8,10},{9,11},{10,... | collective-permute-start | bytes 589832 | tf_op jit(solution)/shard_map/ppermute | solution.py:69
  33.9 13.1 %collective-permute-start.7 = (bf16[48,2048]{1,0:T(8,128)(2,1)}, bf16[48,2048]{1,0:T(8,128)(2,1)S(1)}, u32[]{:S(2)}, u32[]{:S(2)}) collective-permute-start(bf16[48,2048]{1,0:T(8,128)(2,1)} %collective-permute-done.1), channel_id=1, source_target_pairs={{0,1},{1,0},{2,3},{3,2},{4,5},{5,4},{6,7},{7,6},{8,9},{9,8},{10,11... | collective-permute-start | bytes 589832 | tf_op jit(solution)/shard_map/ppermute | solution.py:62
  33.9 13.2 %collective-permute-start.8 = (bf16[48,2048]{1,0:T(8,128)(2,1)}, bf16[48,2048]{1,0:T(8,128)(2,1)S(1)}, u32[]{:S(2)}, u32[]{:S(2)}) collective-permute-start(bf16[48,2048]{1,0:T(8,128)(2,1)} %collective-permute-done.2), channel_id=1, source_target_pairs={{0,1},{1,0},{2,3},{3,2},{4,5},{5,4},{6,7},{7,6},{8,9},{9,8},{10,11... | collective-permute-start | bytes 589832 | tf_op jit(solution)/shard_map/ppermute | solution.py:62
  34.4 11.9 %collective-permute-start.6 = (bf16[48,2048]{1,0:T(8,128)(2,1)S(1)}, bf16[48,2048]{1,0:T(8,128)(2,1)S(1)}, u32[]{:S(2)}, u32[]{:S(2)}) collective-permute-start(bf16[48,2048]{1,0:T(8,128)(2,1)S(1)} %collective-permute-done.4), channel_id=1, source_target_pairs={{0,2},{1,3},{2,6},{3,7},{6,4},{7,5},{4,0},{5,1},{8,10},{9,11},{10,... | collective-permute-start | bytes 589832 | tf_op jit(solution)/shard_map/ppermute | solution.py:69
  54.5 11.2 %collective-permute-start.14 = (bf16[96,1024]{1,0:T(8,128)(2,1)}, bf16[96,1024]{1,0:T(8,128)(2,1)}, u32[]{:S(2)}, u32[]{:S(2)}) collective-permute-start(bf16[96,1024]{1,0:T(8,128)(2,1)} %get-tuple-element.102), channel_id=1, source_target_pairs={{0,8},{8,0},{16,24},{24,16},{1,9},{9,1},{17,25},{25,17},{2,10},{10... | collective-permute-start | bytes 589832 | tf_op jit(solution)/shard_map/ppermute | solution.py:65
  68.2 19.6 %collective-permute-start.19 = (bf16[192,1024]{1,0:T(8,128)(2,1)S(1)}, bf16[192,1024]{1,0:T(8,128)(2,1)S(1)}, u32[]{:S(2)}, u32[]{:S(2)}) collective-permute-start(bf16[192,1024]{1,0:T(8,128)(2,1)S(1)} %pad_maximum_fusion.2), channel_id=1, source_target_pairs={{0,8},{8,0},{16,24},{24,16},{1,9},{9,1},{17,25},{25,17},{2,10},{10... | collective-permute-start | bytes 1179656 | tf_op jit(solution)/shard_map/ppermute | solution.py:65
  68.9 19.0 %collective-permute-start.20 = (bf16[192,1024]{1,0:T(8,128)(2,1)S(1)}, bf16[192,1024]{1,0:T(8,128)(2,1)S(1)}, u32[]{:S(2)}, u32[]{:S(2)}) collective-permute-start(bf16[192,1024]{1,0:T(8,128)(2,1)S(1)} %pad_maximum_fusion.3), channel_id=1, source_target_pairs={{0,16},{8,24},{16,0},{24,8},{1,17},{9,25},{17,1},{25,9},{2,18},{10... | collective-permute-start | bytes 1179656 | tf_op jit(solution)/shard_map/ppermute | solution.py:65
  69.4 15.9 %collective-permute-start.15 = (bf16[96,1536]{1,0:T(8,128)(2,1)S(1)}, bf16[96,1536]{1,0:T(8,128)(2,1)S(1)}, u32[]{:S(2)}, u32[]{:S(2)}) collective-permute-start(bf16[96,1536]{1,0:T(8,128)(2,1)S(1)} %get-tuple-element.50), channel_id=1, source_target_pairs={{0,8},{8,0},{16,24},{24,16},{1,9},{9,1},{17,25},{25,17},{2,10},{10... | collective-permute-start | bytes 884744 | tf_op jit(solution)/shard_map/ppermute | solution.py:65
  70.9 14.7 %collective-permute-start.16 = (bf16[96,1536]{1,0:T(8,128)(2,1)S(1)}, bf16[96,1536]{1,0:T(8,128)(2,1)S(1)}, u32[]{:S(2)}, u32[]{:S(2)}) collective-permute-start(bf16[96,1536]{1,0:T(8,128)(2,1)S(1)} %get-tuple-element.51), channel_id=1, source_target_pairs={{0,16},{8,24},{16,0},{24,8},{1,17},{9,25},{17,1},{25,9},{2,18},{10... | collective-permute-start | bytes 884744 | tf_op jit(solution)/shard_map/ppermute | solution.py:65
  85.6 20.2 %collective-permute-start.18 = (bf16[96,1024]{1,0:T(8,128)(2,1)S(1)}, bf16[96,1024]{1,0:T(8,128)(2,1)S(1)}, u32[]{:S(2)}, u32[]{:S(2)}) collective-permute-start(bf16[96,1024]{1,0:T(8,128)(2,1)S(1)} %get-tuple-element.53), channel_id=1, source_target_pairs={{0,8},{8,0},{16,24},{24,16},{1,9},{9,1},{17,25},{25,17},{2,10},{10... | collective-permute-start | bytes 589832 | tf_op jit(solution)/shard_map/ppermute | solution.py:65
  87.1 19.1 %collective-permute-start.17 = (bf16[96,1024]{1,0:T(8,128)(2,1)S(1)}, bf16[96,1024]{1,0:T(8,128)(2,1)S(1)}, u32[]{:S(2)}, u32[]{:S(2)}) collective-permute-start(bf16[96,1024]{1,0:T(8,128)(2,1)S(1)} %get-tuple-element.52), channel_id=1, source_target_pairs={{0,16},{8,24},{16,0},{24,8},{1,17},{9,25},{17,1},{25,9},{2,18},{10... | collective-permute-start | bytes 589832 | tf_op jit(solution)/shard_map/ppermute | solution.py:65
  87.8 22.1 %collective-permute-start.21 = (bf16[192,1536]{1,0:T(8,128)(2,1)S(1)}, bf16[192,1536]{1,0:T(8,128)(2,1)S(1)}, u32[]{:S(2)}, u32[]{:S(2)}) collective-permute-start(bf16[192,1536]{1,0:T(8,128)(2,1)S(1)} %get-tuple-element.54), channel_id=1, source_target_pairs={{0,8},{8,0},{16,24},{24,16},{1,9},{9,1},{17,25},{25,17},{2,10},{10... | collective-permute-start | bytes 1769480 | tf_op jit(solution)/shard_map/ppermute | solution.py:65
  88.4 21.5 %collective-permute-start.22 = (bf16[192,1536]{1,0:T(8,128)(2,1)S(1)}, bf16[192,1536]{1,0:T(8,128)(2,1)S(1)}, u32[]{:S(2)}, u32[]{:S(2)}) collective-permute-start(bf16[192,1536]{1,0:T(8,128)(2,1)S(1)} %get-tuple-element.55.refs_5_), channel_id=1, source_target_pairs={{0,16},{8,24},{16,0},{24,8},{1,17},{9,25},{17,1},{25,9},{2,18},{10... | collective-permute-start | bytes 1769480 | tf_op jit(solution)/shard_map/ppermute | solution.py:65
  90.2 24.4 %collective-permute-start.31 = (bf16[192,1024]{1,0:T(8,128)(2,1)S(1)}, bf16[192,1024]{1,0:T(8,128)(2,1)}, u32[]{:S(2)}, u32[]{:S(2)}) collective-permute-start(bf16[192,1024]{1,0:T(8,128)(2,1)S(1)} %add_convert_fusion.2.refs_4_.refs_0_), channel_id=1, source_target_pairs={{0,8},{8,0},{16,24},{24,16},{1,9},{9,1},{17,25},{25,17},{2,10},{10... | collective-permute-start | bytes 1179656 | tf_op jit(solution)/shard_map/ppermute | solution.py:65
  105.8 19.5 %collective-permute-start.32 = (bf16[192,1024]{1,0:T(8,128)(2,1)}, bf16[192,1024]{1,0:T(8,128)(2,1)S(1)}, u32[]{:S(2)}, u32[]{:S(2)}) collective-permute-start(bf16[192,1024]{1,0:T(8,128)(2,1)} %copy-done.14), channel_id=1, source_target_pairs={{0,16},{8,24},{16,0},{24,8},{1,17},{9,25},{17,1},{25,9},{2,18},{10... | collective-permute-start | bytes 1179656 | tf_op jit(solution)/shard_map/ppermute | solution.py:65
  106.2 19.8 %collective-permute-start.33 = (bf16[192,1024]{1,0:T(8,128)(2,1)}, bf16[192,1024]{1,0:T(8,128)(2,1)S(1)}, u32[]{:S(2)}, u32[]{:S(2)}) collective-permute-start(bf16[192,1024]{1,0:T(8,128)(2,1)} %copy-done.14), channel_id=1, source_target_pairs={{0,24},{8,16},{16,8},{24,0},{1,25},{9,17},{17,9},{25,1},{2,26},{10... | collective-permute-start | bytes 1179656 | tf_op jit(solution)/shard_map/ppermute | solution.py:65
  112.0 62.7 %collective-permute-start.28 = (bf16[192,1536]{1,0:T(8,128)(2,1)S(1)}, bf16[192,1536]{1,0:T(8,128)(2,1)S(1)}, u32[]{:S(2)}, u32[]{:S(2)}) collective-permute-start(bf16[192,1536]{1,0:T(8,128)(2,1)S(1)} %add_convert_fusion.refs_10_.refs_0_), channel_id=1, source_target_pairs={{0,8},{8,0},{16,24},{24,16},{1,9},{9,1},{17,25},{25,17},{2,10},{10... | collective-permute-start | bytes 1769480 | tf_op jit(solution)/shard_map/ppermute | solution.py:65
  113.4 63.5 %collective-permute-start.29 = (bf16[192,1536]{1,0:T(8,128)(2,1)S(1)}, bf16[192,1536]{1,0:T(8,128)(2,1)S(1)}, u32[]{:S(2)}, u32[]{:S(2)}) collective-permute-start(bf16[192,1536]{1,0:T(8,128)(2,1)S(1)} %add_convert_fusion.refs_10_.refs_0_), channel_id=1, source_target_pairs={{0,16},{8,24},{16,0},{24,8},{1,17},{9,25},{17,1},{25,9},{2,18},{10... | collective-permute-start | bytes 1769480 | tf_op jit(solution)/shard_map/ppermute | solution.py:65
  114.6 62.3 %collective-permute-start.30 = (bf16[192,1536]{1,0:T(8,128)(2,1)S(1)}, bf16[192,1536]{1,0:T(8,128)(2,1)S(1)}, u32[]{:S(2)}, u32[]{:S(2)}) collective-permute-start(bf16[192,1536]{1,0:T(8,128)(2,1)S(1)} %add_convert_fusion.refs_10_.refs_0_), channel_id=1, source_target_pairs={{0,24},{8,16},{16,8},{24,0},{1,25},{9,17},{17,9},{25,1},{2,26},{10... | collective-permute-start | bytes 1769480 | tf_op jit(solution)/shard_map/ppermute | solution.py:65
  125.3 31.0 %collective-permute-start.24 = (bf16[192,1024]{1,0:T(8,128)(2,1)}, bf16[192,1024]{1,0:T(8,128)(2,1)S(1)}, u32[]{:S(2)}, u32[]{:S(2)}) collective-permute-start(bf16[192,1024]{1,0:T(8,128)(2,1)} %get-tuple-element.57), channel_id=1, source_target_pairs={{0,16},{8,24},{16,0},{24,8},{1,17},{9,25},{17,1},{25,9},{2,18},{10... | collective-permute-start | bytes 1179656 | tf_op jit(solution)/shard_map/ppermute | solution.py:65
  126.8 29.5 %collective-permute-start.23 = (bf16[192,1024]{1,0:T(8,128)(2,1)S(1)}, bf16[192,1024]{1,0:T(8,128)(2,1)S(1)}, u32[]{:S(2)}, u32[]{:S(2)}) collective-permute-start(bf16[192,1024]{1,0:T(8,128)(2,1)S(1)} %get-tuple-element.56.refs_11_), channel_id=1, source_target_pairs={{0,8},{8,0},{16,24},{24,16},{1,9},{9,1},{17,25},{25,17},{2,10},{10... | collective-permute-start | bytes 1179656 | tf_op jit(solution)/shard_map/ppermute | solution.py:65
  157.6 44.2 %collective-permute-start.25 = (bf16[192,1024]{1,0:T(8,128)(2,1)S(1)}, bf16[192,1024]{1,0:T(8,128)(2,1)S(1)}, u32[]{:S(2)}, u32[]{:S(2)}) collective-permute-start(bf16[192,1024]{1,0:T(8,128)(2,1)S(1)} %add_convert_fusion.3.refs_0_.refs_15_), channel_id=1, source_target_pairs={{0,8},{8,0},{16,24},{24,16},{1,9},{9,1},{17,25},{25,17},{2,10},{10... | collective-permute-start | bytes 1179656 | tf_op jit(solution)/shard_map/ppermute | solution.py:65
  158.7 43.1 %collective-permute-start.26 = (bf16[192,1024]{1,0:T(8,128)(2,1)S(1)}, bf16[192,1024]{1,0:T(8,128)(2,1)S(1)}, u32[]{:S(2)}, u32[]{:S(2)}) collective-permute-start(bf16[192,1024]{1,0:T(8,128)(2,1)S(1)} %add_convert_fusion.3.refs_0_.refs_15_), channel_id=1, source_target_pairs={{0,16},{8,24},{16,0},{24,8},{1,17},{9,25},{17,1},{25,9},{2,18},{10... | collective-permute-start | bytes 1179656 | tf_op jit(solution)/shard_map/ppermute | solution.py:65
  174.7 27.1 %collective-permute-start.27 = (bf16[192,1024]{1,0:T(8,128)(2,1)S(1)}, bf16[192,1024]{1,0:T(8,128)(2,1)}, u32[]{:S(2)}, u32[]{:S(2)}) collective-permute-start(bf16[192,1024]{1,0:T(8,128)(2,1)S(1)} %copy-done.4), channel_id=1, source_target_pairs={{0,24},{8,16},{16,8},{24,0},{1,25},{9,17},{17,9},{25,1},{2,26},{10... | collective-permute-start | bytes 1179656 | tf_op jit(solution)/shard_map/ppermute | solution.py:65
  221.8 52.2 %collective-permute-start.38 = (f32[96,2048]{1,0:T(8,128)}, f32[96,2048]{1,0:T(8,128)S(1)}, u32[]{:S(2)}, u32[]{:S(2)}) collective-permute-start(f32[96,2048]{1,0:T(8,128)} %get-tuple-element.73), channel_id=1, source_target_pairs={{0,1},{1,0},{2,3},{3,2},{4,5},{5,4},{6,7},{7,6},{8,9},{9,8},{10,11... | collective-permute-start | bytes 2359304 | tf_op jit(solution)/shard_map/ppermute | solution.py:62
  228.3 12.2 %collective-permute-start.35 = (bf16[96,2048]{1,0:T(8,128)(2,1)S(1)}, bf16[96,2048]{1,0:T(8,128)(2,1)}, u32[]{:S(2)}, u32[]{:S(2)}) collective-permute-start(bf16[96,2048]{1,0:T(8,128)(2,1)S(1)} %fusion.4.refs_5_), channel_id=1, source_target_pairs={{0,2},{1,3},{2,6},{3,7},{6,4},{7,5},{4,0},{5,1},{8,10},{9,11},{10,... | collective-permute-start | bytes 1179656 | tf_op jit(solution)/shard_map/ppermute | solution.py:69
  241.8 11.6 %collective-permute-start.36 = (bf16[96,2048]{1,0:T(8,128)(2,1)S(1)}, bf16[96,2048]{1,0:T(8,128)(2,1)S(1)}, u32[]{:S(2)}, u32[]{:S(2)}) collective-permute-start(bf16[96,2048]{1,0:T(8,128)(2,1)S(1)} %fusion.3.refs_2_), channel_id=1, source_target_pairs={{0,2},{1,3},{2,6},{3,7},{6,4},{7,5},{4,0},{5,1},{8,10},{9,11},{10,... | collective-permute-start | bytes 1179656 | tf_op jit(solution)/shard_map/ppermute | solution.py:69
  254.7 19.3 %collective-permute-start.37 = (bf16[96,2048]{1,0:T(8,128)(2,1)S(1)}, bf16[96,2048]{1,0:T(8,128)(2,1)S(1)}, u32[]{:S(2)}, u32[]{:S(2)}) collective-permute-start(bf16[96,2048]{1,0:T(8,128)(2,1)S(1)} %fusion.1.refs_2_), channel_id=1, source_target_pairs={{0,2},{1,3},{2,6},{3,7},{6,4},{7,5},{4,0},{5,1},{8,10},{9,11},{10,... | collective-permute-start | bytes 1179656 | tf_op jit(solution)/shard_map/ppermute | solution.py:69
  (35 other events, 262.3 us)
Sparse Core Ops, SparseCore 0:
  57.7 35.0 all-gather.1
